TPU v7x, 32 devices: a whole 2x2x4 slice. The times are simulated.
32 devices in a mesh: dp: 4 (over z), seq: 8 (over y, x, core).
Axes of the slice: x: 2, y: 2, z: 4, core: 2. Of those that a mesh axis runs over, the one named last changes fastest.
Arguments:
- inputs: bfloat16 [8, 1024, 2048], P('dp', 'seq'), may hold values from -6 to 6
- segment_ids: int32 [8, 1024], P('dp', 'seq'), may hold values from 0 to 5, as said below
- attn_norm: bfloat16 [2048], P(('dp', 'seq')), may hold values from 0.25 to 1.75
- w_query: bfloat16 [2048, 2048], P(('dp', 'seq')), may hold values from -0.125 to 0.125
- w_key: bfloat16 [2048, 256], P(('dp', 'seq')), may hold values from -0.125 to 0.125
- w_value: bfloat16 [2048, 256], P(('dp', 'seq')), may hold values from -0.125 to 0.125
- w_out: bfloat16 [2048, 2048], P(('dp', 'seq')), may hold values from -1.5 to 1.5
- ffn_norm: bfloat16 [2048], P(('dp', 'seq')), may hold values from 0.25 to 1.75
- w_gate: bfloat16 [2048, 5632], P(('dp', 'seq')), may hold values from -0.125 to 0.125
- w_up: bfloat16 [2048, 5632], P(('dp', 'seq')), may hold values from -0.125 to 0.125
- w_down: bfloat16 [5632, 2048], P(('dp', 'seq')), may hold values from -0.3125 to 0.3125
- grad_output: bfloat16 [8, 1024, 2048], P('dp', 'seq'), may hold values from -6 to 6
Outputs:
- output: bfloat16 [8, 1024, 2048], P('dp', 'seq')
- grad_inputs: float32 [8, 1024, 2048], P('dp', 'seq')
- grad_attn_norm: float32 [2048], P(('dp', 'seq'))
- grad_w_query: float32 [2048, 2048], P(('dp', 'seq'))
- grad_w_key: float32 [2048, 256], P(('dp', 'seq'))
- grad_w_value: float32 [2048, 256], P(('dp', 'seq'))
- grad_w_out: float32 [2048, 2048], P(('dp', 'seq'))
- grad_ffn_norm: float32 [2048], P(('dp', 'seq'))
- grad_w_gate: float32 [2048, 5632], P(('dp', 'seq'))
- grad_w_up: float32 [2048, 5632], P(('dp', 'seq'))
- grad_w_down: float32 [5632, 2048], P(('dp', 'seq'))
Inputs may be any that keep to these rules, and one draw needn't show every extreme that they name: `segment_ids`: in each sequence the ids start at 0 and never fall; a document is a run of equal ids. One document of each sequence begins within its first 128 positions and ends within its last 128 positions.
All inputs are finite; a program needn't handle non-finite values.
Results may differ from a plain program's by a relative error of at most 0.015.
Values may be sent and summed in bfloat16 or wider, within the bound.
No kernel may reach another device: no remote copies, remote signals or barrier semaphores. Data moves between devices by JAX's collectives and lax.ppermute only.
A program may use at most 384 MiB of HBM per device.

v0:
```python
import math

import jax
import jax.numpy as jnp
from jax import lax
from jax.sharding import PartitionSpec as P

HEADS = 32
KV_HEADS = 4
HEAD = 64


EPSILON = 1e-05
ROPE_BASE = 10000.0
MASKED = -1e30


def rotary_tables(doc_ids):
    length = doc_ids.shape[0]
    places = jnp.arange(length, dtype=jnp.int32)
    before = jnp.concatenate([doc_ids[:1] - 1, doc_ids[:-1]])
    starts_here = doc_ids != before
    doc_first = lax.cummax(jnp.where(starts_here, places, 0), axis=0)
    offsets = (places - doc_first).astype(jnp.float32)
    halfway = HEAD // 2
    frequency = ROPE_BASE ** (-2.0 * jnp.arange(halfway, dtype=jnp.float32) / HEAD)
    angles = offsets[:, None] * frequency[None, :]
    angles = jnp.concatenate([angles, angles], axis=1)
    return (jnp.cos(angles), jnp.sin(angles))


def rotate(values, cosine, sine_table):
    halfway = HEAD // 2
    turned = jnp.concatenate([-values[..., halfway:], values[..., :halfway]], axis=-1)
    return values * cosine[:, None, :] + turned * sine_table[:, None, :]


def rotate_back(grads, cosine, sine_table):
    halfway = HEAD // 2
    scaled = grads * sine_table[:, None, :]
    return grads * cosine[:, None, :] + jnp.concatenate(
        [scaled[..., halfway:], -scaled[..., :halfway]], axis=-1
    )


def times_transposed(left, right):
    return lax.dot_general(
        left, right, (((1,), (1,)), ((), ())), preferred_element_type=jnp.float32
    )


def outer_rows(left, right):
    return lax.dot_general(
        left, right, (((0,), (0,)), ((), ())), preferred_element_type=jnp.float32
    )


def norm_back(grad_normed, normed, inverse):
    return inverse * (grad_normed - normed * jnp.mean(grad_normed * normed, axis=-1, keepdims=True))


def on_device(
    inputs,
    segment_ids,
    attn_norm,
    w_query,
    w_key,
    w_value,
    w_out,
    ffn_norm,
    w_gate,
    w_up,
    w_down,
    grad_output,
):
    seqs_here = inputs.shape[0]
    rows_here = inputs.shape[1]
    width = inputs.shape[2]
    total_rows = seqs_here * rows_here
    group_size = HEADS // KV_HEADS
    head_scale = 1.0 / math.sqrt(HEAD)
    state = inputs.astype(jnp.float32).reshape(total_rows, width)
    upstream = grad_output.reshape(total_rows, width)
    norm_one, query_w, key_w, value_w, out_w = (
        lax.all_gather(attn_norm, ("dp", "seq"), axis=0, tiled=True),
        lax.all_gather(w_query, ("dp", "seq"), axis=0, tiled=True),
        lax.all_gather(w_key, ("dp", "seq"), axis=0, tiled=True),
        lax.all_gather(w_value, ("dp", "seq"), axis=0, tiled=True),
        lax.all_gather(w_out, ("dp", "seq"), axis=0, tiled=True),
    )
    doc_all = lax.all_gather(segment_ids, "seq", axis=1, tiled=True)
    length = doc_all.shape[1]
    first_row = lax.axis_index("seq") * rows_here
    cosine_all, sine_all = jax.vmap(rotary_tables)(doc_all)
    cosine = lax.dynamic_slice_in_dim(cosine_all, first_row, rows_here, 1).reshape(total_rows, HEAD)
    sine_table = lax.dynamic_slice_in_dim(sine_all, first_row, rows_here, 1).reshape(
        total_rows, HEAD
    )
    doc_here = lax.dynamic_slice_in_dim(doc_all, first_row, rows_here, 1)
    query_places = first_row + jnp.arange(rows_here, dtype=jnp.int32)
    inverse_one = lax.rsqrt(jnp.mean(state * state, axis=-1, keepdims=True) + EPSILON)
    normed_one = state * inverse_one
    gain_one = norm_one.astype(jnp.float32)
    acts_one = (normed_one * gain_one).astype(jnp.bfloat16)
    query_raw = jnp.dot(acts_one, query_w, preferred_element_type=jnp.float32).reshape(
        total_rows, HEADS, HEAD
    )
    key_raw = jnp.dot(acts_one, key_w, preferred_element_type=jnp.float32).reshape(
        total_rows, KV_HEADS, HEAD
    )
    values_here = jnp.dot(acts_one, value_w, preferred_element_type=jnp.float32).astype(
        jnp.bfloat16
    )
    values_here = values_here.reshape(seqs_here, rows_here, KV_HEADS * HEAD)
    queries = (
        rotate(query_raw, cosine, sine_table)
        .astype(jnp.bfloat16)
        .reshape(seqs_here, rows_here, KV_HEADS, group_size, HEAD)
    )
    keys_here = (
        rotate(key_raw, cosine, sine_table)
        .astype(jnp.bfloat16)
        .reshape(seqs_here, rows_here, KV_HEADS * HEAD)
    )
    keys_all, values_all = (
        lax.all_gather(keys_here, "seq", axis=1, tiled=True),
        lax.all_gather(values_here, "seq", axis=1, tiled=True),
    )
    keys_all = keys_all.reshape(seqs_here, length, KV_HEADS, HEAD)
    values_all = values_all.reshape(seqs_here, length, KV_HEADS, HEAD)
    key_block = math.gcd(length, 512)
    blocks = length // key_block
    stat_shape = (KV_HEADS, group_size, rows_here, 1)

    def block_scores(seq_number, block_number):
        offset = block_number * key_block
        block_keys = lax.dynamic_slice_in_dim(keys_all[seq_number], offset, key_block, 0)
        block_values = lax.dynamic_slice_in_dim(values_all[seq_number], offset, key_block, 0)
        scores = (
            jnp.einsum(
                "qkgd,jkd->kgqj",
                queries[seq_number],
                block_keys,
                preferred_element_type=jnp.float32,
            )
            * head_scale
        )
        key_places = offset + jnp.arange(key_block, dtype=jnp.int32)
        block_docs = lax.dynamic_slice_in_dim(doc_all[seq_number], offset, key_block, 0)
        visible = (key_places[None, :] <= query_places[:, None]) & (
            block_docs[None, :] == doc_here[seq_number][:, None]
        )
        visible = visible[None, None]
        return (jnp.where(visible, scores, MASKED), visible, block_keys, block_values)

    log_totals = []
    attended_list = []
    for seq_number in range(seqs_here):

        def first_pass(block_number, running):
            highest, totals = running
            scores, visible, block_keys, block_values = block_scores(seq_number, block_number)
            new_high = jnp.maximum(highest, jnp.max(scores, axis=-1, keepdims=True))
            expo = jnp.where(visible, jnp.exp(scores - new_high), 0.0)
            totals = totals * jnp.exp(highest - new_high) + jnp.sum(expo, axis=-1, keepdims=True)
            return (new_high, totals)

        highest, totals = lax.fori_loop(
            0,
            blocks,
            first_pass,
            (jnp.full(stat_shape, MASKED, jnp.float32), jnp.zeros(stat_shape, jnp.float32)),
        )
        log_total = highest + jnp.log(totals)

        def second_pass(block_number, running):
            scores, visible, block_keys, block_values = block_scores(seq_number, block_number)
            probs = jnp.where(visible, jnp.exp(scores - log_total), 0.0)
            return running + jnp.einsum(
                "kgqj,jkd->qkgd",
                probs.astype(jnp.bfloat16),
                block_values,
                preferred_element_type=jnp.float32,
            )

        attended_one = lax.fori_loop(
            0, blocks, second_pass, jnp.zeros((rows_here, KV_HEADS, group_size, HEAD), jnp.float32)
        )
        log_totals.append(log_total)
        attended_list.append(attended_one)
    attended = jnp.stack(attended_list)
    mixed_heads = attended.reshape(total_rows, HEADS * HEAD).astype(jnp.bfloat16)
    residual = state + jnp.dot(mixed_heads, out_w, preferred_element_type=jnp.float32)
    inverse_two = lax.rsqrt(jnp.mean(residual * residual, axis=-1, keepdims=True) + EPSILON)
    normed_two = residual * inverse_two
    gain_piece = lax.all_gather(ffn_norm, ("dp", "seq"), axis=0, tiled=True)
    gate_piece = lax.all_gather(w_gate, ("dp", "seq"), axis=0, tiled=True)
    up_piece = lax.all_gather(w_up, ("dp", "seq"), axis=0, tiled=True)
    columns = normed_two
    gain_float = gain_piece.astype(jnp.float32)
    part = (columns * gain_float).astype(jnp.bfloat16)
    gate_pre = jnp.dot(part, gate_piece, preferred_element_type=jnp.float32)
    up_pre = jnp.dot(part, up_piece, preferred_element_type=jnp.float32)
    acts_two = part
    hidden = (jax.nn.silu(gate_pre) * up_pre).astype(jnp.bfloat16)
    columns = hidden
    ffn_result = jnp.dot(
        columns,
        lax.all_gather(w_down, ("dp", "seq"), axis=0, tiled=True),
        preferred_element_type=jnp.float32,
    )
    output = (residual + ffn_result).astype(jnp.bfloat16)
    d_hidden = times_transposed(upstream, lax.all_gather(w_down, ("dp", "seq"), axis=0, tiled=True))
    sigmoid_gate = jax.nn.sigmoid(gate_pre)
    d_gate = (d_hidden * up_pre * sigmoid_gate * (1.0 + gate_pre * (1.0 - sigmoid_gate))).astype(
        jnp.bfloat16
    )
    d_up = (d_hidden * gate_pre * sigmoid_gate).astype(jnp.bfloat16)
    columns = hidden
    grad_down = lax.psum_scatter(
        outer_rows(columns, upstream), ("dp", "seq"), scatter_dimension=0, tiled=True
    )
    gate_piece = lax.all_gather(w_gate, ("dp", "seq"), axis=0, tiled=True)
    up_piece = lax.all_gather(w_up, ("dp", "seq"), axis=0, tiled=True)
    part = times_transposed(d_gate, gate_piece) + times_transposed(d_up, up_piece)
    gain_two_term = jnp.sum(part * normed_two, axis=0)
    ffn_terms = (gain_two_term, outer_rows(acts_two, d_gate), outer_rows(acts_two, d_up))
    grad_gain_two, grad_gate, grad_up = (
        lax.psum_scatter(ffn_terms[0], ("dp", "seq"), scatter_dimension=0, tiled=True),
        lax.psum_scatter(ffn_terms[1], ("dp", "seq"), scatter_dimension=0, tiled=True),
        lax.psum_scatter(ffn_terms[2], ("dp", "seq"), scatter_dimension=0, tiled=True),
    )
    grad_res = upstream.astype(jnp.float32) + norm_back(part * gain_float, normed_two, inverse_two)
    grad_res_low = grad_res.astype(jnp.bfloat16)
    out_w_term = outer_rows(mixed_heads, grad_res_low)
    d_heads = (
        times_transposed(grad_res_low, out_w)
        .astype(jnp.bfloat16)
        .reshape(seqs_here, rows_here, KV_HEADS, group_size, HEAD)
    )
    query_grads = []
    key_list = []
    value_list = []
    for seq_number in range(seqs_here):
        heads_one = d_heads[seq_number]
        log_total = log_totals[seq_number]
        row_dots = jnp.sum(heads_one.astype(jnp.float32) * attended_list[seq_number], axis=-1)
        row_dots = jnp.transpose(row_dots, (1, 2, 0))[..., None]

        def back_block(grad_query, block_number):
            scores, visible, block_keys, block_values = block_scores(seq_number, block_number)
            probs = jnp.where(visible, jnp.exp(scores - log_total), 0.0)
            d_probs = jnp.einsum(
                "qkgd,jkd->kgqj", heads_one, block_values, preferred_element_type=jnp.float32
            )
            d_scores = (probs * (d_probs - row_dots)).astype(jnp.bfloat16)
            grad_query = grad_query + jnp.einsum(
                "kgqj,jkd->qkgd", d_scores, block_keys, preferred_element_type=jnp.float32
            )
            grad_keys = jnp.einsum(
                "kgqj,qkgd->jkd", d_scores, queries[seq_number], preferred_element_type=jnp.float32
            )
            grad_values = jnp.einsum(
                "kgqj,qkgd->jkd",
                probs.astype(jnp.bfloat16),
                heads_one,
                preferred_element_type=jnp.float32,
            )
            return (grad_query, (grad_keys, grad_values))

        grad_query_one, key_value_terms = lax.scan(
            back_block,
            jnp.zeros((rows_here, KV_HEADS, group_size, HEAD), jnp.float32),
            jnp.arange(blocks, dtype=jnp.int32),
        )
        query_grads.append(grad_query_one)
        key_list.append(key_value_terms[0].reshape(length, KV_HEADS * HEAD) * head_scale)
        value_list.append(key_value_terms[1].reshape(length, KV_HEADS * HEAD))
    key_terms = jnp.stack(key_list)
    value_terms = jnp.stack(value_list)
    keys_grad, values_grad = (
        lax.psum_scatter(key_terms, "seq", scatter_dimension=1, tiled=True),
        lax.psum_scatter(value_terms, "seq", scatter_dimension=1, tiled=True),
    )
    grad_query = jnp.stack(query_grads).reshape(total_rows, HEADS, HEAD)
    query_grad = rotate_back(grad_query * head_scale, cosine, sine_table)
    query_grad = query_grad.reshape(total_rows, HEADS * HEAD).astype(jnp.bfloat16)
    key_grad = rotate_back(keys_grad.reshape(total_rows, KV_HEADS, HEAD), cosine, sine_table)
    key_grad = key_grad.reshape(total_rows, KV_HEADS * HEAD).astype(jnp.bfloat16)
    value_grad = values_grad.reshape(total_rows, KV_HEADS * HEAD).astype(jnp.bfloat16)
    d_acts_one = (
        times_transposed(query_grad, query_w)
        + times_transposed(key_grad, key_w)
        + times_transposed(value_grad, value_w)
    )
    gain_one_term = jnp.sum(d_acts_one * normed_one, axis=0)
    attn_terms = (
        gain_one_term,
        outer_rows(acts_one, query_grad),
        outer_rows(acts_one, key_grad),
        outer_rows(acts_one, value_grad),
        out_w_term,
    )
    grad_gain_one, grad_query_w, grad_key_w, grad_value_w, grad_out_w = (
        lax.psum_scatter(attn_terms[0], ("dp", "seq"), scatter_dimension=0, tiled=True),
        lax.psum_scatter(attn_terms[1], ("dp", "seq"), scatter_dimension=0, tiled=True),
        lax.psum_scatter(attn_terms[2], ("dp", "seq"), scatter_dimension=0, tiled=True),
        lax.psum_scatter(attn_terms[3], ("dp", "seq"), scatter_dimension=0, tiled=True),
        lax.psum_scatter(attn_terms[4], ("dp", "seq"), scatter_dimension=0, tiled=True),
    )
    grad_input = grad_res + norm_back(d_acts_one * gain_one, normed_one, inverse_one)
    return (
        output.reshape(seqs_here, rows_here, width),
        grad_input.reshape(seqs_here, rows_here, width),
        grad_gain_one,
        grad_query_w,
        grad_key_w,
        grad_value_w,
        grad_out_w,
        grad_gain_two,
        grad_gate,
        grad_up,
        grad_down,
    )


def solution(mesh):
    in_specs = (
        P("dp", "seq", None),
        P("dp", "seq"),
        P(("dp", "seq")),
        P(("dp", "seq"), None),
        P(("dp", "seq"), None),
        P(("dp", "seq"), None),
        P(("dp", "seq"), None),
        P(("dp", "seq")),
        P(("dp", "seq"), None),
        P(("dp", "seq"), None),
        P(("dp", "seq"), None),
        P("dp", "seq", None),
    )
    out_specs = (
        P("dp", "seq", None),
        P("dp", "seq", None),
        P(("dp", "seq")),
        P(("dp", "seq"), None),
        P(("dp", "seq"), None),
        P(("dp", "seq"), None),
        P(("dp", "seq"), None),
        P(("dp", "seq")),
        P(("dp", "seq"), None),
        P(("dp", "seq"), None),
        P(("dp", "seq"), None),
    )
    return jax.shard_map(
        on_device, mesh=mesh, in_specs=in_specs, out_specs=out_specs, check_vma=False
    )
```

profile of v0, /device:TPU:1, one launch (start us, length us, event | category | flops | bytes accessed | tf_op | source)
XLA Modules:
  0.0 3194.5 jit_solution(8637403269354884015)
XLA Ops:
  8.7 10.3 all_gather.42
  20.8 39.4 %all-reduce.5 = (bf16[2048]{0:T(1024)(128)(2,1)S(1)}, bf16[2048]{0:T(1024)(128)(2,1)S(1)}) all-reduce(bf16[2048]{0:T(1024)(128)(2,1)S(1)} %dynamic-update-slice, bf16[2048]{0:T(1024)(128)(2,1)S(1)} %dynamic-update-slice.1), channel_id=1, replica_groups=mesh['dp'=4,'seq'=8] {'dp','seq'}, use_global_device_ids=true, to_apply=%add | all-reduce | flops 4096 | bytes 16384
  72.7 50.3 %all-gather.14.cloned.1.call-done = bf16[2048,256]{1,0:T(8,128)(2,1)} async-done(((bf16[64,256]{1,0:T(8,128)(2,1)}), bf16[2048,256]{1,0:T(8,128)(2,1)}) %all-gather.14.cloned.1.call-update) | async-done | bytes 1048592 | tf_op jit(solution)/shard_map/all_gather | solution.py:87
  129.5 18.4 all-gather.12.cloned.1.call-done
  149.4 28.8 all-gather.16.cloned.1.call-done
  179.7 78.7 %all-gather.18.cloned.1.call-done = bf16[2048,2048]{1,0:T(8,128)(2,1)} async-done(((bf16[64,2048]{1,0:T(8,128)(2,1)}), bf16[2048,2048]{1,0:T(8,128)(2,1)}) %all-gather.18.cloned.1.call-update) | async-done | bytes 8388624 | tf_op jit(solution)/shard_map/all_gather | solution.py:86
  258.4 12.4 copy.123
  270.9 5.8 fusion.174
  280.0 19.4 while.92
  285.0 4.8 select_reduce_fusion.5
  299.4 19.3 while.90
  304.4 4.8 select_reduce_fusion.4
  318.8 13.9 while.93
  327.7 5.0 fusion.283
  334.7 13.4 while.91
  343.2 5.0 fusion.277
  352.8 6.4 multiply_reduce_fusion.4
  361.8 121.5 %all-gather.22.cloned.1.call-done = bf16[2048,5632]{1,0:T(8,128)(2,1)} async-done(((bf16[64,5632]{1,0:T(8,128)(2,1)}), bf16[2048,5632]{1,0:T(8,128)(2,1)}) %all-gather.22.cloned.1.call-update) | async-done | bytes 23068688 | tf_op jit(solution)/shard_map/all_gather | solution.py:197
  483.3 12.6 fusion.175
  495.9 133.1 %all-gather.24.cloned.1.call-done = bf16[2048,5632]{1,0:T(8,128)(2,1)} async-done(((bf16[64,5632]{1,0:T(8,128)(2,1)}), bf16[2048,5632]{1,0:T(8,128)(2,1)}) %all-gather.24.cloned.1.call-update) | async-done | bytes 23068688 | tf_op jit(solution)/shard_map/all_gather | solution.py:198
  628.9 12.8 fusion.176
  641.7 132.9 %all-gather.26.cloned.1.call-done = bf16[5632,2048]{1,0:T(8,128)(2,1)} async-done(((bf16[176,2048]{1,0:T(8,128)(2,1)}), bf16[5632,2048]{1,0:T(8,128)(2,1)}) %all-gather.26.cloned.1.call-update) | async-done | bytes 23068688 | tf_op jit(solution)/shard_map/all_gather | solution.py:209
  774.6 18.6 multiply_convert_fusion
  793.2 12.6 fusion.177
  805.8 14.7 multiply_reduce_fusion
  823.6 6.5 convolution_convert_fusion
  837.1 59.4 %while.95 = (s32[]{:T(128)}, f32[128,4,8,64]{0,3,2,1:T(8,128)}, f32[2,512,4,64]{1,3,2,0:T(8,128)}, f32[2,512,4,64]{1,0,3,2:T(2,128)}, bf16[2,1024,4,64]{1,3,2,0:...) while((s32[]{:T(128)}, f32[128,4,8,64]{0,3,2,1:T(8,128)}, ...), condition=%wide.region_22.23_spmd.clone, body=%wide.region_21.22_spmd.clone.sunk | while | flops 1368064640 | bytes 136319904 | solution.py:271
  856.3 10.4 dynamic_update_slice.26
  886.1 10.4 dynamic_update_slice.26
  902.5 59.8 %while.94 = (s32[]{:T(128)}, f32[128,4,8,64]{0,3,2,1:T(8,128)}, f32[2,512,4,64]{1,3,2,0:T(8,128)}, f32[2,512,4,64]{1,0,3,2:T(2,128)}, bf16[2,1024,4,64]{1,3,2,0:...) while((s32[]{:T(128)}, f32[128,4,8,64]{0,3,2,1:T(8,128)}, ...), condition=%wide.region_19.20_spmd.clone, body=%wide.region_18.19_spmd.clone.sunk | while | flops 1368064640 | bytes 136319904 | solution.py:271
  922.1 10.4 dynamic_update_slice.24
  951.9 10.4 dynamic_update_slice.24
  977.2 33.1 %reduce-scatter.10.cloned.1.call-done = f32[2,128,256]{1,2,0:T(8,128)} async-done(((f32[2,1024,256]{1,2,0:T(8,128)}), f32[2,128,256]{1,2,0:T(8,128)}) %reduce-scatter.10.cloned.1.call-update) | async-done | bytes 262160 | tf_op jit(solution)/shard_map/reduce_scatter | solution.py:282
  1014.4 40.8 %reduce-scatter.12.cloned.1.call-done = f32[2,128,256]{1,2,0:T(8,128)} async-done(((f32[2,1024,256]{1,2,0:T(8,128)}), f32[2,128,256]{1,2,0:T(8,128)}) %reduce-scatter.12.cloned.1.call-update) | async-done | bytes 262160 | tf_op jit(solution)/shard_map/reduce_scatter | solution.py:283
  1066.6 8.2 fusion.179
  1076.7 8.2 fusion.153
  1086.1 19.7 fusion.181
  1105.8 19.7 fusion.182
  1126.8 19.9 fusion.183
  1150.1 7.3 fusion.178
  1157.4 12.1 fusion.148
  1178.3 39.4 %all-reduce.4 = (f32[2048]{0:T(1024)S(1)}, f32[2048]{0:T(1024)S(1)}) all-reduce(f32[2048]{0:T(1024)S(1)} %get-tuple-element.1231, f32[2048]{0:T(1024)S(1)} %copy-done.43), channel_id=4, replica_groups=mesh['dp'=4,'seq'=8] {'dp','seq'}, use_global_device_ids=true, to_apply=%region_27.28.clone | all-reduce | flops 4096 | bytes 32768
  1222.4 102.1 %reduce-scatter.18.cloned.1.call-done = f32[64,256]{1,0:T(8,128)} async-done(((f32[2048,256]{1,0:T(8,128)}), f32[64,256]{1,0:T(8,128)}) %reduce-scatter.18.cloned.1.call-update) | async-done | bytes 65552 | tf_op jit(solution)/shard_map/reduce_scatter | solution.py:308
  1324.4 187.2 %reduce-scatter.14.cloned.1.call-done = f32[64,2048]{1,0:T(8,128)} async-done(((f32[2048,2048]{1,0:T(8,128)}), f32[64,2048]{1,0:T(8,128)}) %reduce-scatter.14.cloned.1.call-update) | async-done | bytes 524304 | tf_op jit(solution)/shard_map/reduce_scatter | solution.py:306
  1511.6 187.2 %reduce-scatter.20.cloned.1.call-done = f32[64,2048]{1,0:T(8,128)} async-done(((f32[2048,2048]{1,0:T(8,128)}), f32[64,2048]{1,0:T(8,128)}) %reduce-scatter.20.cloned.1.call-update) | async-done | bytes 524304 | tf_op jit(solution)/shard_map/reduce_scatter | solution.py:309
  1698.8 496.7 %reduce-scatter.22.cloned.1.call-done = f32[64,5632]{1,0:T(8,128)} async-done(((f32[2048,5632]{1,0:T(8,128)}), f32[64,5632]{1,0:T(8,128)}) %reduce-scatter.22.cloned.1.call-update) | async-done | bytes 1441808 | tf_op jit(solution)/shard_map/reduce_scatter | solution.py:230
  2195.6 495.8 %reduce-scatter.24.cloned.1.call-done = f32[64,5632]{1,0:T(8,128)} async-done(((f32[2048,5632]{1,0:T(8,128)}), f32[64,5632]{1,0:T(8,128)}) %reduce-scatter.24.cloned.1.call-update) | async-done | bytes 1441808 | tf_op jit(solution)/shard_map/reduce_scatter | solution.py:231
  2691.4 495.8 %reduce-scatter.26.cloned.1.call-done = f32[176,2048]{1,0:T(8,128)} async-done(((f32[5632,2048]{1,0:T(8,128)}), f32[176,2048]{1,0:T(8,128)}) %reduce-scatter.26.cloned.1.call-update) | async-done | bytes 1441808 | tf_op jit(solution)/shard_map/reduce_scatter | solution.py:220
  (391 shorter events, 224.6 us)
Async XLA Ops:
  7.2 65.1 %copy-start.8 = (bf16[2,128,2048]{2,1,0:T(8,128)(2,1)S(1)}, bf16[2,128,2048]{2,1,0:T(8,128)(2,1)}, u32[]{:S(2)}) copy-start(bf16[2,128,2048]{2,1,0:T(8,128)(2,1)} %param.24) | copy-start | bytes 3145732
  7.2 60.2 %all-gather.10.cloned.1.call-start = ((), (), s32[]{:S(2)}) async-start(), calls=%async_computation.9 | async-start | bytes 1081344 | tf_op jit(solution)/shard_map/all_gather | solution.py:88
  7.9 115.0 %all-gather.14.cloned.1.call-start = ((), (), s32[]{:S(2)}) async-start(), calls=%async_computation.11 | async-start | bytes 1081344 | tf_op jit(solution)/shard_map/all_gather | solution.py:87
  8.7 139.2 %all-gather.12.cloned.1.call-start = ((), (), s32[]{:S(2)}) async-start(), calls=%async_computation.10 | async-start | bytes 1179648 | tf_op jit(solution)/shard_map/all_gather | solution.py:127
  60.1 12.5 copy-start.37
  62.7 61.7 %copy-start.39 = (f32[256]{0:T(256)}, f32[256]{0:T(256)S(1)}, u32[]{:S(2)}) copy-start(f32[256]{0:T(256)S(1)} %get-tuple-element.1385) | copy-start | bytes 3076
  69.8 108.5 %all-gather.16.cloned.1.call-start = ((), (), s32[]{:S(2)}) async-start(), calls=%async_computation.12 | async-start | bytes 1179648 | tf_op jit(solution)/shard_map/all_gather | solution.py:126
  72.3 204.6 %copy-start.29 = (f32[256,64]{0,1:T(8,128)}, f32[256,64]{0,1:T(8,128)S(1)}, u32[]{:S(2)}) copy-start(f32[256,64]{0,1:T(8,128)S(1)} %get-tuple-element.1391) | copy-start | bytes 196612
  72.3 204.6 %copy-start.31 = (f32[256,64]{0,1:T(8,128)}, f32[256,64]{0,1:T(8,128)S(1)}, u32[]{:S(2)}) copy-start(f32[256,64]{0,1:T(8,128)S(1)} %get-tuple-element.1390) | copy-start | bytes 196612
  72.6 56.5 %copy-start.14 = (bf16[2,128,2048]{2,1,0:T(8,128)(2,1)}, bf16[2,128,2048]{2,1,0:T(8,128)(2,1)S(1)}, u32[]{:S(2)}) copy-start(bf16[2,128,2048]{2,1,0:T(8,128)(2,1)S(1)} %multiply_convert_fusion.4) | copy-start | bytes 3145732
  125.7 132.7 %all-gather.18.cloned.1.call-start = ((), (), s32[]{:S(2)}) async-start(), calls=%async_computation.13 | async-start | bytes 8650752 | tf_op jit(solution)/shard_map/all_gather | solution.py:86
  126.3 226.5 %all-gather.20.cloned.1.call-start = ((), (), s32[]{:S(2)}) async-start(), calls=%async_computation.14 | async-start | bytes 8650752 | tf_op jit(solution)/shard_map/all_gather | solution.py:89
  126.9 356.4 %all-gather.22.cloned.1.call-start = ((), (), s32[]{:S(2)}) async-start(), calls=%async_computation.15 | async-start | bytes 23789568 | tf_op jit(solution)/shard_map/all_gather | solution.py:197
  127.6 501.3 %all-gather.24.cloned.1.call-start = ((), (), s32[]{:S(2)}) async-start(), calls=%async_computation.16 | async-start | bytes 23789568 | tf_op jit(solution)/shard_map/all_gather | solution.py:198
  128.4 646.2 %all-gather.26.cloned.1.call-start = ((), (), s32[]{:S(2)}) async-start(), calls=%async_computation.17 | async-start | bytes 23789568 | tf_op jit(solution)/shard_map/all_gather | solution.py:209
  129.1 881.2 %reduce-scatter.10.cloned.1.call-start = ((), (), s32[]{:S(2)}) async-start(), calls=%async_computation.18 | async-start | bytes 2359296 | tf_op jit(solution)/shard_map/reduce_scatter | solution.py:282
  258.4 12.4 copy-start.15
  348.2 11.1 copy-start.41
  823.6 6.5 copy-start.10
  846.3 6.4 copy-start.3
  871.1 4.7 copy-start.2
  875.8 6.7 copy-start.3
  896.6 6.0 copy-start.42
  912.0 6.4 copy-start.5
  936.8 4.7 copy-start.4
  941.6 6.7 copy-start.5
  966.4 5.0 copy-start.22
  968.3 5.0 copy-start.21
  971.2 84.0 %reduce-scatter.12.cloned.1.call-start = ((), (), s32[]{:S(2)}) async-start(), calls=%async_computation.19 | async-start | bytes 2359296 | tf_op jit(solution)/shard_map/reduce_scatter | solution.py:283
  974.2 37.5 %copy-start.32 = (f32[256,64]{0,1:T(8,128)S(1)}, f32[256,64]{0,1:T(8,128)}, u32[]{:S(2)}) copy-start(f32[256,64]{0,1:T(8,128)} %copy-done.31) | copy-start | bytes 196612
  974.2 37.6 %copy-start.30 = (f32[256,64]{0,1:T(8,128)S(1)}, f32[256,64]{0,1:T(8,128)}, u32[]{:S(2)}) copy-start(f32[256,64]{0,1:T(8,128)} %copy-done.29) | copy-start | bytes 196612
  974.2 38.3 %copy-start.16 = (bf16[2,128,2048]{2,1,0:T(8,128)(2,1)S(1)}, bf16[2,128,2048]{2,1,0:T(8,128)(2,1)}, u32[]{:S(2)}) copy-start(bf16[2,128,2048]{2,1,0:T(8,128)(2,1)} %copy-done.14) | copy-start | bytes 3145732
  977.2 245.2 %reduce-scatter.16.cloned.1.call-start = ((), (), s32[]{:S(2)}) async-start(), calls=%async_computation.21 | async-start | bytes 2162688 | tf_op jit(solution)/shard_map/reduce_scatter | solution.py:307
  1014.3 43.8 %copy-start.36 = (f32[2,128,64]{1,0,2:T(2,128)S(1)}, f32[2,128,64]{1,0,2:T(2,128)}, u32[]{:S(2)}) copy-start(f32[2,128,64]{1,0,2:T(2,128)} %copy-done.35) | copy-start | bytes 196612
  1014.3 43.8 %copy-start.34 = (f32[2,128,64]{1,0,2:T(2,128)S(1)}, f32[2,128,64]{1,0,2:T(2,128)}, u32[]{:S(2)}) copy-start(f32[2,128,64]{1,0,2:T(2,128)} %copy-done.33) | copy-start | bytes 196612
  1014.3 43.9 %copy-start.6 = (f32[128,4,8,64]{0,3,2,1:T(8,128)S(1)}, f32[128,4,8,64]{0,3,2,1:T(8,128)}, u32[]{:S(2)}) copy-start(f32[128,4,8,64]{0,3,2,1:T(8,128)} %get-tuple-element.753) | copy-start | bytes 3145732
  1014.3 43.9 %copy-start.7 = (f32[128,4,8,64]{0,3,2,1:T(8,128)S(1)}, f32[128,4,8,64]{0,3,2,1:T(8,128)}, u32[]{:S(2)}) copy-start(f32[128,4,8,64]{0,3,2,1:T(8,128)} %get-tuple-element.754) | copy-start | bytes 3145732
  1014.4 310.1 %reduce-scatter.18.cloned.1.call-start = ((), (), s32[]{:S(2)}) async-start(), calls=%async_computation.22 | async-start | bytes 2162688 | tf_op jit(solution)/shard_map/reduce_scatter | solution.py:308
  1058.1 453.5 %reduce-scatter.14.cloned.1.call-start = ((), (), s32[]{:S(2)}) async-start(), calls=%async_computation.20 | async-start | bytes 17301504 | tf_op jit(solution)/shard_map/reduce_scatter | solution.py:306
  1074.9 624.0 %reduce-scatter.20.cloned.1.call-start = ((), (), s32[]{:S(2)}) async-start(), calls=%async_computation.23 | async-start | bytes 17301504 | tf_op jit(solution)/shard_map/reduce_scatter | solution.py:309
  1084.9 1110.7 %reduce-scatter.22.cloned.1.call-start = ((), (), s32[]{:S(2)}) async-start(), calls=%async_computation.24 | async-start | bytes 47579136 | tf_op jit(solution)/shard_map/reduce_scatter | solution.py:230
  1105.8 1585.6 %reduce-scatter.24.cloned.1.call-start = ((), (), s32[]{:S(2)}) async-start(), calls=%async_computation.25 | async-start | bytes 47579136 | tf_op jit(solution)/shard_map/reduce_scatter | solution.py:231
  1125.6 2061.6 %reduce-scatter.26.cloned.1.call-start = ((), (), s32[]{:S(2)}) async-start(), calls=%async_computation.26 | async-start | bytes 47579136 | tf_op jit(solution)/shard_map/reduce_scatter | solution.py:220
  1150.1 7.3 copy-start.13
  1150.1 7.3 copy-start.19
  1169.5 6.7 copy-start.9
  1169.5 6.7 copy-start.38
  1169.5 6.7 copy-start.40
  (24 other events, 64.9 us)
Sparse Core Ops, SparseCore 0:
  10.9 56.4 all-gather.9
  70.3 52.6 all-gather.13
  125.4 22.4 all-gather.11
  150.2 28.0 all-gather.15
  180.9 77.4 all-gather.17
  261.2 76.0 all-gather.19
  340.1 143.1 all-gather.21
  486.1 142.7 all-gather.23
  631.8 142.7 all-gather.25
  971.3 38.9 reduce-scatter.9
  1014.0 41.2 reduce-scatter.11
  1057.9 131.0 reduce-scatter.15
  1192.0 132.4 reduce-scatter.17
  1327.2 184.3 reduce-scatter.13
  1514.3 184.4 reduce-scatter.19
  1701.6 493.9 reduce-scatter.21
  2198.3 493.0 reduce-scatter.23
  2694.1 493.0 reduce-scatter.25
where the time goes:
time: 3200 us; the launch traced here: 3190 us
  waiting for transfers between devices  2610 us (82%)
  matrix products  295 us (9%)
  local copies, waits for them, and re-layouts  121 us (4%)
  blocking collectives  89.1 us (3%)
  other arithmetic  58.1 us (2%)
    reduce_scatter x1, waiting for transfers between devices, on_device(): lax.psum_scatter(ffn_terms[1], ('dp', 'seq'), scatter_dimension=0, tiled=...  497 us
    reduce_scatter x1, waiting for transfers between devices, on_device(): lax.psum_scatter(ffn_terms[2], ('dp', 'seq'), scatter_dimension=0, tiled=...  496 us
    reduce_scatter x1, waiting for transfers between devices, on_device(): lax.psum_scatter(outer_rows(columns, upstream), ('dp', 'seq'), scatter_di...  496 us
    reduce_scatter x1, waiting for transfers between devices, on_device(): lax.psum_scatter(attn_terms[4], ('dp', 'seq'), scatter_dimension=0, tiled...  187 us
    reduce_scatter x1, waiting for transfers between devices, on_device(): lax.psum_scatter(attn_terms[1], ('dp', 'seq'), scatter_dimension=0, tiled...  187 us
    all_gather x1, waiting for transfers between devices, on_device(): up_piece = lax.all_gather(w_up, ('dp', 'seq'), axis=0, tiled=True)  133 us
    all_gather x1, waiting for transfers between devices, on_device(): lax.all_gather(w_down, ('dp', 'seq'), axis=0, tiled=True)  133 us
    all_gather x1, waiting for transfers between devices, on_device(): gate_piece = lax.all_gather(w_gate, ('dp', 'seq'), axis=0, tiled=True)  122 us
  transfers between devices with their start and end apart: 18, of which 16 were waited for; matrix products, arithmetic and copies ran while one was open for 9% of the time, Pallas kernels for 0%

commit v1 on v0

v1 whole, which is shorter than its diff:
```python
import functools
import math

import jax
import jax.numpy as jnp
from jax import lax
from jax.experimental import pallas as pl
from jax.experimental.pallas import tpu as pltpu
from jax.sharding import PartitionSpec as P

HEADS = 32
KV_HEADS = 4
HEAD = 64
LANES = 128
ROWS = 256
CHUNK = 128

EPSILON = 1e-05
ROPE_BASE = 10000.0
MASKED = -1e30
VMEM_BYTES = 56 * 1024 * 1024

BF16 = jnp.bfloat16
F32 = jnp.float32
LIGHT = pl.CostEstimate(flops=1, bytes_accessed=1, transcendentals=0)


def swap(block, distance):
    size = lax.axis_size("seq")
    return lax.ppermute(block, "seq", [(i, i ^ distance) for i in range(size)])


def shift(block, step):
    size = lax.axis_size("dp")
    return lax.ppermute(block, "dp", [(i, (i + step) % size) for i in range(size)])


def tie(*values):
    return lax.optimization_barrier(values)


def gather_seq_first(block):
    if lax.axis_size("seq") != 8:
        return (lax.all_gather(block, "seq", axis=0),)
    return swap(block, 2), swap(block, 4), swap(block, 1)


def gather_seq_rest(block, first):
    size = lax.axis_size("seq")
    if size != 8:
        me = lax.axis_index("seq")
        return [lax.dynamic_index_in_dim(first[0], me ^ d, 0, keepdims=False) for d in range(size)]
    half = block.shape[0] // 2
    along_x, along_y, beside = first
    across = [swap(along_y[:half], 2), swap(along_x[half:], 4)]
    blocks = [block, beside, along_x, swap(along_x, 1), along_y, swap(along_y, 1)]
    across = jnp.concatenate(across, axis=0)
    return blocks + [across, swap(across, 1)]


def gather_seq(block):
    return gather_seq_rest(block, gather_seq_first(block))


def scatter_seq_first(parts):
    size = lax.axis_size("seq")
    if size != 8:
        order = lax.axis_index("seq") ^ jnp.arange(size)
        parts = jnp.take(jnp.stack(parts), order, axis=0)
        return (lax.psum_scatter(parts, "seq", scatter_dimension=0),)
    half = parts[0].shape[0] // 2
    across = parts[6] + swap(parts[7], 1)
    corner = swap(across[:half], 2), swap(across[half:], 4)
    return [parts[2 * i] + swap(parts[2 * i + 1], 1) for i in range(3)], corner


def scatter_seq_rest(first):
    if lax.axis_size("seq") != 8:
        return first[0].astype(F32)
    (own, for_x, for_y), (from_x, from_y) = first
    half = own.shape[0] // 2
    for_y = jnp.concatenate([for_y[:half] + from_x, for_y[half:]], axis=0)
    for_x = jnp.concatenate([for_x[:half], for_x[half:] + from_y], axis=0)
    return own.astype(F32) + swap(for_x, 2).astype(F32) + swap(for_y, 4).astype(F32)


def exchange_seq(blocks):
    return lax.all_to_all(blocks, "seq", 0, 0, tiled=True)


def deal(block, back=False):
    n_dp, n_seq = lax.axis_size("dp"), lax.axis_size("seq")
    pairs = [(g, (g % n_dp) * n_seq + g // n_dp) for g in range(n_dp * n_seq)]
    if back:
        pairs = [(there, here) for here, there in pairs]
    return lax.ppermute(block, ("dp", "seq"), pairs)


def halves(block, axis):
    middle = block.shape[axis] // 2
    return (
        lax.slice_in_dim(block, 0, middle, axis=axis),
        lax.slice_in_dim(block, middle, block.shape[axis], axis=axis),
    )


def gather_dp_first(block):
    return shift(block, 1), shift(block, -1)


def gather_dp_rest(block, first, axis, whole=None, offset=0):
    size = lax.axis_size("dp")
    me = lax.axis_index("dp")
    if whole is None:
        whole = jnp.zeros((size,) + block.shape, block.dtype)

    def put(whole, piece, distance):
        return lax.dynamic_update_slice(whole, piece[None], ((me + distance) % size, offset, 0))

    whole = put(whole, block, 0)
    up, down = first
    for step in range(1, size // 2):
        if step > 1:
            up, down = shift(up, 1), shift(down, -1)
        whole = put(put(whole, up, -step), down, step)
    far = [shift(halves(up, axis)[0], 1), shift(halves(down, axis)[1], -1)]
    return put(whole, jnp.concatenate(far, axis=axis), size // 2)


def term_for(terms, distance):
    size = lax.axis_size("dp")
    index = (lax.axis_index("dp") + distance) % size
    if isinstance(terms, tuple):
        terms, low, rows = terms
        return lax.dynamic_slice(terms, (index, low, 0), (1, rows, terms.shape[2]))[0]
    return lax.dynamic_index_in_dim(terms, index, 0, keepdims=False)


def scatter_dp_first(terms, axis):
    size = lax.axis_size("dp")
    far = halves(term_for(terms, size // 2), axis)
    return shift(far[0], 1), shift(far[1], -1)


def scatter_dp_rest(terms, first, axis):
    size = lax.axis_size("dp")
    up, down = first
    for step in range(size // 2 - 1, 0, -1):
        for_up, for_down = term_for(terms, step), term_for(terms, -step)
        if step == size // 2 - 1:
            kept = halves(for_up, axis)
            up = jnp.concatenate([kept[0] + up, kept[1]], axis=axis)
            kept = halves(for_down, axis)
            down = jnp.concatenate([kept[0], kept[1] + down], axis=axis)
        else:
            up, down = for_up + up, for_down + down
        up, down = shift(up, 1), shift(down, -1)
    return term_for(terms, 0) + up + down


def padded(units):
    return units if units % LANES in (0, LANES // 2) else -(-units // LANES) * LANES


def chunk_widths(units):
    widths = []
    left = units
    for width in (256, 128, 64):
        while left >= width:
            widths.append(width)
            left -= width
    return widths


def interleave(gate, up):
    pieces = []
    offset = 0
    for width in chunk_widths(gate.shape[-1]):
        pieces += [gate[..., offset : offset + width], up[..., offset : offset + width]]
        offset += width
    return jnp.concatenate(pieces, axis=-1)


def separate(both):
    gate, up = [], []
    offset = 0
    for width in chunk_widths(both.shape[-1] // 2):
        gate.append(both[..., offset : offset + width])
        up.append(both[..., offset + width : offset + 2 * width])
        offset += 2 * width
    return jnp.concatenate(gate, axis=-1), jnp.concatenate(up, axis=-1)


def contract(left, right, dims):
    return lax.dot_general(left, right, ((dims[0], dims[1]), ((), ())), preferred_element_type=F32)


def nt(left, right):
    return contract(left, right, ((1,), (1,)))


def nn(left, right):
    return contract(left, right, ((1,), (0,)))


def tn(left, right):
    return contract(left, right, ((0,), (0,)))


def params(**more):
    return pltpu.CompilerParams(vmem_limit_bytes=VMEM_BYTES, **more)


def ffn_kernel(count, *refs):
    acts = refs[:count]
    grads = refs[count : 2 * count]
    w_both, w_down = refs[2 * count : 2 * count + 2]
    outs = refs[2 * count + 2 :]
    n_out, f_out, h_out, d_out = (outs[i * count : (i + 1) * count] for i in range(4))
    units = w_down.shape[0]
    width_out = w_down.shape[1]
    for one in range(count):
        x = acts[one][...]
        g = grads[one][...]
        offset = 0
        for width in chunk_widths(units):
            pre = nn(x, w_both[:, 2 * offset : 2 * offset + 2 * width])
            d_hidden = nt(g, w_down[offset : offset + width, :])
            if width % LANES == 0:
                gate, up = pre[:, :width], pre[:, width:]
            else:
                gate, up = pre, pltpu.roll(pre, width, 1)
                d_hidden = jnp.concatenate([d_hidden, d_hidden], axis=1)
            sig = 1.0 / (1.0 + jnp.exp(-gate))
            silu = gate * sig
            hidden = silu * up
            d_gate = d_hidden * up * sig * (1.0 + gate * (1.0 - sig))
            d_up = d_hidden * silu
            if width % LANES == 0:
                d_out[one][:, 2 * offset : 2 * offset + width] = d_gate.astype(BF16)
                d_out[one][:, 2 * offset + width : 2 * offset + 2 * width] = d_up.astype(BF16)
                h_out[one][:, offset : offset + width] = hidden.astype(BF16)
            else:
                lane = lax.broadcasted_iota(jnp.int32, pre.shape, 1)
                both = jnp.where(lane < width, d_gate, pltpu.roll(d_up, width, 1))
                d_out[one][:, 2 * offset : 2 * offset + 2 * width] = both.astype(BF16)
                h_out[one][:, offset : offset + width] = hidden[:, :width].astype(BF16)
            offset += width
        both = d_out[one][...]
        hidden = h_out[one][...]
        for start in range(0, width_out, 512):
            columns = slice(start, start + 512)
            n_out[one][:, columns] = nt(both, w_both[columns, :]).astype(BF16)
            f_out[one][:, columns] = nn(hidden, w_down[:, columns]).astype(BF16)


def ffn(acts, grads, w_both, w_down):
    count = len(acts)
    rows, width = acts[0].shape
    units = w_down.shape[0]
    shapes = (
        [jax.ShapeDtypeStruct((rows, width), BF16)] * (2 * count)
        + [jax.ShapeDtypeStruct((rows, units), BF16)] * count
        + [jax.ShapeDtypeStruct((rows, 2 * units), BF16)] * count
    )
    out = pl.pallas_call(
        functools.partial(ffn_kernel, count),
        out_shape=shapes,
        compiler_params=params(),
        cost_estimate=LIGHT,
        name="ffn",
    )(*acts, *grads, w_both, w_down)
    return [list(out[i * count : (i + 1) * count]) for i in range(4)]


def outer_kernel(count, along_left, *refs):
    left = refs[:count]
    right = refs[count : 2 * count]
    out, left_all, right_all = refs[2 * count :]
    rows = left[0].shape[0]

    def fill(target, sources):
        for one in range(count):
            target[one * rows : (one + 1) * rows, :] = sources[one][...]

    still, still_from = (right_all, right) if along_left else (left_all, left)
    moving, moving_from = (left_all, left) if along_left else (right_all, right)

    @pl.when(pl.program_id(0) == 0)
    def _():
        fill(still, still_from)

    fill(moving, moving_from)
    out[...] = tn(left_all[...], right_all[...]).astype(out.dtype)


def outer(left, right, along_left, block):
    count = len(left)
    rows, left_width = left[0].shape
    right_width = right[0].shape[1]
    left_block = block if along_left else left_width
    right_block = right_width if along_left else block
    steps = (left_width if along_left else right_width) // block
    moving = lambda i: (0, i)
    still = lambda i: (0, 0)
    return pl.pallas_call(
        functools.partial(outer_kernel, count, along_left),
        out_shape=jax.ShapeDtypeStruct((left_width, right_width), BF16),
        grid=(steps,),
        in_specs=[pl.BlockSpec((rows, left_block), moving if along_left else still)] * count
        + [pl.BlockSpec((rows, right_block), still if along_left else moving)] * count,
        out_specs=pl.BlockSpec(
            (left_block, right_block), (lambda i: (i, 0)) if along_left else (lambda i: (0, i))
        ),
        scratch_shapes=[
            pltpu.VMEM((count * rows, left_block), BF16),
            pltpu.VMEM((count * rows, right_block), BF16),
        ],
        compiler_params=params(),
        cost_estimate=LIGHT,
        name="outer",
    )(*left, *right)


def multiply_kernel(count, transposed, *refs):
    right = refs[count]
    product = nt if transposed else nn
    for one in range(count):
        left, out = refs[one], refs[count + 1 + one]
        out[...] = product(left[...], right[...]).astype(out.dtype)


def multiply(lefts, right, transposed=False):
    rows = lefts[0].shape[0]
    columns = right.shape[0 if transposed else 1]
    return pl.pallas_call(
        functools.partial(multiply_kernel, len(lefts), transposed),
        out_shape=[jax.ShapeDtypeStruct((rows, columns), BF16)] * len(lefts),
        compiler_params=params(),
        cost_estimate=LIGHT,
        name="multiply",
    )(*lefts, right)


def enter_kernel(count, *refs):
    gain, right = refs[count], refs[count + 1]
    acts_out, raw_out = refs[count + 2 : 2 * count + 2], refs[2 * count + 2 :]
    for one in range(count):
        values = refs[one][...].astype(F32)
        inverse = lax.rsqrt(jnp.mean(values * values, axis=-1, keepdims=True) + EPSILON)
        acts = (values * inverse * gain[...]).astype(BF16)
        acts_out[one][...] = acts
        raw_out[one][...] = nn(acts, right[...])


def enter(blocks, gain, right):
    count = len(blocks)
    rows, width = blocks[0].shape
    out = pl.pallas_call(
        functools.partial(enter_kernel, count),
        out_shape=[jax.ShapeDtypeStruct((rows, width), BF16)] * count
        + [jax.ShapeDtypeStruct((rows, right.shape[1]), F32)] * count,
        compiler_params=params(),
        cost_estimate=LIGHT,
        name="enter",
    )(*blocks, gain, right)
    return list(out[:count]), list(out[count:])


def turned(tile):
    lane = lax.broadcasted_iota(jnp.int32, tile.shape, 1)
    return jnp.where(
        lane % HEAD < HEAD // 2,
        pltpu.roll(tile, LANES - HEAD // 2, 1),
        pltpu.roll(tile, HEAD // 2, 1),
    )


def visible(first, low, high, start, diagonal):
    places = low + lax.broadcasted_iota(jnp.int32, (high - low, ROWS), 0)
    seen = places >= first
    if diagonal:
        seen &= places <= start + lax.broadcasted_iota(jnp.int32, (high - low, ROWS), 1)
    return seen


def attend_kernel(blocks, me_ref, *refs):
    raw_refs, refs = refs[:blocks], refs[blocks:]
    (cos_ref, sin_ref, first_ref), refs = refs[:3], refs[3:]
    mixed_refs, refs = refs[:blocks], refs[blocks:]
    kept_ref, q_ref, kv_ref, lse_ref, keys, vals_t, scores, weights, turned_out = refs
    me = me_ref[0]
    here = raw_refs[0].shape[1]
    pairs = q_ref.shape[1]
    length = q_ref.shape[2]
    scale = 1.0 / math.sqrt(HEAD)
    lane = lax.broadcasted_iota(jnp.int32, (here, LANES), 1)
    low_half = lane < HEAD
    for one in range(blocks):
        rows = pl.ds(pl.multiple_of((one ^ me) * here, here), here)
        raw = raw_refs[one][0]
        cosine, sine = cos_ref[0, rows, :], sin_ref[0, rows, :]
        for pair in range(pairs):
            tile = raw[:, pair * LANES : (pair + 1) * LANES]
            tile = tile * cosine + turned(tile) * sine
            q_ref[0, pair, rows, :] = (tile * scale).astype(BF16)
        tile = raw[:, pairs * LANES :]
        tile = jnp.where(low_half, tile * cosine + turned(tile) * sine, tile)
        kv_ref[0, rows, :] = tile.astype(BF16)
    for one in range(blocks):
        rows = slice(one * here, (one + 1) * here)
        tile = kv_ref[0, rows, :].astype(F32)
        other = pltpu.roll(tile, HEAD, 1)
        keys[0, rows, :] = jnp.where(low_half, tile, 0.0).astype(BF16)
        keys[1, rows, :] = jnp.where(low_half, 0.0, other).astype(BF16)
        vals_t[:, rows] = other.T[:HEAD].astype(BF16)

    for start in range(0, length, ROWS):
        times = slice(start, start + ROWS)
        first = first_ref[0, :, times]
        end = start + ROWS

        def one_head(head, carry):
            query = q_ref[0, head // 2, times, :]
            top = jnp.full((8, ROWS), MASKED, F32)
            for low in range(0, end, CHUNK):
                rows = slice(low, low + CHUNK)
                score = nt(keys[head % 2, rows, :], query)
                seen = visible(first, low, low + CHUNK, start, low >= start)
                score = jnp.where(seen, score, MASKED)
                scores[rows, :] = score
                top = jnp.maximum(top, jnp.max(score.reshape(CHUNK // 8, 8, ROWS), axis=0))
            top = jnp.max(top, axis=0, keepdims=True)
            total = jnp.zeros((8, ROWS), F32)
            for low in range(0, end, CHUNK):
                rows = slice(low, low + CHUNK)
                expo = jnp.exp(scores[rows, :] - top)
                total = total + jnp.sum(expo.reshape(CHUNK // 8, 8, ROWS), axis=0)
                weights[rows, :] = expo.astype(BF16)
            total = jnp.sum(total, axis=0, keepdims=True)
            turned_out[head] = nn(vals_t[:, :end], weights[:end, :]) / total
            lse_ref[0, head, :, times] = top + jnp.log(total)
            return carry

        lax.fori_loop(0, 2 * pairs, one_head, 0)
        done = turned_out[...].reshape(2 * pairs * HEAD, ROWS).T.astype(BF16)
        kept_ref[0, times, :] = done
    for one in range(blocks):
        rows = pl.ds(pl.multiple_of((one ^ me) * here, here), here)
        mixed_refs[one][0] = kept_ref[0, rows, :]


def attend_back_kernel(blocks, me_ref, *refs):
    grad_refs, refs = refs[:blocks], refs[blocks:]
    (kept_ref, q_ref, kv_ref, lse_ref, cos_ref, sin_ref, first_ref), refs = refs[:7], refs[7:]
    raw_refs, refs = refs[:blocks], refs[blocks:]
    keys, vals, keys_t, grads, weights, d_scores, dots, turned_out, acc_k, acc_v, result = refs
    me = me_ref[0]
    here = raw_refs[0].shape[1]
    pairs = q_ref.shape[1]
    length = q_ref.shape[2]
    scale = 1.0 / math.sqrt(HEAD)
    lane = lax.broadcasted_iota(jnp.int32, (here, LANES), 1)
    low_half = lane < HEAD
    acc_k[...] = jnp.zeros_like(acc_k)
    acc_v[...] = jnp.zeros_like(acc_v)
    for one in range(blocks):
        rows = slice(one * here, (one + 1) * here)
        tile = kv_ref[0, rows, :].astype(F32)
        other = pltpu.roll(tile, HEAD, 1)
        keys[0, rows, :] = jnp.where(low_half, tile, 0.0).astype(BF16)
        keys[1, rows, :] = jnp.where(low_half, 0.0, other).astype(BF16)
        vals[0, rows, :] = jnp.where(low_half, other, 0.0).astype(BF16)
        vals[1, rows, :] = jnp.where(low_half, 0.0, tile).astype(BF16)
        keys_t[:, rows] = tile.T[:HEAD].astype(BF16)
        there = pl.ds(pl.multiple_of((one ^ me) * here, here), here)
        for pair in range(pairs):
            grads[pair, there, :] = grad_refs[one][0, :, pair * LANES : (pair + 1) * LANES]

    wide_lane = lax.broadcasted_iota(jnp.int32, (ROWS, LANES), 1)
    for start in range(0, length, ROWS):
        times = slice(start, start + ROWS)
        first = first_ref[0, :, times]
        end = start + ROWS
        for pair in range(pairs):
            product = grads[pair, times, :].astype(F32) * kept_ref[
                0, times, pair * LANES : (pair + 1) * LANES
            ].astype(F32)
            product = product.T
            dots[2 * pair] = jnp.sum(product[:HEAD], axis=0, keepdims=True)
            dots[2 * pair + 1] = jnp.sum(product[HEAD:], axis=0, keepdims=True)

        def one_head(head, carry):
            odd = head % 2
            mine = (wide_lane >= HEAD) == (odd == 1)
            query = q_ref[0, head // 2, times, :]
            grad = grads[head // 2, times, :]
            log_total = lse_ref[0, head, :, times]
            dot = dots[head]
            for low in range(0, end, CHUNK):
                rows = slice(low, low + CHUNK)
                score = nt(keys[odd, rows, :], query)
                seen = visible(first, low, low + CHUNK, start, low >= start)
                prob = jnp.where(seen, jnp.exp(score - log_total), 0.0)
                d_prob = nt(vals[odd, rows, :], grad)
                weights[rows, :] = prob.astype(BF16)
                d_scores[rows, :] = (prob * (d_prob - dot)).astype(BF16)
            grad_own = jnp.where(mine, grad, jnp.zeros_like(grad))
            query_own = jnp.where(mine, query, jnp.zeros_like(query))
            acc_v[:end, :] += nn(weights[:end, :], grad_own)
            acc_k[:end, :] += nn(d_scores[:end, :], query_own)
            turned_out[head] = nn(keys_t[:, :end], d_scores[:end, :])
            return carry

        lax.fori_loop(0, 2 * pairs, one_head, 0)
        done = turned_out[...].reshape(2 * pairs * HEAD, ROWS).T
        cosine, sine = cos_ref[0, times, :], sin_ref[0, times, :]
        for pair in range(pairs):
            tile = done[:, pair * LANES : (pair + 1) * LANES] * scale
            tile = tile * cosine - turned(tile) * sine
            result[times, pair * LANES : (pair + 1) * LANES] = tile.astype(BF16)

    for one in range(blocks):
        rows = slice(one * here, (one + 1) * here)
        cosine, sine = cos_ref[0, rows, :], sin_ref[0, rows, :]
        d_key, d_value = acc_k[rows, :], acc_v[rows, :]
        d_key = d_key + pltpu.roll(d_key, HEAD, 1)
        d_value = d_value + pltpu.roll(d_value, HEAD, 1)
        d_key = d_key * cosine - turned(d_key) * sine
        result[rows, pairs * LANES :] = jnp.where(low_half, d_key, d_value).astype(BF16)
    for one in range(blocks):
        raw_refs[one][0] = result[pl.ds(pl.multiple_of((one ^ me) * here, here), here), :]


def whole_of(shape):
    rest = tuple(shape[1:])
    return pl.BlockSpec((1,) + rest, lambda b, me: (b,) + (0,) * len(rest))


def attend(me, raw, cosine, sine, first):
    blocks = len(raw)
    seqs, here, width = raw[0].shape
    length = blocks * here
    pairs = width // LANES - 1
    mine = 2 * pairs * HEAD
    shapes = [jax.ShapeDtypeStruct((seqs, here, mine), BF16)] * blocks + [
        jax.ShapeDtypeStruct((seqs, length, mine), BF16),
        jax.ShapeDtypeStruct((seqs, pairs, length, LANES), BF16),
        jax.ShapeDtypeStruct((seqs, length, LANES), BF16),
        jax.ShapeDtypeStruct((seqs, 2 * pairs, 1, length), F32),
    ]
    inputs = (*raw, cosine, sine, first)
    out = pl.pallas_call(
        functools.partial(attend_kernel, blocks),
        out_shape=shapes,
        grid_spec=pltpu.PrefetchScalarGridSpec(
            num_scalar_prefetch=1,
            grid=(seqs,),
            in_specs=[whole_of(one.shape) for one in inputs],
            out_specs=[whole_of(one.shape) for one in shapes],
            scratch_shapes=[
                pltpu.VMEM((2, length, LANES), BF16),
                pltpu.VMEM((HEAD, length), BF16),
                pltpu.VMEM((length, ROWS), F32),
                pltpu.VMEM((length, ROWS), BF16),
                pltpu.VMEM((2 * pairs, HEAD, ROWS), F32),
            ],
        ),
        compiler_params=params(),
        cost_estimate=LIGHT,
        name="attend",
    )(me, *inputs)
    return list(out[:blocks]), list(out[blocks:])


def attend_back(me, grads, kept, queries, keys_values, lse, cosine, sine, first):
    blocks = len(grads)
    seqs, here, mine = grads[0].shape
    length = blocks * here
    pairs = queries.shape[1]
    shapes = [jax.ShapeDtypeStruct((seqs, here, mine + LANES), BF16)] * blocks
    inputs = (*grads, kept, queries, keys_values, lse, cosine, sine, first)
    return pl.pallas_call(
        functools.partial(attend_back_kernel, blocks),
        out_shape=shapes,
        grid_spec=pltpu.PrefetchScalarGridSpec(
            num_scalar_prefetch=1,
            grid=(seqs,),
            in_specs=[whole_of(one.shape) for one in inputs],
            out_specs=[whole_of(one.shape) for one in shapes],
            scratch_shapes=[
                pltpu.VMEM((2, length, LANES), BF16),
                pltpu.VMEM((2, length, LANES), BF16),
                pltpu.VMEM((HEAD, length), BF16),
                pltpu.VMEM((pairs, length, LANES), BF16),
                pltpu.VMEM((length, ROWS), BF16),
                pltpu.VMEM((length, ROWS), BF16),
                pltpu.VMEM((2 * pairs, 1, ROWS), F32),
                pltpu.VMEM((2 * pairs, HEAD, ROWS), F32),
                pltpu.VMEM((length, LANES), F32),
                pltpu.VMEM((length, LANES), F32),
                pltpu.VMEM((length, mine + LANES), BF16),
            ],
        ),
        compiler_params=params(),
        cost_estimate=LIGHT,
        name="attend_back",
    )(me, *inputs)


def rotary(doc_ids):
    length = doc_ids.shape[1]
    places = jnp.broadcast_to(jnp.arange(length, dtype=jnp.int32)[None], doc_ids.shape)
    before = jnp.concatenate([doc_ids[:, :1] - 1, doc_ids[:, :-1]], axis=1)
    first = lax.cummax(jnp.where(doc_ids != before, places, 0), axis=1)
    offsets = (places - first).astype(F32)
    frequency = ROPE_BASE ** (-2.0 * jnp.arange(HEAD // 2, dtype=F32) / HEAD)
    angles = offsets[..., None] * frequency
    cosine, sine = jnp.cos(angles), jnp.sin(angles)
    return (
        jnp.concatenate([cosine] * 4, axis=-1),
        jnp.concatenate([-sine, sine, -sine, sine], axis=-1),
        first[:, None, :],
    )


def norm_back(grad_normed, normed, inverse):
    return inverse * (grad_normed - normed * jnp.mean(grad_normed * normed, axis=-1, keepdims=True))


def normalize(values):
    inverse = lax.rsqrt(jnp.mean(values * values, axis=-1, keepdims=True) + EPSILON)
    return values * inverse, inverse


def on_device(
    inputs, segment_ids, attn_norm, w_query, w_key, w_value, w_out, ffn_norm, w_gate, w_up, w_down, grad_output
):
    n_dp, n_seq = lax.axis_size("dp"), lax.axis_size("seq")
    me = lax.axis_index("seq")
    seqs, here, width = inputs.shape
    tokens = seqs * here
    owned = w_query.shape[0]
    group = n_seq // KV_HEADS
    own_heads = HEADS // n_seq
    units_here = w_down.shape[0]
    units = units_here * n_dp
    me_array = me.reshape(1).astype(jnp.int32)

    mine = own_heads * HEAD

    def per_kv_head(weight):
        return jnp.repeat(weight.reshape(owned, KV_HEADS, HEAD), group, axis=1)

    gains = jnp.pad(jnp.concatenate([attn_norm, ffn_norm]), (0, mine + LANES - 2 * owned))
    ids = segment_ids.astype(BF16).reshape(seqs, here)
    ids = jnp.pad(ids, ((0, 0), (0, mine + LANES - here)))
    extra = jnp.pad(jnp.concatenate([gains[None], ids]), ((0, 15 - seqs), (0, 0)))
    qkv_blocks = jnp.concatenate(
        [
            w_query.reshape(owned, n_seq, own_heads * HEAD),
            per_kv_head(w_key),
            per_kv_head(w_value),
        ],
        axis=2,
    ).transpose(1, 0, 2)
    qkv_blocks = jnp.concatenate(
        [qkv_blocks, jnp.broadcast_to(extra, (n_seq,) + extra.shape)], axis=1
    )

    def unit_blocks(weight):
        blocks = weight.reshape(owned, n_dp, n_seq, units_here).transpose(2, 0, 1, 3)
        blocks = blocks.reshape(n_seq, owned, units)
        return jnp.pad(blocks, ((0, 0), (0, 0), (0, padded(units) - units)))

    def as_rows(received):
        return received.reshape(received.shape[0] * received.shape[1], received.shape[2])

    pairs = [0, n_seq - 2] + list(range(2, n_seq - 2, 2))

    def by_pairs(function, *lists):
        results = None
        for pair in pairs:
            found = function(*[one[pair : pair + 2] for one in lists])
            results = results or [[None] * n_seq for _ in found]
            for target, pieces in zip(results, found):
                target[pair : pair + 2] = pieces
        return results

    def in_sequences(blocks):
        return [one.reshape(seqs, here, one.shape[-1]) for one in blocks]

    def in_rows(blocks):
        return [one.reshape(tokens, one.shape[-1]) for one in blocks]

    block = inputs.reshape(tokens, width)
    upstream = grad_output.reshape(tokens, width)
    w_down_here = lax.all_gather(w_down, "dp", axis=0, tiled=True)
    qkv_rows = exchange_seq(qkv_blocks)
    doc_all = qkv_rows[:, owned + 1 : owned + 1 + seqs, :here].astype(jnp.int32)
    doc_all = doc_all.transpose(1, 0, 2).reshape(seqs, n_seq * here)
    qkv_rows = as_rows(qkv_rows)
    out_rows = deal(w_out)
    inputs_first = gather_seq_first(block)
    qkv_rows, doc_all, out_rows, inputs_first = tie(qkv_rows, doc_all, out_rows, inputs_first)
    w_qkv = gather_dp_rest(qkv_rows, gather_dp_first(qkv_rows), 0)
    inputs_all = gather_seq_rest(block, inputs_first)
    both_blocks = interleave(unit_blocks(w_gate), unit_blocks(w_up))
    cosine, sine, first = rotary(doc_all)
    w_qkv, inputs_all, both_blocks, cosine, sine, first = tie(
        w_qkv, inputs_all, both_blocks, cosine, sine, first
    )

    both_rows = as_rows(exchange_seq(both_blocks))
    w_both = lax.all_gather(both_rows, "dp", axis=0, tiled=True)
    w_out_here = gather_dp_rest(out_rows, gather_dp_first(out_rows), 1).reshape(mine, width)
    w_qkv = w_qkv.reshape(n_dp * n_seq, owned + 16, mine + LANES)
    gain_one = w_qkv[:, owned, :owned].reshape(1, width).astype(F32)
    gain_two = w_qkv[:, owned, owned : 2 * owned].reshape(1, width).astype(F32)
    w_qkv = w_qkv[:, :owned].reshape(width, mine + LANES)
    acts_one, raw = by_pairs(lambda blocks: enter(blocks, gain_one, w_qkv), inputs_all)
    mixed, saved = attend(me_array, in_sequences(raw), cosine, sine, first)
    mixed, saved, both_rows, w_out_here = tie(mixed, saved, both_rows, w_out_here)
    mixed = in_rows(mixed)

    state = block.astype(F32)
    (out_terms,) = by_pairs(lambda blocks: (multiply(blocks, w_out_here),), mixed)
    out_first = scatter_seq_first(out_terms)
    residual = state + scatter_seq_rest(out_first)
    normed_two, inverse_two = normalize(residual)
    acts_two = (normed_two * gain_two).astype(BF16)
    grads_first = gather_seq_first(upstream)
    residual, acts_two, grads_first = tie(residual, acts_two, grads_first)

    w_down_here = jnp.pad(w_down_here, ((0, padded(units) - units), (0, 0)))
    acts_all = gather_seq(acts_two)
    grads_all = gather_seq_rest(upstream, grads_first)
    n_terms, f_terms, hidden, d_both = by_pairs(
        lambda acts, grads: ffn(acts, grads, w_both, w_down_here), acts_all, grads_all
    )
    n_first = scatter_seq_first(n_terms)
    n_first, f_terms, hidden, d_both = tie(n_first, f_terms, hidden, d_both)
    both_term = outer(acts_all, d_both, True, 512)
    both_sum = lax.psum_scatter(both_term, "dp", scatter_dimension=0, tiled=True)
    down_term = outer(hidden, grads_all, False, 512)[:units]
    grad_down = lax.psum_scatter(down_term, "dp", scatter_dimension=0, tiled=True).astype(F32)
    grad_normed = scatter_seq_rest(n_first) * gain_two
    normed_two, inverse_two = normalize(residual)
    grad_res = upstream.astype(F32) + norm_back(grad_normed, normed_two, inverse_two)
    grad_res_low = grad_res.astype(BF16)
    grad_res, grad_res_low, both_term, down_term = tie(grad_res, grad_res_low, both_term, down_term)

    res_first = gather_seq_first(grad_res_low)
    f_first = scatter_seq_first(f_terms)
    res_all = gather_seq_rest(grad_res_low, res_first)
    (d_heads,) = by_pairs(lambda blocks: (multiply(blocks, w_out_here, True),), res_all)
    d_heads, f_first = tie(d_heads, f_first)
    d_raw = attend_back(me_array, in_sequences(d_heads), *saved, cosine, sine, first)
    out_term = outer(mixed, res_all, False, 512).reshape(n_dp, owned, width)
    output = (residual + scatter_seq_rest(f_first)).astype(BF16)
    d_raw, out_term, output = tie(d_raw, out_term, output)
    d_raw = in_rows(d_raw)
    (normed_terms,) = by_pairs(lambda blocks: (multiply(blocks, w_qkv, True),), d_raw)
    normed_first = scatter_seq_first(normed_terms)
    qkv_term = outer(acts_one, d_raw, True, 512).reshape(n_dp, n_seq * owned, mine + LANES)
    qkv_first = scatter_dp_first(qkv_term, 0)
    out_sum = scatter_dp_rest(out_term, scatter_dp_first(out_term, 1), 1)
    normed_first, qkv_first, out_sum = tie(normed_first, qkv_first, out_sum)
    qkv_sum = scatter_dp_rest(qkv_term, qkv_first, 0)
    grad_out = deal(out_sum, back=True).astype(F32)
    grad_normed = scatter_seq_rest(normed_first) * gain_one
    normed_one, inverse_one = normalize(state)
    grad_input = grad_res + norm_back(grad_normed, normed_one, inverse_one)

    def rows_here(total):
        return exchange_seq(total.reshape(n_seq, owned, total.shape[1])).astype(F32)

    def unit_columns(blocks):
        blocks = blocks[..., :units].reshape(n_seq, owned, n_dp, units_here).transpose(1, 2, 0, 3)
        return blocks.reshape(owned, n_dp * n_seq * units_here)

    raw_gate, raw_up = (unit_columns(one) for one in separate(rows_here(both_sum)))
    qkv_rows = rows_here(qkv_sum)

    def kv_columns(blocks):
        blocks = blocks.reshape(KV_HEADS, group, owned, HEAD).sum(axis=1)
        return blocks.transpose(1, 0, 2).reshape(owned, KV_HEADS * HEAD)

    raw_query = qkv_rows[:, :, :mine].transpose(1, 0, 2).reshape(owned, n_seq * mine)
    raw_key = kv_columns(qkv_rows[:, :, mine : mine + HEAD])
    raw_value = kv_columns(qkv_rows[:, :, mine + HEAD :])

    def gain_grad(gain, *pairs):
        total = sum(jnp.sum(weight.astype(F32) * grad, axis=1) for weight, grad in pairs)
        return total / gain.astype(F32)

    return (
        output.reshape(seqs, here, width),
        grad_input.reshape(seqs, here, width),
        gain_grad(attn_norm, (w_query, raw_query), (w_key, raw_key), (w_value, raw_value)),
        raw_query,
        raw_key,
        raw_value,
        grad_out,
        gain_grad(ffn_norm, (w_gate, raw_gate), (w_up, raw_up)),
        raw_gate,
        raw_up,
        grad_down,
    )


def solution(mesh):
    rows = P(("dp", "seq"))
    matrix = P(("dp", "seq"), None)
    tokens = P("dp", "seq", None)
    in_specs = (
        tokens, P("dp", "seq"), rows, matrix, matrix, matrix, matrix, rows, matrix, matrix, matrix, tokens,
    )
    out_specs = (tokens, tokens, rows, matrix, matrix, matrix, matrix, rows, matrix, matrix, matrix)
    return jax.shard_map(
        on_device, mesh=mesh, in_specs=in_specs, out_specs=out_specs, check_vma=False
    )
```

time: 3200 us -> 744 us (0.23)
  waiting for transfers between devices: 2610 us -> 241 us
  matrix products: 295 us -> 0 us
  Pallas kernels: 0 us -> 229 us
  starting transfers between devices: 1.57 us -> 119 us
  blocking collectives: 89.1 us -> 0 us
  local copies, waits for them, and re-layouts: 121 us -> 61.5 us
    reduce_scatter x9 -> x2, waiting for transfers between devices: 2040 us -> 0.01 us  [the longest x1 0.01 us: on_device(): lax.psum_scatter(down_term, 'dp', scatter_dimension=0, tiled=True)]
    all_gather x9 -> x2, waiting for transfers between devices: 567 us -> 0.01 us  [the longest x1 0.01 us: on_device(): w_down_here = lax.all_gather(w_down, 'dp', axis=0, tiled=True)]
    dot_general x49 -> x0, matrix products: 295 us -> none  [the longest x7 79.3 us: outer_rows(): lax.dot_general(left, right, (((0,), (0,)), ((), ())), preferred_element_...]
    pallas_call x0 -> x26, Pallas kernels: none -> 229 us  [the longest x4 70.4 us: ffn(): pl.pallas_call(functools.partial(ffn_kernel, count), out_shape=shapes, co...]
    ppermute x0 -> x82, waiting for transfers between devices: none -> 223 us  [the longest x64 135 us: swap(): return lax.ppermute(block, 'seq', [(i, i ^ distance) for i in range(size)])]
    ppermute x0 -> x82, starting transfers between devices: none -> 99 us  [the longest x64 72.9 us: swap(): return lax.ppermute(block, 'seq', [(i, i ^ distance) for i in range(size)])]
    unnamed x2 -> x0, blocking collectives: 78.8 us -> none
    dynamic_update_slice x8 -> x6, local copies, waits for them, and re-layouts: 46.9 us -> 3.17 us  [put(): lax.dynamic_update_slice(whole, piece[None], ((me + distance) % size, off...]
  transfers between devices with their start and end apart: 18 -> 90, of which waited for: 16 -> 29; matrix products, arithmetic and copies ran while one was open for 9% -> 13% of each run, Pallas kernels for 0% -> 30%
where the time goes in v1:
time: 744 us; the launch traced here: 732 us
  waiting for transfers between devices  241 us (32%)
  Pallas kernels  229 us (31%)
  starting transfers between devices  119 us (16%)
  other arithmetic  66.5 us (9%)
  local copies, waits for them, and re-layouts  61.5 us (8%)
  between operations  15.4 us (2%)
    ppermute x64, waiting for transfers between devices, swap(): return lax.ppermute(block, 'seq', [(i, i ^ distance) for i in range(size)])  135 us
    ppermute x16, waiting for transfers between devices, shift(): lax.ppermute(block, 'dp', [(i, (i + step) % size) for i in range(size)])  88.5 us
    ppermute x64, starting transfers between devices, swap(): return lax.ppermute(block, 'seq', [(i, i ^ distance) for i in range(size)])  72.9 us
    pallas_call x4, Pallas kernels, ffn(): pl.pallas_call(functools.partial(ffn_kernel, count), out_shape=shapes, co...  70.4 us
    pallas_call x4, Pallas kernels, outer(): pl.pallas_call(functools.partial(outer_kernel, count, along_left), out_sh...  45.8 us
    pallas_call x12, Pallas kernels, multiply(): pl.pallas_call(functools.partial(multiply_kernel, len(lefts), transposed)...  41.6 us
    pallas_call x1, Pallas kernels, attend_back(): pl.pallas_call(functools.partial(attend_back_kernel, blocks), out_shape=s...  28.9 us
    pallas_call x1, Pallas kernels, attend(): pl.pallas_call(functools.partial(attend_kernel, blocks), out_shape=shapes...  23.6 us
  transfers between devices with their start and end apart: 90, of which 29 were waited for; matrix products, arithmetic and copies ran while one was open for 13% of the time, Pallas kernels for 30%

profile of v1, /device:TPU:1, one launch (start us, length us, event | category | flops | bytes accessed | tf_op | source)
XLA Modules:
  0.0 731.6 jit_solution(10335623229455024410)
XLA Ops:
  16.6 4.0 all-to-all-start
  35.2 9.4 %all-to-all-done = bf16[8,80,384]{2,1,0:T(8,128)(2,1)S(1)} async-done(((bf16[8,80,384]{2,1,0:T(8,128)(2,1)}), bf16[8,80,384]{2,1,0:T(8,128)(2,1)S(1)}, u32[]{:S(2)}, u32[]{:S(2)}) %all-to-all-start) | async-done | bytes 491552 | tf_op jit(solution)/shard_map/all_to_all | solution.py:88
  54.7 14.2 %collective-permute-start.10 = (bf16[128,2048]{1,0:T(8,128)(2,1)S(1)}, bf16[128,2048]{1,0:T(8,128)(2,1)S(1)}, u32[]{:S(2)}, u32[]{:S(2)}) collective-permute-start(bf16[128,2048]{1,0:T(8,128)(2,1)S(1)} %slice.246), channel_id=1, source_target_pairs={{0,2},{1,3},{2,0},{3,1},{4,6},{5,7},{6,4},{7,5},{8,10},{9,11},{10,... | collective-permute-start | bytes 1572872 | tf_op jit(solution)/shard_map/ppermute | solution.py:30
  85.2 23.9 %collective-permute-done.5 = bf16[640,384]{1,0:T(8,128)(2,1)S(1)} collective-permute-done((bf16[640,384]{1,0:T(8,128)(2,1)S(1)}, bf16[640,384]{1,0:T(8,128)(2,1)S(1)}, u32[]{:S(2)}, u32[]{:S(2)}) %collective-permute-start.5) | collective-permute-done | bytes 491552 | tf_op jit(solution)/shard_map/ppermute | solution.py:35
  109.2 4.9 collective-permute-done.4
  114.4 14.5 %collective-permute-done.7 = bf16[320,384]{1,0:T(8,128)(2,1)S(1)} collective-permute-done((bf16[320,384]{1,0:T(8,128)(2,1)S(1)}, bf16[320,384]{1,0:T(8,128)(2,1)S(1)}, u32[]{:S(2)}, u32[]{:S(2)}) %collective-permute-start.7) | collective-permute-done | bytes 245792 | tf_op jit(solution)/shard_map/ppermute | solution.py:35
  132.7 5.2 all-to-all-start.1
  142.5 4.5 enter.7
  147.0 4.6 enter.6
  151.6 4.6 enter.5
  156.2 4.5 enter.4
  160.7 23.6 %attend.1 = (bf16[2,128,256]{2,1,0:T(8,128)(2,1)}, bf16[2,128,256]{2,1,0:T(8,128)(2,1)}, bf16[2,128,256]{2,1,0:T(8,128)(2,1)}, bf16[2,128,256]{2,1,0:T(8,128)(2,...) custom-call(s32[1]{0:T(128)} %bitcast.me_ref, ...), custom_call_target="tpu_custom_call" | custom-call | flops 1 | bytes 1 | tf_op jit(solution)/shard_map/attend/pallas_call | solution.py:553
  202.8 6.3 collective-permute-done.20
  218.8 18.1 %collective-permute-done.21 = bf16[256,2048]{1,0:T(8,128)(2,1)} collective-permute-done((bf16[256,2048]{1,0:T(8,128)(2,1)S(1)}, bf16[256,2048]{1,0:T(8,128)(2,1)}, u32[]{:S(2)}, u32[]{:S(2)}) %collective-permute-start.21) | collective-permute-done | bytes 1048608 | tf_op jit(solution)/shard_map/ppermute | solution.py:30
  242.6 18.2 %collective-permute-done.26.refs_2_.refs_12_ = bf16[256,2048]{1,0:T(8,128)(2,1)} collective-permute-done((bf16[256,2048]{1,0:T(8,128)(2,1)}, bf16[256,2048]{1,0:T(8,128)(2,1)}, u32[]{:S(2)}, u32[]{:S(2)}) %collective-permute-start.26) | collective-permute-done | bytes 1048608 | tf_op jit(solution)/shard_map/ppermute | solution.py:30
  266.1 17.7 %collective-permute-done.34.refs_0_.refs_4_ = bf16[256,2048]{1,0:T(8,128)(2,1)} collective-permute-done((bf16[256,2048]{1,0:T(8,128)(2,1)}, bf16[256,2048]{1,0:T(8,128)(2,1)}, u32[]{:S(2)}, u32[]{:S(2)}) %collective-permute-start.34) | collective-permute-done | bytes 1048608 | tf_op jit(solution)/shard_map/ppermute | solution.py:30
  287.3 8.5 %collective-permute-done.41 = bf16[128,2048]{1,0:T(8,128)(2,1)S(1)} collective-permute-done((bf16[128,2048]{1,0:T(8,128)(2,1)S(1)}, bf16[128,2048]{1,0:T(8,128)(2,1)S(1)}, u32[]{:S(2)}, u32[]{:S(2)}) %collective-permute-start.41) | collective-permute-done | bytes 524320 | tf_op jit(solution)/shard_map/ppermute | solution.py:30
  296.9 5.6 collective-permute-start.43
  302.5 4.5 collective-permute-done.38
  314.6 17.5 %ffn.7 = (bf16[256,2048]{1,0:T(8,128)(2,1)}, bf16[256,2048]{1,0:T(8,128)(2,1)}, bf16[256,2048]{1,0:T(8,128)(2,1)}, bf16[256,2048]{1,0:T(8,128)(2,1)}, bf16[256,7...) custom-call(bf16[256,2048]{1,0:T(8,128)(2,1)} %copy-done.5, ...), custom_call_target="tpu_custom_call" | custom-call | flops 1 | bytes 1 | tf_op jit(solution)/shard_map/ffn/pallas_call | solution.py:266
  332.3 17.6 %ffn.4 = (bf16[256,2048]{1,0:T(8,128)(2,1)}, bf16[256,2048]{1,0:T(8,128)(2,1)}, bf16[256,2048]{1,0:T(8,128)(2,1)}, bf16[256,2048]{1,0:T(8,128)(2,1)}, bf16[256,7...) custom-call(bf16[256,2048]{1,0:T(8,128)(2,1)} %multiply_convert_fusion.refs_0_, ...), custom_call_target="tpu_custom_call" | custom-call | flops 1 | bytes 1 | tf_op jit(solution)/shard_map/ffn/pallas_call | solution.py:266
  350.3 17.5 %ffn.5 = (bf16[256,2048]{1,0:T(8,128)(2,1)}, bf16[256,2048]{1,0:T(8,128)(2,1)}, bf16[256,2048]{1,0:T(8,128)(2,1)}, bf16[256,2048]{1,0:T(8,128)(2,1)}, bf16[256,7...) custom-call(bf16[256,2048]{1,0:T(8,128)(2,1)} %collective-permute-done.30.refs, ...), custom_call_target="tpu_custom_call" | custom-call | flops 1 | bytes 1 | tf_op jit(solution)/shard_map/ffn/pallas_call | solution.py:266
  368.0 17.9 %ffn.6 = (bf16[256,2048]{1,0:T(8,128)(2,1)}, bf16[256,2048]{1,0:T(8,128)(2,1)}, bf16[256,2048]{1,0:T(8,128)(2,1)}, bf16[256,2048]{1,0:T(8,128)(2,1)}, bf16[256,7...) custom-call(bf16[256,2048]{1,0:T(8,128)(2,1)} %collective-permute-done.34.refs, ...), custom_call_target="tpu_custom_call" | custom-call | flops 1 | bytes 1 | tf_op jit(solution)/shard_map/ffn/pallas_call | solution.py:266
  392.4 7.8 %collective-permute-done.46 = bf16[128,2048]{1,0:T(8,128)(2,1)} collective-permute-done((bf16[128,2048]{1,0:T(8,128)(2,1)S(1)}, bf16[128,2048]{1,0:T(8,128)(2,1)}, u32[]{:S(2)}, u32[]{:S(2)}) %collective-permute-start.46) | collective-permute-done | bytes 524320 | tf_op jit(solution)/shard_map/ppermute | solution.py:30
  400.4 10.8 %outer.5 = bf16[704,2048]{1,0:T(8,128)(2,1)} custom-call(bf16[256,704]{1,0:T(8,128)(2,1)} %get-tuple-element.308.refs_0_, bf16[256,704]{1,0:T(8,128)(2,1)} %get-tuple-element.309.refs_1_, bf16[256,704]{1,0:T(8,128)(2,1)} %get-tuple-element.310.refs_2_, bf16[256,704]{1,0:T(8,128)(2,1)} %get-tuple-element.311.refs_3_, ...), custom_call_target="tpu_custom_call" | custom-call | flops 1 | bytes 1 | tf_op jit(solution)/shard_map/outer/pallas_call | solution.py:306
  418.0 19.0 %outer.4 = bf16[2048,1408]{1,0:T(8,128)(2,1)} custom-call(bf16[256,2048]{1,0:T(8,128)(2,1)} %multiply_convert_fusion.refs_0_, bf16[256,2048]{1,0:T(8,128)(2,1)} %collective-permute-done.28.refs_1_, bf16[256,2048]{1,0:T(8,128)(2,1)} %collective-permute-done.30.refs_0_.refs_2_, bf16[256,2048]{1,0:T(8,128)(2,1)} %collective-permute-done.31.refs_1_.refs_3_, ...), custom_call_target="tpu_custom_call" | custom-call | flops 1 | bytes 1 | tf_op jit(solution)/shard_map/outer/pallas_call | solution.py:306
  443.2 4.7 fusion.22
  452.7 17.6 %collective-permute-done.52.refs_0_.refs_12_ = bf16[256,2048]{1,0:T(8,128)(2,1)} collective-permute-done((bf16[256,2048]{1,0:T(8,128)(2,1)}, bf16[256,2048]{1,0:T(8,128)(2,1)}, u32[]{:S(2)}, u32[]{:S(2)}) %collective-permute-start.52) | collective-permute-done | bytes 1048608 | tf_op jit(solution)/shard_map/ppermute | solution.py:30
  471.9 3.8 collective-permute-start.60
  481.5 4.3 collective-permute-start.59
  485.8 4.9 collective-permute-done.55
  518.1 28.9 %attend_back.1 = (bf16[2,128,384]{2,1,0:T(8,128)(2,1)}, bf16[2,128,384]{2,1,0:T(8,128)(2,1)}, bf16[2,128,384]{2,1,0:T(8,128)(2,1)}, bf16[2,128,384]{2,1,0:T(8,12...) custom-call(s32[1]{0:T(128)} %bitcast.me_ref, ...), custom_call_target="tpu_custom_call" | custom-call | flops 1 | bytes 1 | tf_op jit(solution)/shard_map/attend_back/pallas_call | solution.py:583
  547.0 7.2 outer.6
  558.8 3.9 multiply.61
  564.7 3.9 multiply.60
  569.0 3.9 multiply.58
  573.0 4.0 multiply.59
  577.0 8.8 %outer.7 = bf16[2048,384]{1,0:T(8,128)(2,1)} custom-call(bf16[256,2048]{1,0:T(8,128)(2,1)} %get-tuple-element.376.refs_0_, bf16[256,2048]{1,0:T(8,128)(2,1)} %get-tuple-element.377.refs_1_, bf16[256,2048]{1,0:T(8,128)(2,1)} %get-tuple-element.378.refs_2_, bf16[256,2048]{1,0:T(8,128)(2,1)} %get-tuple-element.379.refs_3_, ...), custom_call_target="tpu_custom_call" | custom-call | flops 1 | bytes 1 | tf_op jit(solution)/shard_map/outer/pallas_call | solution.py:306
  590.4 4.9 collective-permute-done.76
  596.1 5.6 collective-permute-done.74
  609.0 4.7 collective-permute-done.72
  614.5 4.3 collective-permute-start.81
  622.6 30.1 %collective-permute-done.80 = bf16[512,384]{1,0:T(8,128)(2,1)S(1)} collective-permute-done((bf16[512,384]{1,0:T(8,128)(2,1)S(1)}, bf16[512,384]{1,0:T(8,128)(2,1)S(1)}, u32[]{:S(2)}, u32[]{:S(2)}) %collective-permute-start.80) | collective-permute-done | bytes 393248 | tf_op jit(solution)/shard_map/ppermute | solution.py:35
  653.5 4.7 all-to-all-start.2
  668.0 4.8 all-to-all-start.3
  674.0 13.3 %collective-permute-done.77 = bf16[256,2048]{1,0:T(8,128)(2,1)} collective-permute-done((bf16[256,2048]{1,0:T(8,128)(2,1)}, bf16[256,2048]{1,0:T(8,128)(2,1)}, u32[]{:S(2)}, u32[]{:S(2)}) %collective-permute-start.77) | collective-permute-done | bytes 1048608 | tf_op jit(solution)/shard_map/ppermute | solution.py:30
  689.7 3.9 fusion.5
  693.6 7.4 %all-to-all-done.3 = bf16[8,64,1408]{2,1,0:T(8,128)(2,1)S(1)} async-done(((bf16[8,64,1408]{2,1,0:T(8,128)(2,1)}), bf16[8,64,1408]{2,1,0:T(8,128)(2,1)S(1)}, u32[]{:S(2)}, u32[]{:S(2)}) %all-to-all-start.3) | async-done | bytes 1441824 | tf_op jit(solution)/shard_map/all_to_all | solution.py:88
  (436 shorter events, 231.9 us)
Async XLA Ops:
  7.2 37.5 %collective-permute-start.3 = (bf16[256,2048]{1,0:T(8,128)(2,1)}, bf16[256,2048]{1,0:T(8,128)(2,1)}, u32[]{:S(2)}, u32[]{:S(2)}) collective-permute-start(bf16[256,2048]{1,0:T(8,128)(2,1)} %bitcast.167), channel_id=1, source_target_pairs={{0,1},{1,0},{2,3},{3,2},{4,5},{5,4},{6,7},{7,6},{8,9},{9,8},{10,11... | collective-permute-start | bytes 3145736 | tf_op jit(solution)/shard_map/ppermute | solution.py:30
  7.3 37.3 %collective-permute-start.2 = (bf16[256,2048]{1,0:T(8,128)(2,1)}, bf16[256,2048]{1,0:T(8,128)(2,1)}, u32[]{:S(2)}, u32[]{:S(2)}) collective-permute-start(bf16[256,2048]{1,0:T(8,128)(2,1)} %bitcast.168), channel_id=1, source_target_pairs={{0,4},{1,5},{2,6},{3,7},{4,0},{5,1},{6,2},{7,3},{8,12},{9,13},{10,... | collective-permute-start | bytes 3145736 | tf_op jit(solution)/shard_map/ppermute | solution.py:30
  10.0 34.7 %collective-permute-start.1 = (bf16[256,2048]{1,0:T(8,128)(2,1)}, bf16[256,2048]{1,0:T(8,128)(2,1)}, u32[]{:S(2)}, u32[]{:S(2)}) collective-permute-start(bf16[256,2048]{1,0:T(8,128)(2,1)} %bitcast.169), channel_id=1, source_target_pairs={{0,2},{1,3},{2,0},{3,1},{4,6},{5,7},{6,4},{7,5},{8,10},{9,11},{10,... | collective-permute-start | bytes 3145736 | tf_op jit(solution)/shard_map/ppermute | solution.py:30
  16.6 28.0 %all-to-all-start = ((bf16[8,80,384]{2,1,0:T(8,128)(2,1)}), bf16[8,80,384]{2,1,0:T(8,128)(2,1)S(1)}, u32[]{:S(2)}, u32[]{:S(2)}) async-start(bf16[8,80,384]{2,1,0:T(8,128)(2,1)} %copy.58), calls=%async_computation | async-start | bytes 983040 | tf_op jit(solution)/shard_map/all_to_all | solution.py:88
  20.7 293.9 %all-gather.5.cloned.1.call-start = ((), (), s32[]{:S(2)}) async-start(), calls=%async_computation.7 | async-start | bytes 3604480 | tf_op jit(solution)/shard_map/all_gather | solution.py:698
  44.7 35.7 %collective-permute-start.14 = (bf16[64,2048]{1,0:T(8,128)(2,1)}, bf16[64,2048]{1,0:T(8,128)(2,1)}, u32[]{:S(2)}, u32[]{:S(2)}) collective-permute-start(bf16[64,2048]{1,0:T(8,128)(2,1)} %collective-permute-done), channel_id=1, source_target_pairs={{0,24},{8,0},{16,8},{24,16},{1,25},{9,1},{17,9},{25,17},{2,26},{10... | collective-permute-start | bytes 786440 | tf_op jit(solution)/shard_map/ppermute | solution.py:35
  47.9 33.0 %collective-permute-start.13 = (bf16[64,2048]{1,0:T(8,128)(2,1)}, bf16[64,2048]{1,0:T(8,128)(2,1)}, u32[]{:S(2)}, u32[]{:S(2)}) collective-permute-start(bf16[64,2048]{1,0:T(8,128)(2,1)} %collective-permute-done), channel_id=1, source_target_pairs={{0,8},{8,16},{16,24},{24,0},{1,9},{9,17},{17,25},{25,1},{2,10},{10... | collective-permute-start | bytes 786440 | tf_op jit(solution)/shard_map/ppermute | solution.py:35
  49.1 60.1 %collective-permute-start.5 = (bf16[640,384]{1,0:T(8,128)(2,1)S(1)}, bf16[640,384]{1,0:T(8,128)(2,1)S(1)}, u32[]{:S(2)}, u32[]{:S(2)}) collective-permute-start(bf16[640,384]{1,0:T(8,128)(2,1)S(1)} %bitcast.186), channel_id=1, source_target_pairs={{0,24},{8,0},{16,8},{24,16},{1,25},{9,1},{17,9},{25,17},{2,26},{10... | collective-permute-start | bytes 1474568 | tf_op jit(solution)/shard_map/ppermute | solution.py:35
  54.7 23.6 %collective-permute-start.10 = (bf16[128,2048]{1,0:T(8,128)(2,1)S(1)}, bf16[128,2048]{1,0:T(8,128)(2,1)S(1)}, u32[]{:S(2)}, u32[]{:S(2)}) collective-permute-start(bf16[128,2048]{1,0:T(8,128)(2,1)S(1)} %slice.246), channel_id=1, source_target_pairs={{0,2},{1,3},{2,0},{3,1},{4,6},{5,7},{6,4},{7,5},{8,10},{9,11},{10,... | collective-permute-start | bytes 1572872 | tf_op jit(solution)/shard_map/ppermute | solution.py:30
  78.3 35.8 %collective-permute-start.4 = (bf16[640,384]{1,0:T(8,128)(2,1)S(1)}, bf16[640,384]{1,0:T(8,128)(2,1)S(1)}, u32[]{:S(2)}, u32[]{:S(2)}) collective-permute-start(bf16[640,384]{1,0:T(8,128)(2,1)S(1)} %bitcast.188), channel_id=1, source_target_pairs={{0,8},{8,16},{16,24},{24,0},{1,9},{9,17},{17,25},{25,1},{2,10},{10... | collective-permute-start | bytes 1474568 | tf_op jit(solution)/shard_map/ppermute | solution.py:35
  80.3 50.2 %collective-permute-start.8 = (bf16[256,2048]{1,0:T(8,128)(2,1)}, bf16[256,2048]{1,0:T(8,128)(2,1)S(1)}, u32[]{:S(2)}, u32[]{:S(2)}) collective-permute-start(bf16[256,2048]{1,0:T(8,128)(2,1)} %collective-permute-done.1.refs_0_), channel_id=1, source_target_pairs={{0,1},{1,0},{2,3},{3,2},{4,5},{5,4},{6,7},{7,6},{8,9},{9,8},{10,11... | collective-permute-start | bytes 3145736 | tf_op jit(solution)/shard_map/ppermute | solution.py:30
  80.3 50.1 %collective-permute-start.9 = (bf16[256,2048]{1,0:T(8,128)(2,1)}, bf16[256,2048]{1,0:T(8,128)(2,1)S(1)}, u32[]{:S(2)}, u32[]{:S(2)}) collective-permute-start(bf16[256,2048]{1,0:T(8,128)(2,1)} %collective-permute-done.2.refs_0_), channel_id=1, source_target_pairs={{0,1},{1,0},{2,3},{3,2},{4,5},{5,4},{6,7},{7,6},{8,9},{9,8},{10,11... | collective-permute-start | bytes 3145736 | tf_op jit(solution)/shard_map/ppermute | solution.py:30
  80.9 49.6 %collective-permute-start.12 = (bf16[256,2048]{1,0:T(8,128)(2,1)S(1)}, bf16[256,2048]{1,0:T(8,128)(2,1)S(1)}, u32[]{:S(2)}, u32[]{:S(2)}) collective-permute-start(bf16[256,2048]{1,0:T(8,128)(2,1)S(1)} %constant_dynamic-update-slice_fusion.refs_0_), channel_id=1, source_target_pairs={{0,1},{1,0},{2,3},{3,2},{4,5},{5,4},{6,7},{7,6},{8,9},{9,8},{10,11... | collective-permute-start | bytes 3145736 | tf_op jit(solution)/shard_map/ppermute | solution.py:30
  132.7 51.6 %all-to-all-start.1 = ((bf16[8,64,1408]{2,1,0:T(8,128)(2,1)}), bf16[8,64,1408]{2,1,0:T(8,128)(2,1)}, u32[]{:S(2)}, u32[]{:S(2)}) async-start(bf16[8,64,1408]{2,1,0:T(8,128)(2,1)} %concatenate.90), calls=%async_computation.1 | async-start | bytes 2883584 | tf_op jit(solution)/shard_map/all_to_all | solution.py:88
  138.0 176.6 %all-gather.3.cloned.1.call-start = ((), (), s32[]{:S(2)}) async-start(), calls=%async_computation.6 | async-start | bytes 7208960 | tf_op jit(solution)/shard_map/all_gather | solution.py:715
  187.7 473.9 %reduce-scatter.5.cloned.1.call-start = ((), (), s32[]{:S(2)}) async-start(), calls=%async_computation.9 | async-start | bytes 3604480 | tf_op jit(solution)/shard_map/reduce_scatter | solution.py:746
  209.2 27.7 %collective-permute-start.21 = (bf16[256,2048]{1,0:T(8,128)(2,1)S(1)}, bf16[256,2048]{1,0:T(8,128)(2,1)}, u32[]{:S(2)}, u32[]{:S(2)}) collective-permute-start(bf16[256,2048]{1,0:T(8,128)(2,1)S(1)} %pad_maximum_fusion.4), channel_id=1, source_target_pairs={{0,2},{1,3},{2,0},{3,1},{4,6},{5,7},{6,4},{7,5},{8,10},{9,11},{10,... | collective-permute-start | bytes 3145736 | tf_op jit(solution)/shard_map/ppermute | solution.py:30
  214.6 23.7 %collective-permute-start.24 = (bf16[256,2048]{1,0:T(8,128)(2,1)S(1)}, bf16[256,2048]{1,0:T(8,128)(2,1)}, u32[]{:S(2)}, u32[]{:S(2)}) collective-permute-start(bf16[256,2048]{1,0:T(8,128)(2,1)S(1)} %pad_maximum_fusion.5), channel_id=1, source_target_pairs={{0,4},{1,5},{2,6},{3,7},{4,0},{5,1},{6,2},{7,3},{8,12},{9,13},{10,... | collective-permute-start | bytes 3145736 | tf_op jit(solution)/shard_map/ppermute | solution.py:30
  215.5 27.1 %collective-permute-start.27 = (bf16[256,2048]{1,0:T(8,128)(2,1)}, bf16[256,2048]{1,0:T(8,128)(2,1)}, u32[]{:S(2)}, u32[]{:S(2)}) collective-permute-start(bf16[256,2048]{1,0:T(8,128)(2,1)} %bitcast.1.refs_2_.refs_8_), channel_id=1, source_target_pairs={{0,1},{1,0},{2,3},{3,2},{4,5},{5,4},{6,7},{7,6},{8,9},{9,8},{10,11... | collective-permute-start | bytes 3145736 | tf_op jit(solution)/shard_map/ppermute | solution.py:30
  216.6 44.2 %collective-permute-start.26 = (bf16[256,2048]{1,0:T(8,128)(2,1)}, bf16[256,2048]{1,0:T(8,128)(2,1)}, u32[]{:S(2)}, u32[]{:S(2)}) collective-permute-start(bf16[256,2048]{1,0:T(8,128)(2,1)} %bitcast.1.refs_2_.refs_8_), channel_id=1, source_target_pairs={{0,4},{1,5},{2,6},{3,7},{4,0},{5,1},{6,2},{7,3},{8,12},{9,13},{10,... | collective-permute-start | bytes 3145736 | tf_op jit(solution)/shard_map/ppermute | solution.py:30
  217.6 43.2 %collective-permute-start.25 = (bf16[256,2048]{1,0:T(8,128)(2,1)}, bf16[256,2048]{1,0:T(8,128)(2,1)}, u32[]{:S(2)}, u32[]{:S(2)}) collective-permute-start(bf16[256,2048]{1,0:T(8,128)(2,1)} %bitcast.1.refs_2_.refs_8_), channel_id=1, source_target_pairs={{0,2},{1,3},{2,0},{3,1},{4,6},{5,7},{6,4},{7,5},{8,10},{9,11},{10,... | collective-permute-start | bytes 3145736 | tf_op jit(solution)/shard_map/ppermute | solution.py:30
  261.8 24.1 %collective-permute-start.30 = (bf16[256,2048]{1,0:T(8,128)(2,1)}, bf16[256,2048]{1,0:T(8,128)(2,1)}, u32[]{:S(2)}, u32[]{:S(2)}) collective-permute-start(bf16[256,2048]{1,0:T(8,128)(2,1)} %multiply_convert_fusion.refs_0_), channel_id=1, source_target_pairs={{0,2},{1,3},{2,0},{3,1},{4,6},{5,7},{6,4},{7,5},{8,10},{9,11},{10,... | collective-permute-start | bytes 3145736 | tf_op jit(solution)/shard_map/ppermute | solution.py:30
  263.4 32.4 %collective-permute-start.41 = (bf16[128,2048]{1,0:T(8,128)(2,1)S(1)}, bf16[128,2048]{1,0:T(8,128)(2,1)S(1)}, u32[]{:S(2)}, u32[]{:S(2)}) collective-permute-start(bf16[128,2048]{1,0:T(8,128)(2,1)S(1)} %slice.273), channel_id=1, source_target_pairs={{0,2},{1,3},{2,0},{3,1},{4,6},{5,7},{6,4},{7,5},{8,10},{9,11},{10,... | collective-permute-start | bytes 1572872 | tf_op jit(solution)/shard_map/ppermute | solution.py:30
  265.5 30.4 %collective-permute-start.42 = (bf16[128,2048]{1,0:T(8,128)(2,1)S(1)}, bf16[128,2048]{1,0:T(8,128)(2,1)S(1)}, u32[]{:S(2)}, u32[]{:S(2)}) collective-permute-start(bf16[128,2048]{1,0:T(8,128)(2,1)S(1)} %slice.274), channel_id=1, source_target_pairs={{0,4},{1,5},{2,6},{3,7},{4,0},{5,1},{6,2},{7,3},{8,12},{9,13},{10,... | collective-permute-start | bytes 1572872 | tf_op jit(solution)/shard_map/ppermute | solution.py:30
  310.3 39.6 %collective-permute-start.32 = (bf16[256,2048]{1,0:T(8,128)(2,1)}, bf16[256,2048]{1,0:T(8,128)(2,1)}, u32[]{:S(2)}, u32[]{:S(2)}) collective-permute-start(bf16[256,2048]{1,0:T(8,128)(2,1)} %collective-permute-done.25.refs_2_.refs_10_), channel_id=1, source_target_pairs={{0,1},{1,0},{2,3},{3,2},{4,5},{5,4},{6,7},{7,6},{8,9},{9,8},{10,11... | collective-permute-start | bytes 3145736 | tf_op jit(solution)/shard_map/ppermute | solution.py:30
  310.7 39.6 %collective-permute-start.31 = (bf16[256,2048]{1,0:T(8,128)(2,1)}, bf16[256,2048]{1,0:T(8,128)(2,1)}, u32[]{:S(2)}, u32[]{:S(2)}) collective-permute-start(bf16[256,2048]{1,0:T(8,128)(2,1)} %collective-permute-done.30.refs_0_.refs_2_), channel_id=1, source_target_pairs={{0,1},{1,0},{2,3},{3,2},{4,5},{5,4},{6,7},{7,6},{8,9},{9,8},{10,11... | collective-permute-start | bytes 3145736 | tf_op jit(solution)/shard_map/ppermute | solution.py:30
  310.8 57.2 %collective-permute-start.36 = (bf16[256,2048]{1,0:T(8,128)(2,1)}, bf16[256,2048]{1,0:T(8,128)(2,1)}, u32[]{:S(2)}, u32[]{:S(2)}) collective-permute-start(bf16[256,2048]{1,0:T(8,128)(2,1)} %collective-permute-done.26.refs_2_.refs_12_), channel_id=1, source_target_pairs={{0,1},{1,0},{2,3},{3,2},{4,5},{5,4},{6,7},{7,6},{8,9},{9,8},{10,11... | collective-permute-start | bytes 3145736 | tf_op jit(solution)/shard_map/ppermute | solution.py:30
  314.2 53.8 %collective-permute-start.35 = (bf16[256,2048]{1,0:T(8,128)(2,1)}, bf16[256,2048]{1,0:T(8,128)(2,1)}, u32[]{:S(2)}, u32[]{:S(2)}) collective-permute-start(bf16[256,2048]{1,0:T(8,128)(2,1)} %collective-permute-done.34.refs_0_.refs_4_), channel_id=1, source_target_pairs={{0,1},{1,0},{2,3},{3,2},{4,5},{5,4},{6,7},{7,6},{8,9},{9,8},{10,11... | collective-permute-start | bytes 3145736 | tf_op jit(solution)/shard_map/ppermute | solution.py:30
  332.1 54.1 %collective-permute-start.44 = (bf16[256,2048]{1,0:T(8,128)(2,1)}, bf16[256,2048]{1,0:T(8,128)(2,1)S(1)}, u32[]{:S(2)}, u32[]{:S(2)}) collective-permute-start(bf16[256,2048]{1,0:T(8,128)(2,1)} %get-tuple-element.270), channel_id=1, source_target_pairs={{0,1},{1,0},{2,3},{3,2},{4,5},{5,4},{6,7},{7,6},{8,9},{9,8},{10,11... | collective-permute-start | bytes 3145736 | tf_op jit(solution)/shard_map/ppermute | solution.py:30
  349.9 38.4 %collective-permute-start.29 = (bf16[256,2048]{1,0:T(8,128)(2,1)}, bf16[256,2048]{1,0:T(8,128)(2,1)S(1)}, u32[]{:S(2)}, u32[]{:S(2)}) collective-permute-start(bf16[256,2048]{1,0:T(8,128)(2,1)} %get-tuple-element.262), channel_id=1, source_target_pairs={{0,1},{1,0},{2,3},{3,2},{4,5},{5,4},{6,7},{7,6},{8,9},{9,8},{10,11... | collective-permute-start | bytes 3145736 | tf_op jit(solution)/shard_map/ppermute | solution.py:30
  411.2 256.8 %reduce-scatter.3.cloned.1.call-start = ((), (), s32[]{:S(2)}) async-start(), calls=%async_computation.8 | async-start | bytes 7208960 | tf_op jit(solution)/shard_map/reduce_scatter | solution.py:744
  414.1 23.6 %collective-permute-start.48 = (bf16[256,2048]{1,0:T(8,128)(2,1)}, bf16[256,2048]{1,0:T(8,128)(2,1)}, u32[]{:S(2)}, u32[]{:S(2)}) collective-permute-start(bf16[256,2048]{1,0:T(8,128)(2,1)} %pad_maximum_fusion.7), channel_id=1, source_target_pairs={{0,4},{1,5},{2,6},{3,7},{4,0},{5,1},{6,2},{7,3},{8,12},{9,13},{10,... | collective-permute-start | bytes 3145736 | tf_op jit(solution)/shard_map/ppermute | solution.py:30
  417.3 23.3 %collective-permute-start.47 = (bf16[256,2048]{1,0:T(8,128)(2,1)}, bf16[256,2048]{1,0:T(8,128)(2,1)}, u32[]{:S(2)}, u32[]{:S(2)}) collective-permute-start(bf16[256,2048]{1,0:T(8,128)(2,1)} %pad_maximum_fusion.6), channel_id=1, source_target_pairs={{0,2},{1,3},{2,0},{3,1},{4,6},{5,7},{6,4},{7,5},{8,10},{9,11},{10,... | collective-permute-start | bytes 3145736 | tf_op jit(solution)/shard_map/ppermute | solution.py:30
  448.4 27.3 %collective-permute-start.50 = (bf16[256,2048]{1,0:T(8,128)(2,1)}, bf16[256,2048]{1,0:T(8,128)(2,1)}, u32[]{:S(2)}, u32[]{:S(2)}) collective-permute-start(bf16[256,2048]{1,0:T(8,128)(2,1)} %get-tuple-element.316.refs_0_.refs_8_), channel_id=1, source_target_pairs={{0,2},{1,3},{2,0},{3,1},{4,6},{5,7},{6,4},{7,5},{8,10},{9,11},{10,... | collective-permute-start | bytes 3145736 | tf_op jit(solution)/shard_map/ppermute | solution.py:30
  449.4 42.0 %collective-permute-start.57 = (bf16[256,2048]{1,0:T(8,128)(2,1)}, bf16[256,2048]{1,0:T(8,128)(2,1)S(1)}, u32[]{:S(2)}, u32[]{:S(2)}) collective-permute-start(bf16[256,2048]{1,0:T(8,128)(2,1)} %get-tuple-element.326), channel_id=1, source_target_pairs={{0,1},{1,0},{2,3},{3,2},{4,5},{5,4},{6,7},{7,6},{8,9},{9,8},{10,11... | collective-permute-start | bytes 3145736 | tf_op jit(solution)/shard_map/ppermute | solution.py:30
  452.6 38.9 %collective-permute-start.58 = (bf16[256,2048]{1,0:T(8,128)(2,1)}, bf16[256,2048]{1,0:T(8,128)(2,1)S(1)}, u32[]{:S(2)}, u32[]{:S(2)}) collective-permute-start(bf16[256,2048]{1,0:T(8,128)(2,1)} %get-tuple-element.328), channel_id=1, source_target_pairs={{0,1},{1,0},{2,3},{3,2},{4,5},{5,4},{6,7},{7,6},{8,9},{9,8},{10,11... | collective-permute-start | bytes 3145736 | tf_op jit(solution)/shard_map/ppermute | solution.py:30
  515.9 38.3 %collective-permute-start.64 = (bf16[256,2048]{1,0:T(8,128)(2,1)S(1)}, bf16[256,2048]{1,0:T(8,128)(2,1)S(1)}, u32[]{:S(2)}, u32[]{:S(2)}) collective-permute-start(bf16[256,2048]{1,0:T(8,128)(2,1)S(1)} %pad_maximum_fusion.9), channel_id=1, source_target_pairs={{0,4},{1,5},{2,6},{3,7},{4,0},{5,1},{6,2},{7,3},{8,12},{9,13},{10,... | collective-permute-start | bytes 3145736 | tf_op jit(solution)/shard_map/ppermute | solution.py:30
  517.2 37.0 %collective-permute-start.63 = (bf16[256,2048]{1,0:T(8,128)(2,1)S(1)}, bf16[256,2048]{1,0:T(8,128)(2,1)}, u32[]{:S(2)}, u32[]{:S(2)}) collective-permute-start(bf16[256,2048]{1,0:T(8,128)(2,1)S(1)} %pad_maximum_fusion.8), channel_id=1, source_target_pairs={{0,2},{1,3},{2,0},{3,1},{4,6},{5,7},{6,4},{7,5},{8,10},{9,11},{10,... | collective-permute-start | bytes 3145736 | tf_op jit(solution)/shard_map/ppermute | solution.py:30
  557.2 28.5 %collective-permute-start.75 = (bf16[64,1024]{1,0:T(8,128)(2,1)S(1)}, bf16[64,1024]{1,0:T(8,128)(2,1)S(1)}, u32[]{:S(2)}, u32[]{:S(2)}) collective-permute-start(bf16[64,1024]{1,0:T(8,128)(2,1)S(1)} %get-tuple-element.449), channel_id=1, source_target_pairs={{0,24},{8,0},{16,8},{24,16},{1,25},{9,1},{17,9},{25,17},{2,26},{10... | collective-permute-start | bytes 393224 | tf_op jit(solution)/shard_map/ppermute | solution.py:35
  562.7 26.9 %collective-permute-start.68 = (bf16[256,2048]{1,0:T(8,128)(2,1)}, bf16[256,2048]{1,0:T(8,128)(2,1)S(1)}, u32[]{:S(2)}, u32[]{:S(2)}) collective-permute-start(bf16[256,2048]{1,0:T(8,128)(2,1)} %get-tuple-element.375), channel_id=1, source_target_pairs={{0,1},{1,0},{2,3},{3,2},{4,5},{5,4},{6,7},{7,6},{8,9},{9,8},{10,11... | collective-permute-start | bytes 3145736 | tf_op jit(solution)/shard_map/ppermute | solution.py:30
  568.6 33.3 %collective-permute-start.67 = (bf16[256,2048]{1,0:T(8,128)(2,1)}, bf16[256,2048]{1,0:T(8,128)(2,1)S(1)}, u32[]{:S(2)}, u32[]{:S(2)}) collective-permute-start(bf16[256,2048]{1,0:T(8,128)(2,1)} %get-tuple-element.371), channel_id=1, source_target_pairs={{0,1},{1,0},{2,3},{3,2},{4,5},{5,4},{6,7},{7,6},{8,9},{9,8},{10,11... | collective-permute-start | bytes 3145736 | tf_op jit(solution)/shard_map/ppermute | solution.py:30
  572.9 30.3 %collective-permute-start.65 = (bf16[256,2048]{1,0:T(8,128)(2,1)}, bf16[256,2048]{1,0:T(8,128)(2,1)S(1)}, u32[]{:S(2)}, u32[]{:S(2)}) collective-permute-start(bf16[256,2048]{1,0:T(8,128)(2,1)} %get-tuple-element.363), channel_id=1, source_target_pairs={{0,1},{1,0},{2,3},{3,2},{4,5},{5,4},{6,7},{7,6},{8,9},{9,8},{10,11... | collective-permute-start | bytes 3145736 | tf_op jit(solution)/shard_map/ppermute | solution.py:30
  614.5 49.5 %collective-permute-start.81 = (bf16[64,2048]{1,0:T(8,128)(2,1)}, bf16[64,2048]{1,0:T(8,128)(2,1)}, u32[]{:S(2)}, u32[]{:S(2)}) collective-permute-start(bf16[64,2048]{1,0:T(8,128)(2,1)} %fusion.10), channel_id=1, source_target_pairs={{0,0},{8,1},{16,2},{24,3},{1,4},{9,5},{17,6},{25,7},{2,8},{10,9},{... | collective-permute-start | bytes 786440 | tf_op jit(solution)/shard_map/ppermute | solution.py:96
  619.0 33.7 %collective-permute-start.80 = (bf16[512,384]{1,0:T(8,128)(2,1)S(1)}, bf16[512,384]{1,0:T(8,128)(2,1)S(1)}, u32[]{:S(2)}, u32[]{:S(2)}) collective-permute-start(bf16[512,384]{1,0:T(8,128)(2,1)S(1)} %pad_maximum_fusion.14), channel_id=1, source_target_pairs={{0,24},{8,0},{16,8},{24,16},{1,25},{9,1},{17,9},{25,17},{2,26},{10... | collective-permute-start | bytes 1179656 | tf_op jit(solution)/shard_map/ppermute | solution.py:35
  620.8 31.9 %collective-permute-start.79 = (bf16[512,384]{1,0:T(8,128)(2,1)S(1)}, bf16[512,384]{1,0:T(8,128)(2,1)S(1)}, u32[]{:S(2)}, u32[]{:S(2)}) collective-permute-start(bf16[512,384]{1,0:T(8,128)(2,1)S(1)} %pad_maximum_fusion.13), channel_id=1, source_target_pairs={{0,8},{8,16},{16,24},{24,0},{1,9},{9,17},{17,25},{25,1},{2,10},{10... | collective-permute-start | bytes 1179656 | tf_op jit(solution)/shard_map/ppermute | solution.py:35
  622.1 51.9 %collective-permute-start.78 = (bf16[256,2048]{1,0:T(8,128)(2,1)}, bf16[256,2048]{1,0:T(8,128)(2,1)}, u32[]{:S(2)}, u32[]{:S(2)}) collective-permute-start(bf16[256,2048]{1,0:T(8,128)(2,1)} %pad_maximum_fusion.11), channel_id=1, source_target_pairs={{0,4},{1,5},{2,6},{3,7},{4,0},{5,1},{6,2},{7,3},{8,12},{9,13},{10,... | collective-permute-start | bytes 3145736 | tf_op jit(solution)/shard_map/ppermute | solution.py:30
  659.3 28.1 %collective-permute-start.77 = (bf16[256,2048]{1,0:T(8,128)(2,1)}, bf16[256,2048]{1,0:T(8,128)(2,1)}, u32[]{:S(2)}, u32[]{:S(2)}) collective-permute-start(bf16[256,2048]{1,0:T(8,128)(2,1)} %pad_maximum_fusion.10), channel_id=1, source_target_pairs={{0,2},{1,3},{2,0},{3,1},{4,6},{5,7},{6,4},{7,5},{8,10},{9,11},{10,... | collective-permute-start | bytes 3145736 | tf_op jit(solution)/shard_map/ppermute | solution.py:30
  668.0 33.0 %all-to-all-start.3 = ((bf16[8,64,1408]{2,1,0:T(8,128)(2,1)}), bf16[8,64,1408]{2,1,0:T(8,128)(2,1)S(1)}, u32[]{:S(2)}, u32[]{:S(2)}) async-start(bf16[8,64,1408]{2,1,0:T(8,128)(2,1)} %bitcast.190), calls=%async_computation.4 | async-start | bytes 2883584 | tf_op jit(solution)/shard_map/all_to_all | solution.py:88
  (97 other events, 964.0 us)
Sparse Core Ops, SparseCore 0:
  23.0 97.0 all-gather.4
  187.8 106.7 all-gather.2
  411.4 55.6 reduce-scatter.4
  469.2 107.9 reduce-scatter.2

commit v2 on v1

--- a/solution.py
+++ b/solution.py
@@ -30,62 +30,73 @@
     return lax.ppermute(block, "seq", [(i, i ^ distance) for i in range(size)])
 
 
-def shift(block, step):
-    size = lax.axis_size("dp")
-    return lax.ppermute(block, "dp", [(i, (i + step) % size) for i in range(size)])
-
-
 def tie(*values):
     return lax.optimization_barrier(values)
 
 
-def gather_seq_first(block):
+def gather_seq_sides(block):
     if lax.axis_size("seq") != 8:
         return (lax.all_gather(block, "seq", axis=0),)
     return swap(block, 2), swap(block, 4), swap(block, 1)
 
 
-def gather_seq_rest(block, first):
+def gather_seq_corner(sides):
+    if lax.axis_size("seq") != 8:
+        return ()
+    along_x, along_y, _ = sides
+    for_x, for_y = cut(along_y, along_x)
+    return swap(for_x, 2), swap(for_y, 4), swap(along_x, 1), swap(along_y, 1)
+
+
+def gather_seq_all(block, sides, corner):
     size = lax.axis_size("seq")
     if size != 8:
         me = lax.axis_index("seq")
-        return [lax.dynamic_index_in_dim(first[0], me ^ d, 0, keepdims=False) for d in range(size)]
-    half = block.shape[0] // 2
-    along_x, along_y, beside = first
-    across = [swap(along_y[:half], 2), swap(along_x[half:], 4)]
-    blocks = [block, beside, along_x, swap(along_x, 1), along_y, swap(along_y, 1)]
-    across = jnp.concatenate(across, axis=0)
-    return blocks + [across, swap(across, 1)]
-
-
-def gather_seq(block):
-    return gather_seq_rest(block, gather_seq_first(block))
-
-
-def scatter_seq_first(parts):
+        return [lax.dynamic_index_in_dim(sides[0], me ^ d, 0, keepdims=False) for d in range(size)]
+    across = join(corner[0], corner[1])
+    return [block, sides[2], sides[0], corner[2], sides[1], corner[3], across, swap(across, 1)]
+
+
+def scatter_seq_beside(parts):
+    return () if lax.axis_size("seq") != 8 else (swap(parts[7], 1),)
+
+
+def scatter_seq_halves(parts, beside):
+    return () if lax.axis_size("seq") != 8 else cut_sum(parts[6], beside[0])
+
+
+def scatter_seq_ways(halves):
+    return () if lax.axis_size("seq") != 8 else (swap(halves[0], 2), swap(halves[1], 4))
+
+
+def scatter_seq_corner(parts, ways):
     size = lax.axis_size("seq")
     if size != 8:
         order = lax.axis_index("seq") ^ jnp.arange(size)
         parts = jnp.take(jnp.stack(parts), order, axis=0)
         return (lax.psum_scatter(parts, "seq", scatter_dimension=0),)
-    half = parts[0].shape[0] // 2
-    across = parts[6] + swap(parts[7], 1)
-    corner = swap(across[:half], 2), swap(across[half:], 4)
-    return [parts[2 * i] + swap(parts[2 * i + 1], 1) for i in range(3)], corner
-
-
-def scatter_seq_rest(first):
+    return list(ways) + [swap(parts[d], 1) for d in (1, 3, 5)]
+
+
+def scatter_seq_sums(parts, corner):
     if lax.axis_size("seq") != 8:
-        return first[0].astype(F32)
-    (own, for_x, for_y), (from_x, from_y) = first
-    half = own.shape[0] // 2
-    for_y = jnp.concatenate([for_y[:half] + from_x, for_y[half:]], axis=0)
-    for_x = jnp.concatenate([for_x[:half], for_x[half:] + from_y], axis=0)
-    return own.astype(F32) + swap(for_x, 2).astype(F32) + swap(for_y, 4).astype(F32)
+        return ()
+    from_x, from_y, _, beside_x, beside_y = corner
+    return sums_for_sides(parts[2], beside_x, parts[4], beside_y, from_x, from_y)
+
+
+def scatter_seq_sides(parts, corner, sums):
+    if lax.axis_size("seq") != 8:
+        return [corner[0]] + [jnp.zeros_like(corner[0])] * 3
+    return [parts[0], corner[2], swap(sums[0], 2), swap(sums[1], 4)]
 
 
 def exchange_seq(blocks):
     return lax.all_to_all(blocks, "seq", 0, 0, tiled=True)
+
+
+def exchange_all(blocks):
+    return lax.all_to_all(blocks, ("dp", "seq"), 0, 0, tiled=True)
 
 
 def deal(block, back=False):
@@ -96,66 +107,51 @@
     return lax.ppermute(block, ("dp", "seq"), pairs)
 
 
-def halves(block, axis):
-    middle = block.shape[axis] // 2
-    return (
-        lax.slice_in_dim(block, 0, middle, axis=axis),
-        lax.slice_in_dim(block, middle, block.shape[axis], axis=axis),
-    )
-
-
-def gather_dp_first(block):
-    return shift(block, 1), shift(block, -1)
-
-
-def gather_dp_rest(block, first, axis, whole=None, offset=0):
+def shift(block, step):
     size = lax.axis_size("dp")
-    me = lax.axis_index("dp")
-    if whole is None:
-        whole = jnp.zeros((size,) + block.shape, block.dtype)
-
-    def put(whole, piece, distance):
-        return lax.dynamic_update_slice(whole, piece[None], ((me + distance) % size, offset, 0))
-
-    whole = put(whole, block, 0)
-    up, down = first
-    for step in range(1, size // 2):
-        if step > 1:
-            up, down = shift(up, 1), shift(down, -1)
-        whole = put(put(whole, up, -step), down, step)
-    far = [shift(halves(up, axis)[0], 1), shift(halves(down, axis)[1], -1)]
-    return put(whole, jnp.concatenate(far, axis=axis), size // 2)
-
-
-def term_for(terms, distance):
+    return lax.ppermute(block, "dp", [(i, (i + step) % size) for i in range(size)])
+
+
+def gather_dp_near(block):
+    blocks = [block]
+    up = down = block
+    for _ in range(1, lax.axis_size("dp") // 2):
+        up, down = shift(up, -1), shift(down, 1)
+        blocks += [up, down]
+    return blocks
+
+
+def gather_dp_far(near):
+    up, down = cut_columns(near[-2], near[-1])
+    return [shift(up, -1), shift(down, 1)]
+
+
+def scatter_dp_far(blocks):
+    return [shift(blocks[-2], 1), shift(blocks[-1], -1)]
+
+
+def scatter_dp_near(blocks, far):
+    up, down = far
+    near = blocks[1:-2]
+    for step in range(len(near) // 2, 0, -1):
+        for_up, for_down = near[2 * step - 2 : 2 * step]
+        if 2 * step == len(near):
+            up, down = add_columns(for_up, up, 0), add_columns(for_down, down, up.shape[1])
+        else:
+            up, down = add_up([for_up, up], BF16), add_up([for_down, down], BF16)
+        up, down = shift(up, 1), shift(down, -1)
+    return [up, down]
+
+
+def gather_dp_direct(block):
     size = lax.axis_size("dp")
-    index = (lax.axis_index("dp") + distance) % size
-    if isinstance(terms, tuple):
-        terms, low, rows = terms
-        return lax.dynamic_slice(terms, (index, low, 0), (1, rows, terms.shape[2]))[0]
-    return lax.dynamic_index_in_dim(terms, index, 0, keepdims=False)
-
-
-def scatter_dp_first(terms, axis):
+    return [block] + [shift(block, -d) for d in range(1, size)]
+
+
+def scatter_dp_direct(term):
     size = lax.axis_size("dp")
-    far = halves(term_for(terms, size // 2), axis)
-    return shift(far[0], 1), shift(far[1], -1)
-
-
-def scatter_dp_rest(terms, first, axis):
-    size = lax.axis_size("dp")
-    up, down = first
-    for step in range(size // 2 - 1, 0, -1):
-        for_up, for_down = term_for(terms, step), term_for(terms, -step)
-        if step == size // 2 - 1:
-            kept = halves(for_up, axis)
-            up = jnp.concatenate([kept[0] + up, kept[1]], axis=axis)
-            kept = halves(for_down, axis)
-            down = jnp.concatenate([kept[0], kept[1] + down], axis=axis)
-        else:
-            up, down = for_up + up, for_down + down
-        up, down = shift(up, 1), shift(down, -1)
-    return term_for(terms, 0) + up + down
+    blocks = pick(lax.axis_index("dp"), term)
+    return [blocks[0]] + [shift(blocks[d], d) for d in range(1, size)]
 
 
 def padded(units):
@@ -209,6 +205,468 @@
 
 def params(**more):
     return pltpu.CompilerParams(vmem_limit_bytes=VMEM_BYTES, **more)
+
+
+STEPS = 2
+
+
+def by_rows(name, body, ins, outs):
+    half = STEPS // 2
+    index = {
+        "all": lambda i: (i, 0),
+        "low": lambda i: (jnp.minimum(i, half - 1), 0),
+        "high": lambda i: (jnp.maximum(i - half, 0), 0),
+        "still": lambda i: (0, 0),
+    }
+
+    def block(shape, how):
+        rows = shape[0] // {"all": STEPS, "low": half, "high": half, "still": 1}[how]
+        return pl.BlockSpec((rows, shape[1]), index[how])
+
+    def kernel(*refs):
+        body(pl.program_id(0), *refs)
+
+    return pl.pallas_call(
+        kernel,
+        out_shape=[jax.ShapeDtypeStruct(shape[:2], shape[2]) for shape, _ in outs],
+        grid=(STEPS,),
+        in_specs=[block(array.shape, how) for array, how in ins],
+        out_specs=[block(shape, how) for shape, how in outs],
+        compiler_params=params(),
+        cost_estimate=LIGHT,
+        name=name,
+    )(*[array for array, _ in ins])
+
+
+def copied(name, outs, shapes, plan, *arrays, prefetch=0):
+    count = len(shapes)
+
+    def kernel(*refs):
+        refs, held, came, went = refs[: -count - 2], refs[-count - 2 : -2], refs[-2], refs[-1]
+        pairs = plan(*refs)
+        inward = [
+            pltpu.make_async_copy(source, held[i], came.at[i]) for i, (source, _) in enumerate(pairs)
+        ]
+        outward = [
+            pltpu.make_async_copy(held[i], target, went.at[i]) for i, (_, target) in enumerate(pairs)
+        ]
+        for one in inward:
+            one.start()
+        for one, other in zip(inward, outward):
+            one.wait()
+            other.start()
+        for one in outward:
+            one.wait()
+
+    spaces = [pl.BlockSpec(memory_space=pltpu.SMEM)] * prefetch
+    spaces += [pl.BlockSpec(memory_space=pl.ANY)] * (len(arrays) - prefetch)
+    return pl.pallas_call(
+        kernel,
+        out_shape=[jax.ShapeDtypeStruct(*out) for out in outs],
+        in_specs=spaces,
+        out_specs=[pl.BlockSpec(memory_space=pl.ANY)] * len(outs),
+        scratch_shapes=[pltpu.VMEM(shape, BF16) for shape in shapes]
+        + [pltpu.SemaphoreType.DMA((count,))] * 2,
+        compiler_params=params(),
+        cost_estimate=LIGHT,
+        name=name,
+    )(*arrays)
+
+
+def first_half(ref, rows):
+    return ref.at[pl.ds(0, rows // 2), :]
+
+
+def second_half(ref, rows):
+    return ref.at[pl.ds(rows // 2, rows // 2), :]
+
+
+def cut(first, second):
+    rows, columns = first.shape
+
+    def plan(first, second, low, high):
+        return [(first_half(first, rows), low), (second_half(second, rows), high)]
+
+    shape = (rows // 2, columns)
+    return copied("cut", [(shape, BF16)] * 2, [shape] * 2, plan, first, second)
+
+
+def join(low, high):
+    rows, columns = 2 * low.shape[0], low.shape[1]
+
+    def plan(low, high, out):
+        return [(low, first_half(out, rows)), (high, second_half(out, rows))]
+
+    return copied("join", [((rows, columns), BF16)], [low.shape] * 2, plan, low, high)[0]
+
+
+def cut_sum(left, right):
+    rows, columns = left.shape
+    out = (rows // 2, columns, left.dtype)
+
+    def body(step, left, right, low, high):
+        total = left[...] + right[...]
+
+        @pl.when(step < STEPS // 2)
+        def _():
+            low[...] = total
+
+        @pl.when(step >= STEPS // 2)
+        def _():
+            high[...] = total
+
+    return by_rows("cut_sum", body, [(left, "all"), (right, "all")], [(out, "low"), (out, "high")])
+
+
+def sums_for_sides(own_x, beside_x, own_y, beside_y, from_x, from_y):
+    out = own_x.shape + (own_x.dtype,)
+
+    def body(step, own_x, beside_x, own_y, beside_y, from_x, from_y, for_x, for_y):
+        late = step >= STEPS // 2
+        sum_x = own_x[...].astype(F32) + beside_x[...].astype(F32)
+        sum_y = own_y[...].astype(F32) + beside_y[...].astype(F32)
+        for_x[...] = (sum_x + jnp.where(late, from_y[...].astype(F32), 0.0)).astype(for_x.dtype)
+        for_y[...] = (sum_y + jnp.where(late, 0.0, from_x[...].astype(F32))).astype(for_y.dtype)
+
+    ins = [(one, "all") for one in (own_x, beside_x, own_y, beside_y)]
+    return by_rows("sums_for_sides", body, ins + [(from_x, "low"), (from_y, "high")], [(out, "all")] * 2)
+
+
+def total_of(terms):
+    return sum(one[...].astype(F32) for one in terms)
+
+
+def end_attention(me, block, mixed, w_out, gain):
+    count, rows, mine = mixed.shape
+    width = block.shape[1]
+
+    def kernel(me, block, mixed, gain, *refs):
+        w_refs, refs = refs[:count], refs[count:]
+        residual, acts, w_all, mixed_all, done = refs
+        copies = [
+            pltpu.make_async_copy(w_refs[one], w_all.at[pl.ds(one * mine, mine), :], done.at[one])
+            for one in range(count)
+        ]
+        for one in copies:
+            one.start()
+        for one in range(count):
+            mixed_all[:, one * mine : (one + 1) * mine] = mixed[one ^ me[0]]
+        for one in copies:
+            one.wait()
+        for start in range(0, width, 512):
+            columns = slice(start, start + 512)
+            residual[:, columns] = block[:, columns].astype(F32) + nn(mixed_all[...], w_all[:, columns])
+        acts[...] = (normalize(residual[...])[0] * gain[...]).astype(BF16)
+
+    vmem = pl.BlockSpec(memory_space=pltpu.VMEM)
+    return pl.pallas_call(
+        kernel,
+        out_shape=[jax.ShapeDtypeStruct((rows, width), F32), jax.ShapeDtypeStruct((rows, width), BF16)],
+        in_specs=[pl.BlockSpec(memory_space=pltpu.SMEM)] + [vmem] * 3 + [pl.BlockSpec(memory_space=pl.ANY)] * count,
+        scratch_shapes=[
+            pltpu.VMEM((count * mine, width), BF16),
+            pltpu.VMEM((rows, count * mine), BF16),
+            pltpu.SemaphoreType.DMA((count,)),
+        ],
+        compiler_params=params(),
+        cost_estimate=LIGHT,
+        name="end_attention",
+    )(scalar(me), block, mixed, gain, *w_out)
+
+
+def back_to_heads(me, grad, w_out):
+    count, (mine, width), rows = len(w_out), w_out[0].shape, grad.shape[0]
+
+    def kernel(me, grad, *refs):
+        for one in range(count):
+            refs[-1][one ^ me[0]] = nt(grad[...], refs[one][...]).astype(BF16)
+
+    shape = ((count, rows, mine), BF16)
+    return local("back_to_heads", kernel, [shape], scalar(me), grad, *w_out, prefetch=1)[0]
+
+
+def out_products(me, mixed, grad):
+    count, _, mine = mixed.shape
+    width = grad.shape[1]
+
+    def kernel(me, mixed, grad, *outs):
+        for one, out in enumerate(outs):
+            out[...] = tn(mixed[one ^ me[0]], grad[...]).astype(BF16)
+
+    shapes = [((mine, width), BF16)] * count
+    return list(local("out_products", kernel, shapes, scalar(me), mixed, grad, prefetch=1))
+
+
+def back_through_norm(before, inputs, terms, gain, low):
+    rows, width = inputs.shape
+
+    def body(step, before, inputs, one, two, three, four, gain, grad, *grad_low):
+        normed, inverse = normalize(inputs[...].astype(F32))
+        grad_normed = total_of((one, two, three, four)) * gain[...]
+        result = before[...].astype(F32) + norm_back(grad_normed, normed, inverse)
+        grad[...] = result
+        if low:
+            grad_low[0][...] = result.astype(BF16)
+
+    ins = [(one, "all") for one in (before, inputs, *terms)] + [(gain, "still")]
+    outs = [((rows, width, F32), "all")] + [((rows, width, BF16), "all")] * low
+    return by_rows("back_through_norm", body, ins, outs)
+
+
+def end_output(residual, terms):
+    def body(step, residual, one, two, three, four, out):
+        out[...] = (residual[...] + total_of((one, two, three, four))).astype(BF16)
+
+    ins = [(one, "all") for one in (residual, *terms)]
+    return by_rows("end_output", body, ins, [(residual.shape + (BF16,), "all")])[0]
+
+
+def local(name, kernel, outs, *arrays, prefetch=0):
+    spaces = [pl.BlockSpec(memory_space=pltpu.SMEM)] * prefetch
+    spaces += [pl.BlockSpec(memory_space=pltpu.VMEM)] * (len(arrays) - prefetch)
+    return pl.pallas_call(
+        kernel,
+        out_shape=[jax.ShapeDtypeStruct(*out) for out in outs],
+        in_specs=spaces,
+        compiler_params=params(),
+        cost_estimate=LIGHT,
+        name=name,
+    )(*arrays)
+
+
+def cut_columns(first, second):
+    rows, columns = first.shape
+    half = columns // 2
+
+    def plan(first, second, low, high):
+        return [(first.at[:, pl.ds(0, half)], low), (second.at[:, pl.ds(half, half)], high)]
+
+    shape = (rows, half)
+    return copied("cut_columns", [(shape, BF16)] * 2, [shape] * 2, plan, first, second)
+
+
+def scalar(value):
+    return value.reshape(1).astype(jnp.int32)
+
+
+def place(me, blocks, distances, far=()):
+    size = len(blocks) + (1 if far else 0)
+    rows, columns = blocks[0].shape
+    half = columns // 2
+
+    def plan(me, *refs):
+        out = refs[-1]
+
+        def at(distance):
+            return lax.rem(me[0] + distance + size, size)
+
+        pairs = [(block, out.at[at(distance)]) for block, distance in zip(refs, distances)]
+        if far:
+            pairs.append((refs[-3], out.at[at(size // 2), :, pl.ds(0, half)]))
+            pairs.append((refs[-2], out.at[at(size // 2), :, pl.ds(half, half)]))
+        return pairs
+
+    out = ((size, rows, columns), BF16)
+    shapes = [one.shape for one in (*blocks, *far)]
+    whole = copied("place", [out], shapes, plan, scalar(me), *blocks, *far, prefetch=1)[0]
+    return whole.reshape(size * rows, columns)
+
+
+def pick(me, term):
+    size, rows, columns = term.shape
+
+    def plan(me, term, *outs):
+        return [
+            (term.at[lax.rem(me[0] + distance, size)], out)
+            for distance, out in enumerate(outs)
+        ]
+
+    shapes = [(rows, columns)] * size
+    outs = [(shape, BF16) for shape in shapes]
+    return copied("pick", outs, shapes, plan, scalar(me), term, prefetch=1)
+
+
+def pick_halves(me, term):
+    size, rows, columns = term.shape
+    half = columns // 2
+    distances = [0] + [sign * one for one in range(1, size // 2) for sign in (1, -1)]
+
+    def plan(me, term, *outs):
+        def at(distance):
+            return lax.rem(me[0] + distance + size, size)
+
+        pairs = [(term.at[at(distance)], out) for distance, out in zip(distances, outs)]
+        for which in range(2):
+            pairs.append((term.at[at(size // 2), :, pl.ds(which * half, half)], outs[which - 2]))
+        return pairs
+
+    shapes = [(rows, columns)] * len(distances) + [(rows, half)] * 2
+    outs = [(shape, BF16) for shape in shapes]
+    return copied("pick_halves", outs, shapes, plan, scalar(me), term, prefetch=1)
+
+
+def add_columns(block, part, start):
+    def kernel(block, part, out):
+        out[...] = block[...]
+        columns = slice(start, start + part.shape[1])
+        out[:, columns] = block[:, columns] + part[...]
+
+    return local("add_columns", kernel, [(block.shape, BF16)], block, part)[0]
+
+
+def pack_projections(w_query, w_key, w_value, attn_norm, ffn_norm, ids, n_dp, n_seq):
+    owned = w_query.shape[0]
+    mine = w_query.shape[1] // n_seq
+    group = n_seq // KV_HEADS
+    tiles = mine // LANES
+    spare = jnp.zeros((HEAD - owned,), BF16)
+    gains = jnp.concatenate([attn_norm, spare, ffn_norm, spare]).reshape(1, LANES)
+    ids = ids.astype(BF16).reshape(-1, LANES)
+    small = jnp.pad(jnp.concatenate([gains, ids]), ((0, 15 - ids.shape[0]), (0, 0)))
+
+    def kernel(w_query, w_key, w_value, small, out):
+        for there in range(n_seq):
+            for tile in range(tiles):
+                start = there * mine + tile * LANES
+                for copy in range(n_dp):
+                    out[copy * n_seq + there, tile * owned : (tile + 1) * owned] = w_query[:, start : start + LANES]
+            head = there // group
+            columns = slice(head * HEAD, (head + 1) * HEAD)
+            tile = jnp.concatenate([w_key[:, columns], w_value[:, columns]], axis=1)
+            for copy in range(n_dp):
+                out[copy * n_seq + there, tiles * owned : (tiles + 1) * owned] = tile
+                out[copy * n_seq + there, (tiles + 1) * owned :] = small[...]
+
+    shape = ((n_dp * n_seq, (tiles + 1) * owned + 16, LANES), BF16)
+    return local("pack_projections", kernel, [shape], w_query, w_key, w_value, small)[0]
+
+
+def unpack_projections(me_dp, packed, owned, n_seq, seqs, here):
+    devices, rows, _ = packed.shape
+    tiles = (rows - 16) // owned
+    width = devices * owned
+    length = n_seq * here
+
+    def kernel(me, packed, w_qkv, gain_one, gain_two, cosine, sine, first):
+        gains = [[], []]
+        for one in range(devices):
+            for tile in range(tiles):
+                w_qkv[one * owned : (one + 1) * owned, tile * LANES : (tile + 1) * LANES] = packed[
+                    one, tile * owned : (tile + 1) * owned
+                ]
+            row = packed[one, tiles * owned :].astype(F32)[:1]
+            gains[0].append(row[:, :owned])
+            gains[1].append(row[:, HEAD : HEAD + owned])
+        gain_one[...] = jnp.concatenate(gains[0], axis=1)
+        gain_two[...] = jnp.concatenate(gains[1], axis=1)
+        lane = lax.broadcasted_iota(jnp.int32, (here, LANES), 1)
+        frequency = jnp.exp((lane % (HEAD // 2)).astype(F32) * (-2.0 * math.log(ROPE_BASE) / HEAD))
+        sign = jnp.where(lane % HEAD < HEAD // 2, -1.0, 1.0)
+        for seq in range(seqs):
+            ids = []
+            for there in range(n_seq):
+                block = packed[me[0] * n_seq + there, tiles * owned :].astype(F32)
+                pieces = here // LANES
+                ids += [block[1 + seq * pieces + piece :][:1] for piece in range(pieces)]
+            ids = jnp.concatenate(ids, axis=1)
+            places = lax.broadcasted_iota(jnp.int32, (1, length), 1)
+            begins = (places == 0) | (ids != pltpu.roll(ids, 1, 1))
+            latest = jnp.where(begins, places, 0)
+            step = 1
+            while step < length:
+                moved = jnp.where(places >= step, pltpu.roll(latest, step, 1), 0)
+                latest = jnp.maximum(latest, moved)
+                step *= 2
+            first[seq] = latest
+            offsets = (places - latest).astype(F32)
+            for low in range(0, length, LANES):
+                column = jnp.broadcast_to(offsets[:, low : low + LANES], (LANES, LANES)).T
+                angles = column * frequency[:LANES]
+                cosine[seq, low : low + LANES] = jnp.cos(angles)
+                sine[seq, low : low + LANES] = jnp.sin(angles) * sign[:LANES]
+
+    outs = [
+        ((width, tiles * LANES), BF16),
+        ((1, width), F32),
+        ((1, width), F32),
+        ((seqs, length, LANES), F32),
+        ((seqs, length, LANES), F32),
+        ((seqs, 1, length), jnp.int32),
+    ]
+    return local("unpack_projections", kernel, outs, scalar(me_dp), packed, prefetch=1)
+
+
+def pack_units(w_gate, w_up, n_dp, n_seq):
+    owned = w_gate.shape[0]
+    here = w_gate.shape[1] // (n_dp * n_seq)
+    spare = padded(n_dp * here) - n_dp * here
+
+    def kernel(w_gate, w_up, out):
+        for there in range(n_seq):
+            both = []
+            for weight in (w_gate, w_up):
+                pieces = [
+                    weight[:, (one * n_seq + there) * here : (one * n_seq + there + 1) * here]
+                    for one in range(n_dp)
+                ]
+                if spare:
+                    pieces.append(jnp.zeros((owned, spare), BF16))
+                both.append(jnp.concatenate(pieces, axis=1))
+            out[there] = interleave(*both)
+
+    shape = ((n_seq, owned, 2 * padded(n_dp * here)), BF16)
+    return local("pack_units", kernel, [shape], w_gate, w_up)[0]
+
+
+def unpack_units(parts, w_gate, w_up, n_dp, n_seq):
+    owned, columns = w_gate.shape
+    here = columns // (n_dp * n_seq)
+
+    def kernel(parts, w_gate, w_up, grad_gate, grad_up, sums):
+        pieces = [[None] * (n_dp * n_seq) for _ in range(2)]
+        for there in range(n_seq):
+            for which, values in enumerate(separate(parts[there].astype(F32))):
+                for one in range(n_dp):
+                    pieces[which][one * n_seq + there] = values[:, one * here : (one + 1) * here]
+        total = 0.0
+        for found, weight, out in zip(pieces, (w_gate, w_up), (grad_gate, grad_up)):
+            whole = jnp.concatenate(found, axis=1)
+            out[...] = whole
+            total = total + jnp.sum(whole * weight[...].astype(F32), axis=1, keepdims=True)
+        sums[...] = jnp.broadcast_to(total, sums.shape)
+
+    outs = [((owned, columns), F32), ((owned, columns), F32), ((owned, LANES), F32)]
+    return local("unpack_units", kernel, outs, parts, w_gate, w_up)
+
+
+def unpack_columns(parts, w_query, w_key, w_value, n_dp, n_seq):
+    owned = w_query.shape[0]
+    mine = w_query.shape[1] // n_seq
+    group = n_seq // KV_HEADS
+
+    def kernel(parts, w_query, w_key, w_value, grad_query, grad_key, grad_value, sums):
+        last = []
+        for there in range(n_seq):
+            total = sum(parts[one * n_seq + there].astype(F32) for one in range(n_dp))
+            grad_query[:, there * mine : (there + 1) * mine] = total[:, :mine]
+            last.append(total[:, mine:])
+        heads = [sum(last[head * group : (head + 1) * group]) for head in range(KV_HEADS)]
+        grad_key[...] = jnp.concatenate([one[:, :HEAD] for one in heads], axis=1)
+        grad_value[...] = jnp.concatenate([one[:, HEAD:] for one in heads], axis=1)
+        total = 0.0
+        for weight, grad in ((w_query, grad_query), (w_key, grad_key), (w_value, grad_value)):
+            total = total + jnp.sum(weight[...].astype(F32) * grad[...], axis=1, keepdims=True)
+        sums[...] = jnp.broadcast_to(total, sums.shape)
+
+    outs = [(one.shape, F32) for one in (w_query, w_key, w_value)] + [((owned, LANES), F32)]
+    return local("unpack_columns", kernel, outs, parts, w_query, w_key, w_value)
+
+
+def add_up(terms, dtype):
+    def kernel(*refs):
+        refs[-1][...] = total_of(refs[:-1]).astype(dtype)
+
+    return local("add_up", kernel, [(terms[0].shape, dtype)], *terms)[0]
 
 
 def ffn_kernel(count, *refs):
@@ -387,8 +845,7 @@
 def attend_kernel(blocks, me_ref, *refs):
     raw_refs, refs = refs[:blocks], refs[blocks:]
     (cos_ref, sin_ref, first_ref), refs = refs[:3], refs[3:]
-    mixed_refs, refs = refs[:blocks], refs[blocks:]
-    kept_ref, q_ref, kv_ref, lse_ref, keys, vals_t, scores, weights, turned_out = refs
+    mixed_ref, kept_ref, q_ref, kv_ref, lse_ref, keys, vals_t, scores, weights, turned_out = refs
     me = me_ref[0]
     here = raw_refs[0].shape[1]
     pairs = q_ref.shape[1]
@@ -446,12 +903,11 @@
         done = turned_out[...].reshape(2 * pairs * HEAD, ROWS).T.astype(BF16)
         kept_ref[0, times, :] = done
     for one in range(blocks):
-        rows = pl.ds(pl.multiple_of((one ^ me) * here, here), here)
-        mixed_refs[one][0] = kept_ref[0, rows, :]
+        mixed_ref[one, 0] = kept_ref[0, one * here : (one + 1) * here, :]
 
 
 def attend_back_kernel(blocks, me_ref, *refs):
-    grad_refs, refs = refs[:blocks], refs[blocks:]
+    grad_ref, refs = refs[0], refs[1:]
     (kept_ref, q_ref, kv_ref, lse_ref, cos_ref, sin_ref, first_ref), refs = refs[:7], refs[7:]
     raw_refs, refs = refs[:blocks], refs[blocks:]
     keys, vals, keys_t, grads, weights, d_scores, dots, turned_out, acc_k, acc_v, result = refs
@@ -473,9 +929,8 @@
         vals[0, rows, :] = jnp.where(low_half, other, 0.0).astype(BF16)
         vals[1, rows, :] = jnp.where(low_half, 0.0, tile).astype(BF16)
         keys_t[:, rows] = tile.T[:HEAD].astype(BF16)
-        there = pl.ds(pl.multiple_of((one ^ me) * here, here), here)
         for pair in range(pairs):
-            grads[pair, there, :] = grad_refs[one][0, :, pair * LANES : (pair + 1) * LANES]
+            grads[pair, rows, :] = grad_ref[one, 0, :, pair * LANES : (pair + 1) * LANES]
 
     wide_lane = lax.broadcasted_iota(jnp.int32, (ROWS, LANES), 1)
     for start in range(0, length, ROWS):
@@ -543,7 +998,8 @@
     length = blocks * here
     pairs = width // LANES - 1
     mine = 2 * pairs * HEAD
-    shapes = [jax.ShapeDtypeStruct((seqs, here, mine), BF16)] * blocks + [
+    shapes = [
+        jax.ShapeDtypeStruct((blocks, seqs, here, mine), BF16),
         jax.ShapeDtypeStruct((seqs, length, mine), BF16),
         jax.ShapeDtypeStruct((seqs, pairs, length, LANES), BF16),
         jax.ShapeDtypeStruct((seqs, length, LANES), BF16),
@@ -557,7 +1013,7 @@
             num_scalar_prefetch=1,
             grid=(seqs,),
             in_specs=[whole_of(one.shape) for one in inputs],
-            out_specs=[whole_of(one.shape) for one in shapes],
+            out_specs=[listed(shapes[0].shape)] + [whole_of(one.shape) for one in shapes[1:]],
             scratch_shapes=[
                 pltpu.VMEM((2, length, LANES), BF16),
                 pltpu.VMEM((HEAD, length), BF16),
@@ -570,23 +1026,26 @@
         cost_estimate=LIGHT,
         name="attend",
     )(me, *inputs)
-    return list(out[:blocks]), list(out[blocks:])
+    return out[0], list(out[1:])
+
+
+def listed(shape):
+    return pl.BlockSpec((shape[0], 1) + tuple(shape[2:]), lambda b, me: (0, b, 0, 0))
 
 
 def attend_back(me, grads, kept, queries, keys_values, lse, cosine, sine, first):
-    blocks = len(grads)
-    seqs, here, mine = grads[0].shape
+    blocks, seqs, here, mine = grads.shape
     length = blocks * here
     pairs = queries.shape[1]
     shapes = [jax.ShapeDtypeStruct((seqs, here, mine + LANES), BF16)] * blocks
-    inputs = (*grads, kept, queries, keys_values, lse, cosine, sine, first)
+    inputs = (kept, queries, keys_values, lse, cosine, sine, first)
     return pl.pallas_call(
         functools.partial(attend_back_kernel, blocks),
         out_shape=shapes,
         grid_spec=pltpu.PrefetchScalarGridSpec(
             num_scalar_prefetch=1,
             grid=(seqs,),
-            in_specs=[whole_of(one.shape) for one in inputs],
+            in_specs=[listed(grads.shape)] + [whole_of(one.shape) for one in inputs],
             out_specs=[whole_of(one.shape) for one in shapes],
             scratch_shapes=[
                 pltpu.VMEM((2, length, LANES), BF16),
@@ -605,23 +1064,7 @@
         compiler_params=params(),
         cost_estimate=LIGHT,
         name="attend_back",
-    )(me, *inputs)
-
-
-def rotary(doc_ids):
-    length = doc_ids.shape[1]
-    places = jnp.broadcast_to(jnp.arange(length, dtype=jnp.int32)[None], doc_ids.shape)
-    before = jnp.concatenate([doc_ids[:, :1] - 1, doc_ids[:, :-1]], axis=1)
-    first = lax.cummax(jnp.where(doc_ids != before, places, 0), axis=1)
-    offsets = (places - first).astype(F32)
-    frequency = ROPE_BASE ** (-2.0 * jnp.arange(HEAD // 2, dtype=F32) / HEAD)
-    angles = offsets[..., None] * frequency
-    cosine, sine = jnp.cos(angles), jnp.sin(angles)
-    return (
-        jnp.concatenate([cosine] * 4, axis=-1),
-        jnp.concatenate([-sine, sine, -sine, sine], axis=-1),
-        first[:, None, :],
-    )
+    )(me, grads, *inputs)
 
 
 def norm_back(grad_normed, normed, inverse):
@@ -637,48 +1080,19 @@
     inputs, segment_ids, attn_norm, w_query, w_key, w_value, w_out, ffn_norm, w_gate, w_up, w_down, grad_output
 ):
     n_dp, n_seq = lax.axis_size("dp"), lax.axis_size("seq")
-    me = lax.axis_index("seq")
+    me, me_dp = lax.axis_index("seq"), lax.axis_index("dp")
     seqs, here, width = inputs.shape
     tokens = seqs * here
     owned = w_query.shape[0]
-    group = n_seq // KV_HEADS
-    own_heads = HEADS // n_seq
+    mine = HEADS // n_seq * HEAD
     units_here = w_down.shape[0]
     units = units_here * n_dp
-    me_array = me.reshape(1).astype(jnp.int32)
-
-    mine = own_heads * HEAD
-
-    def per_kv_head(weight):
-        return jnp.repeat(weight.reshape(owned, KV_HEADS, HEAD), group, axis=1)
-
-    gains = jnp.pad(jnp.concatenate([attn_norm, ffn_norm]), (0, mine + LANES - 2 * owned))
-    ids = segment_ids.astype(BF16).reshape(seqs, here)
-    ids = jnp.pad(ids, ((0, 0), (0, mine + LANES - here)))
-    extra = jnp.pad(jnp.concatenate([gains[None], ids]), ((0, 15 - seqs), (0, 0)))
-    qkv_blocks = jnp.concatenate(
-        [
-            w_query.reshape(owned, n_seq, own_heads * HEAD),
-            per_kv_head(w_key),
-            per_kv_head(w_value),
-        ],
-        axis=2,
-    ).transpose(1, 0, 2)
-    qkv_blocks = jnp.concatenate(
-        [qkv_blocks, jnp.broadcast_to(extra, (n_seq,) + extra.shape)], axis=1
-    )
-
-    def unit_blocks(weight):
-        blocks = weight.reshape(owned, n_dp, n_seq, units_here).transpose(2, 0, 1, 3)
-        blocks = blocks.reshape(n_seq, owned, units)
-        return jnp.pad(blocks, ((0, 0), (0, 0), (0, padded(units) - units)))
-
-    def as_rows(received):
-        return received.reshape(received.shape[0] * received.shape[1], received.shape[2])
-
-    pairs = [0, n_seq - 2] + list(range(2, n_seq - 2, 2))
-
-    def by_pairs(function, *lists):
+    me_array = scalar(me)
+
+    outwards = list(range(0, n_seq, 2))
+    inwards = outwards[::-1]
+
+    def by_pairs(function, pairs, *lists):
         results = None
         for pair in pairs:
             found = function(*[one[pair : pair + 2] for one in lists])
@@ -695,117 +1109,147 @@
 
     block = inputs.reshape(tokens, width)
     upstream = grad_output.reshape(tokens, width)
-    w_down_here = lax.all_gather(w_down, "dp", axis=0, tiled=True)
-    qkv_rows = exchange_seq(qkv_blocks)
-    doc_all = qkv_rows[:, owned + 1 : owned + 1 + seqs, :here].astype(jnp.int32)
-    doc_all = doc_all.transpose(1, 0, 2).reshape(seqs, n_seq * here)
-    qkv_rows = as_rows(qkv_rows)
+    both_blocks = pack_units(w_gate, w_up, n_dp, n_seq)
+    both_rows = exchange_seq(both_blocks).reshape(n_seq * owned, both_blocks.shape[2])
+    sides = gather_seq_sides(block)
+    down_near = gather_dp_near(w_down)
+    packed = pack_projections(w_query, w_key, w_value, attn_norm, ffn_norm, segment_ids, n_dp, n_seq)
+    sides, packed, both_rows, w_out, down_near = tie(sides, packed, both_rows, w_out, down_near)
+    packed = exchange_all(packed)
+    inputs_all = gather_seq_all(block, sides, gather_seq_corner(sides))
     out_rows = deal(w_out)
-    inputs_first = gather_seq_first(block)
-    qkv_rows, doc_all, out_rows, inputs_first = tie(qkv_rows, doc_all, out_rows, inputs_first)
-    w_qkv = gather_dp_rest(qkv_rows, gather_dp_first(qkv_rows), 0)
-    inputs_all = gather_seq_rest(block, inputs_first)
-    both_blocks = interleave(unit_blocks(w_gate), unit_blocks(w_up))
-    cosine, sine, first = rotary(doc_all)
-    w_qkv, inputs_all, both_blocks, cosine, sine, first = tie(
-        w_qkv, inputs_all, both_blocks, cosine, sine, first
+    packed, inputs_all, out_rows, both_rows = tie(packed, inputs_all, out_rows, both_rows)
+
+    out_blocks = gather_dp_direct(out_rows)
+    grad_sides = gather_seq_sides(upstream)
+    w_qkv, gain_one, gain_two, cosine, sine, first = unpack_projections(
+        me_dp, packed, owned, n_seq, seqs, here
     )
-
-    both_rows = as_rows(exchange_seq(both_blocks))
+    acts_one, raw = by_pairs(lambda blocks: enter(blocks, gain_one, w_qkv), outwards, inputs_all)
+    acts_one, raw, out_blocks, both_rows, grad_sides = tie(
+        acts_one, raw, out_blocks, both_rows, grad_sides
+    )
     w_both = lax.all_gather(both_rows, "dp", axis=0, tiled=True)
-    w_out_here = gather_dp_rest(out_rows, gather_dp_first(out_rows), 1).reshape(mine, width)
-    w_qkv = w_qkv.reshape(n_dp * n_seq, owned + 16, mine + LANES)
-    gain_one = w_qkv[:, owned, :owned].reshape(1, width).astype(F32)
-    gain_two = w_qkv[:, owned, owned : 2 * owned].reshape(1, width).astype(F32)
-    w_qkv = w_qkv[:, :owned].reshape(width, mine + LANES)
-    acts_one, raw = by_pairs(lambda blocks: enter(blocks, gain_one, w_qkv), inputs_all)
+    w_out_here = place(me_dp, out_blocks, range(n_dp))
+    out_sides = gather_seq_sides(w_out_here)
     mixed, saved = attend(me_array, in_sequences(raw), cosine, sine, first)
-    mixed, saved, both_rows, w_out_here = tie(mixed, saved, both_rows, w_out_here)
-    mixed = in_rows(mixed)
-
-    state = block.astype(F32)
-    (out_terms,) = by_pairs(lambda blocks: (multiply(blocks, w_out_here),), mixed)
-    out_first = scatter_seq_first(out_terms)
-    residual = state + scatter_seq_rest(out_first)
-    normed_two, inverse_two = normalize(residual)
-    acts_two = (normed_two * gain_two).astype(BF16)
-    grads_first = gather_seq_first(upstream)
-    residual, acts_two, grads_first = tie(residual, acts_two, grads_first)
-
+    mixed, saved, down_near, out_sides = tie(mixed, saved, down_near, out_sides)
+
+    mixed = exchange_seq(mixed.reshape(n_seq, tokens, mine))
+    w_out_all = gather_seq_all(w_out_here, out_sides, gather_seq_corner(out_sides))
+    mixed, w_out_all = tie(mixed, w_out_all)
+    down_far = gather_dp_far(down_near)
+    residual, acts_two = end_attention(me, block, mixed, w_out_all, gain_two)
+    residual, acts_two, grad_sides = tie(residual, acts_two, grad_sides)
+    grad_corner = gather_seq_corner(grad_sides)
+
+    def multiplied(target, blocks, right, transposed, pairs):
+        for pair in pairs:
+            target[pair : pair + 2] = multiply(blocks[pair : pair + 2], right, transposed)
+
+    distances = [0] + [sign * one for one in range(1, n_dp // 2) for sign in (1, -1)]
+    w_down_here = place(me_dp, down_near, distances, down_far)
     w_down_here = jnp.pad(w_down_here, ((0, padded(units) - units), (0, 0)))
-    acts_all = gather_seq(acts_two)
-    grads_all = gather_seq_rest(upstream, grads_first)
-    n_terms, f_terms, hidden, d_both = by_pairs(
-        lambda acts, grads: ffn(acts, grads, w_both, w_down_here), acts_all, grads_all
+    grads_all = gather_seq_all(upstream, grad_sides, grad_corner)
+    n_terms, f_terms, hidden, d_both = ([None] * n_seq for _ in range(4))
+
+    def feed_forward(acts, pair):
+        results = ffn(acts, grads_all[pair : pair + 2], w_both, w_down_here)
+        for target, found in zip((n_terms, f_terms, hidden, d_both), results):
+            target[pair : pair + 2] = found
+
+    sides = gather_seq_sides(acts_two)
+    if n_seq == 8:
+        feed_forward([acts_two, sides[2]], 0)
+        sides, n_terms, w_both, w_down_here = tie(sides, n_terms, w_both, w_down_here)
+        corner = gather_seq_corner(sides)
+        feed_forward([sides[0], corner[2]], 2)
+        corner, n_terms = tie(corner, n_terms)
+        acts_all = gather_seq_all(acts_two, sides, corner)
+        feed_forward(acts_all[6:], 6)
+        beside = scatter_seq_beside(n_terms)
+        beside, n_terms, acts_all = tie(beside, n_terms, acts_all)
+        n_ways = scatter_seq_ways(scatter_seq_halves(n_terms, beside))
+        feed_forward(acts_all[4:6], 4)
+        n_ways, n_terms = tie(n_ways, n_terms)
+    else:
+        acts_all = gather_seq_all(acts_two, sides, ())
+        for pair in outwards:
+            feed_forward(acts_all[pair : pair + 2], pair)
+        n_ways = ()
+    n_corner = scatter_seq_corner(n_terms, n_ways)
+    down_term = outer(hidden, grads_all, False, 512)
+    n_corner, n_terms, down_term = tie(n_corner, n_terms, down_term)
+    grad_down = lax.psum_scatter(down_term[:units], "dp", scatter_dimension=0, tiled=True)
+    n_sums = scatter_seq_sums(n_terms, n_corner)
+    n_sums, f_terms, d_both = tie(n_sums, f_terms, d_both)
+    n_sides = scatter_seq_sides(n_terms, n_corner, n_sums)
+    f_beside = scatter_seq_beside(f_terms)
+    both_term = outer(acts_all, d_both, True, 512)
+    f_halves = scatter_seq_halves(f_terms, f_beside)
+    n_sides, both_term, f_halves = tie(n_sides, both_term, f_halves)
+    grad_res, grad_res_low = back_through_norm(upstream, residual, n_sides, gain_two, True)
+    grad_res, grad_res_low = tie(grad_res, grad_res_low)
+
+    d_mixed = back_to_heads(me, grad_res_low, w_out_all)
+    f_ways = scatter_seq_ways(f_halves)
+    d_mixed, grad_res_low, f_ways, f_terms = tie(d_mixed, grad_res_low, f_ways, f_terms)
+    f_corner = scatter_seq_corner(f_terms, f_ways)
+    d_mixed = exchange_seq(d_mixed)
+    out_terms = out_products(me, mixed, grad_res_low)
+    out_beside = scatter_seq_beside(out_terms)
+    d_mixed, out_beside, out_terms, f_corner, grad_down, both_term = tie(
+        d_mixed, out_beside, out_terms, f_corner, grad_down, both_term
     )
-    n_first = scatter_seq_first(n_terms)
-    n_first, f_terms, hidden, d_both = tie(n_first, f_terms, hidden, d_both)
-    both_term = outer(acts_all, d_both, True, 512)
     both_sum = lax.psum_scatter(both_term, "dp", scatter_dimension=0, tiled=True)
-    down_term = outer(hidden, grads_all, False, 512)[:units]
-    grad_down = lax.psum_scatter(down_term, "dp", scatter_dimension=0, tiled=True).astype(F32)
-    grad_normed = scatter_seq_rest(n_first) * gain_two
-    normed_two, inverse_two = normalize(residual)
-    grad_res = upstream.astype(F32) + norm_back(grad_normed, normed_two, inverse_two)
-    grad_res_low = grad_res.astype(BF16)
-    grad_res, grad_res_low, both_term, down_term = tie(grad_res, grad_res_low, both_term, down_term)
-
-    res_first = gather_seq_first(grad_res_low)
-    f_first = scatter_seq_first(f_terms)
-    res_all = gather_seq_rest(grad_res_low, res_first)
-    (d_heads,) = by_pairs(lambda blocks: (multiply(blocks, w_out_here, True),), res_all)
-    d_heads, f_first = tie(d_heads, f_first)
-    d_raw = attend_back(me_array, in_sequences(d_heads), *saved, cosine, sine, first)
-    out_term = outer(mixed, res_all, False, 512).reshape(n_dp, owned, width)
-    output = (residual + scatter_seq_rest(f_first)).astype(BF16)
-    d_raw, out_term, output = tie(d_raw, out_term, output)
+    f_sides = scatter_seq_sides(f_terms, f_corner, scatter_seq_sums(f_terms, f_corner))
+    out_ways = scatter_seq_ways(scatter_seq_halves(out_terms, out_beside))
+    d_raw = attend_back(
+        me_array, d_mixed.reshape(n_seq, seqs, here, mine), *saved, cosine, sine, first
+    )
+    d_raw, out_ways, f_sides, out_terms = tie(d_raw, out_ways, f_sides, out_terms)
     d_raw = in_rows(d_raw)
-    (normed_terms,) = by_pairs(lambda blocks: (multiply(blocks, w_qkv, True),), d_raw)
-    normed_first = scatter_seq_first(normed_terms)
-    qkv_term = outer(acts_one, d_raw, True, 512).reshape(n_dp, n_seq * owned, mine + LANES)
-    qkv_first = scatter_dp_first(qkv_term, 0)
-    out_sum = scatter_dp_rest(out_term, scatter_dp_first(out_term, 1), 1)
-    normed_first, qkv_first, out_sum = tie(normed_first, qkv_first, out_sum)
-    qkv_sum = scatter_dp_rest(qkv_term, qkv_first, 0)
-    grad_out = deal(out_sum, back=True).astype(F32)
-    grad_normed = scatter_seq_rest(normed_first) * gain_one
-    normed_one, inverse_one = normalize(state)
-    grad_input = grad_res + norm_back(grad_normed, normed_one, inverse_one)
-
-    def rows_here(total):
-        return exchange_seq(total.reshape(n_seq, owned, total.shape[1])).astype(F32)
-
-    def unit_columns(blocks):
-        blocks = blocks[..., :units].reshape(n_seq, owned, n_dp, units_here).transpose(1, 2, 0, 3)
-        return blocks.reshape(owned, n_dp * n_seq * units_here)
-
-    raw_gate, raw_up = (unit_columns(one) for one in separate(rows_here(both_sum)))
-    qkv_rows = rows_here(qkv_sum)
-
-    def kv_columns(blocks):
-        blocks = blocks.reshape(KV_HEADS, group, owned, HEAD).sum(axis=1)
-        return blocks.transpose(1, 0, 2).reshape(owned, KV_HEADS * HEAD)
-
-    raw_query = qkv_rows[:, :, :mine].transpose(1, 0, 2).reshape(owned, n_seq * mine)
-    raw_key = kv_columns(qkv_rows[:, :, mine : mine + HEAD])
-    raw_value = kv_columns(qkv_rows[:, :, mine + HEAD :])
-
-    def gain_grad(gain, *pairs):
-        total = sum(jnp.sum(weight.astype(F32) * grad, axis=1) for weight, grad in pairs)
-        return total / gain.astype(F32)
-
+    out_corner = scatter_seq_corner(out_terms, out_ways)
+    terms = [None] * n_seq
+    multiplied(terms, d_raw, w_qkv, True, inwards[:1])
+    terms, d_raw, out_corner, out_terms = tie(terms, d_raw, out_corner, out_terms)
+    beside = scatter_seq_beside(terms)
+    out_sums = scatter_seq_sums(out_terms, out_corner)
+    qkv_term = outer(acts_one, d_raw, True, 512).reshape(n_dp * n_seq, owned, mine + LANES)
+    beside, terms, d_raw, qkv_term, out_sums = tie(beside, terms, d_raw, qkv_term, out_sums)
+    qkv_parts = exchange_all(qkv_term)
+    ways = scatter_seq_ways(scatter_seq_halves(terms, beside))
+    multiplied(terms, d_raw, w_qkv, True, inwards[1:])
+    ways, terms, out_sums = tie(ways, terms, out_sums)
+    out_sides = scatter_seq_sides(out_terms, out_corner, out_sums)
+    corner = scatter_seq_corner(terms, ways)
+    sums = scatter_seq_sums(terms, corner)
+    (sums,) = tie(sums)
+    out_term = add_up(out_sides, BF16).reshape(n_dp, owned, width)
+    out_parts = scatter_dp_direct(out_term)
+    sides = scatter_seq_sides(terms, corner, sums)
+    (grad_input,) = back_through_norm(grad_res, block, sides, gain_one, False)
+    grad_input, out_parts = tie(grad_input, out_parts)
+    both_parts = exchange_seq(both_sum.reshape(n_seq, owned, 2 * padded(units)))
+    grad_out = deal(add_up(out_parts, BF16), back=True).astype(F32)
+    output = end_output(residual, f_sides)
+
+    grad_gate, grad_up, sums_two = unpack_units(both_parts, w_gate, w_up, n_dp, n_seq)
+    grad_query, grad_key, grad_value, sums_one = unpack_columns(
+        qkv_parts, w_query, w_key, w_value, n_dp, n_seq
+    )
     return (
         output.reshape(seqs, here, width),
         grad_input.reshape(seqs, here, width),
-        gain_grad(attn_norm, (w_query, raw_query), (w_key, raw_key), (w_value, raw_value)),
-        raw_query,
-        raw_key,
-        raw_value,
+        sums_one[:, 0] / attn_norm.astype(F32),
+        grad_query,
+        grad_key,
+        grad_value,
         grad_out,
-        gain_grad(ffn_norm, (w_gate, raw_gate), (w_up, raw_up)),
-        raw_gate,
-        raw_up,
-        grad_down,
+        sums_two[:, 0] / ffn_norm.astype(F32),
+        grad_gate,
+        grad_up,
+        grad_down.astype(F32),
     )
 
 

time: 744 us -> 676 us (0.909); the launches traced: 732 us -> 671 us
  Pallas kernels: 229 us -> 309 us
  other arithmetic: 66.5 us -> 3.84 us
  waiting for transfers between devices: 241 us -> 187 us
  local copies, waits for them, and re-layouts: 61.5 us -> 25 us
  blocking collectives: 0 us -> 34.9 us
  starting transfers between devices: 119 us -> 97.2 us
    pallas_call x0 -> x33, Pallas kernels: none -> 114 us  [the longest x11 40.7 us: by_rows(): pl.pallas_call(kernel, out_shape=[jax.ShapeDtypeStruct(shape[:2], shape[2...]
    ppermute x64, waiting for transfers between devices: 135 us -> 61.9 us  [swap(): return lax.ppermute(block, 'seq', [(i, i ^ distance) for i in range(size)])]
    all_to_all x0 -> x2, blocking collectives: none -> 34.9 us  [exchange_seq(): return lax.all_to_all(blocks, 'seq', 0, 0, tiled=True)]
    all_to_all x0 -> x2, waiting for transfers between devices: none -> 31.7 us  [exchange_all(): return lax.all_to_all(blocks, ('dp', 'seq'), 0, 0, tiled=True)]
    pallas_call x12 -> x4, Pallas kernels: 41.6 us -> 15.6 us  [multiply(): pl.pallas_call(functools.partial(multiply_kernel, len(lefts), transposed)...]
    reshape x15 -> x0, local copies, waits for them, and re-layouts: 25.1 us -> none  [the longest x4 11.1 us: unit_columns(): blocks[..., :units].reshape(n_seq, owned, n_dp, units_here)]
    add x24 -> x0, other arithmetic: 21.3 us -> none  [the longest x11 10.2 us: scatter_seq_first(): parts[2 * i] + swap(parts[2 * i + 1], 1)]
    ppermute x2, waiting for transfers between devices: 0.01 us -> 19.8 us  [deal(): return lax.ppermute(block, ('dp', 'seq'), pairs)]
  transfers between devices with their start and end apart: 90 -> 83, of which waited for: 29 -> 27; matrix products, arithmetic and copies ran while one was open for 13% -> 1% of each run, Pallas kernels for 30% -> 42%
where the time goes in v2:
time: 676 us; the launch traced here: 671 us
  Pallas kernels  309 us (46%)
  waiting for transfers between devices  187 us (28%)
  starting transfers between devices  97.2 us (14%)
  blocking collectives  34.9 us (5%)
  local copies, waits for them, and re-layouts  25 us (4%)
  between operations  14.9 us (2%)
    ppermute x10, waiting for transfers between devices, shift(): lax.ppermute(block, 'dp', [(i, (i + step) % size) for i in range(size)])  73 us
    pallas_call x4, Pallas kernels, ffn(): pl.pallas_call(functools.partial(ffn_kernel, count), out_shape=shapes, co...  70.1 us
    ppermute x64, waiting for transfers between devices, swap(): return lax.ppermute(block, 'seq', [(i, i ^ distance) for i in range(size)])  61.9 us
    ppermute x64, starting transfers between devices, swap(): return lax.ppermute(block, 'seq', [(i, i ^ distance) for i in range(size)])  58.9 us
    pallas_call x11, Pallas kernels, by_rows(): pl.pallas_call(kernel, out_shape=[jax.ShapeDtypeStruct(shape[:2], shape[2...  40.7 us
    pallas_call x3, Pallas kernels, outer(): pl.pallas_call(functools.partial(outer_kernel, count, along_left), out_sh...  38.7 us
    pallas_call x9, Pallas kernels, local(): pl.pallas_call(kernel, out_shape=[jax.ShapeDtypeStruct(*out) for out in o...  38.6 us
    all_to_all x2, blocking collectives, exchange_seq(): return lax.all_to_all(blocks, 'seq', 0, 0, tiled=True)  34.9 us
  transfers between devices with their start and end apart: 83, of which 27 were waited for; matrix products, arithmetic and copies ran while one was open for 1% of the time, Pallas kernels for 42%

profile of v2, /device:TPU:1, one launch (start us, length us, event | category | flops | bytes accessed | tf_op | source)
XLA Modules:
  0.0 671.1 jit_solution(18086158343858382338)
XLA Ops:
  10.6 5.4 all-to-all-start
  25.3 12.1 %collective-permute-done.3.refs_0_.refs_2_ = bf16[176,2048]{1,0:T(8,128)(2,1)S(1)} collective-permute-done((bf16[176,2048]{1,0:T(8,128)(2,1)}, bf16[176,2048]{1,0:T(8,128)(2,1)S(1)}, u32[]{:S(2)}, u32[]{:S(2)}) %collective-permute-start.3) | collective-permute-done | bytes 720928 | tf_op jit(solution)/shard_map/ppermute | solution.py:112
  37.4 16.2 %collective-permute-done.4.refs_1_.refs_3_ = bf16[176,2048]{1,0:T(8,128)(2,1)S(1)} collective-permute-done((bf16[176,2048]{1,0:T(8,128)(2,1)}, bf16[176,2048]{1,0:T(8,128)(2,1)S(1)}, u32[]{:S(2)}, u32[]{:S(2)}) %collective-permute-start.4) | collective-permute-done | bytes 720928 | tf_op jit(solution)/shard_map/ppermute | solution.py:112
  57.6 5.5 all-to-all-start.1
  69.0 23.6 %collective-permute-done.7.refs_0_ = bf16[128,2048]{1,0:T(8,128)(2,1)S(1)} collective-permute-done((bf16[128,2048]{1,0:T(8,128)(2,1)}, bf16[128,2048]{1,0:T(8,128)(2,1)S(1)}, u32[]{:S(2)}, u32[]{:S(2)}) %collective-permute-start.7) | collective-permute-done | bytes 524320 | tf_op jit(solution)/shard_map/ppermute | solution.py:30
  100.2 4.6 collective-permute-done.10.refs_1_
  104.8 10.9 %collective-permute-start.15 = (bf16[256,2048]{1,0:T(8,128)(2,1)S(1)}, bf16[256,2048]{1,0:T(8,128)(2,1)S(1)}, u32[]{:S(2)}, u32[]{:S(2)}) collective-permute-start(bf16[256,2048]{1,0:T(8,128)(2,1)S(1)} %bitcast.40), channel_id=1, source_target_pairs={{0,4},{1,5},{2,6},{3,7},{4,0},{5,1},{6,2},{7,3},{8,12},{9,13},{10,... | collective-permute-start | bytes 3145736 | tf_op jit(solution)/shard_map/ppermute | solution.py:30
  121.1 7.7 %unpack_projections.1 = (bf16[2048,384]{1,0:T(8,128)(2,1)}, f32[1,2048]{1,0:T(1,128)}, f32[1,2048]{1,0:T(1,128)}, f32[2,1024,128]{2,1,0:T(8,128)}, f32[2,1024,128]{2,1,0:T(8,128)}, /*index=5*/s32[2,1,1024]{2,1,0:T(1,128)}) custom-call(s32[1]{0:T(128)} %bitcast.4.me.refs_0_, bf16[32,208,128]{2,1,0:T(8,128)(2,1)} %all-to-all-done.1.packed), custom_call_target="tpu_custom_call" | custom-call | flops 1 | bytes 1 | tf_op jit(solution)/shard_map/unpack_projections/pallas_call | solution.py:427
  128.8 4.6 enter.7
  133.3 4.6 enter.6
  137.9 4.6 enter.5
  142.5 4.5 enter.4
  152.0 23.9 %attend.1 = (bf16[8,2,128,256]{3,2,1,0:T(8,128)(2,1)}, bf16[2,1024,256]{2,1,0:T(8,128)(2,1)}, bf16[2,2,1024,128]{3,2,1,0:T(8,128)(2,1)}, bf16[2,1024,128]{2,1,0:T(8,128)(2,1)}, f32[2,4,1,1024]{3,2,1,0:T(1,128)}) custom-call(s32[1]{0:T(128)} %bitcast.me_ref.me, f32[2,128,384]{2,1,0:T(8,128)} %bitcast.83, f32[2,128,384]{2,1,0:T(8,128)} %bitcast.84, ...), custom_call_target="tpu_custom_call" | custom-call | flops 1 | bytes 1 | tf_op jit(solution)/shard_map/attend/pallas_call | solution.py:1009
  183.0 9.8 %collective-permute-done.22.refs_0_ = bf16[128,2048]{1,0:T(8,128)(2,1)S(1)} collective-permute-done((bf16[128,2048]{1,0:T(8,128)(2,1)}, bf16[128,2048]{1,0:T(8,128)(2,1)S(1)}, u32[]{:S(2)}, u32[]{:S(2)}) %collective-permute-start.22) | collective-permute-done | bytes 524320 | tf_op jit(solution)/shard_map/ppermute | solution.py:30
  198.1 17.2 %all_to_all.30.mixed = bf16[8,256,256]{2,1,0:T(8,128)(2,1)} all-to-all(bf16[8,256,256]{2,1,0:T(8,128)(2,1)S(1)} %bitcast.60), channel_id=1, replica_groups=mesh['dp'=4,'seq'=8] {'seq'}, dimensions={0} | all-to-all | bytes 2097152 | tf_op jit(solution)/shard_map/all_to_all | solution.py:95
  216.9 9.1 %end_attention.1 = (f32[256,2048]{1,0:T(8,128)}, bf16[256,2048]{1,0:T(8,128)(2,1)}) custom-call(s32[1]{0:T(128)} %bitcast.me_ref.me, bf16[256,2048]{1,0:T(8,128)(2,1)} %bitcast.43, bf16[8,256,256]{2,1,0:T(8,128)(2,1)} %all_to_all.30.mixed, f32[1,2048]{1,0:T(1,128)} %get-tuple-element.432.gain.refs_6_, bf16[256,2048]{1,0:T(8,128)(2,1)} %bitcast.51, ...), custom_call_target="tpu_custom_call" | custom-call | flops 1 | bytes 1 | tf_op jit(solution)/shard_map/end_attention/pallas_call | solution.py:362
  231.4 27.5 %collective-permute-done.28.refs_4_ = bf16[176,1024]{1,0:T(8,128)(2,1)S(1)} collective-permute-done((bf16[176,1024]{1,0:T(8,128)(2,1)}, bf16[176,1024]{1,0:T(8,128)(2,1)S(1)}, u32[]{:S(2)}, u32[]{:S(2)}) %collective-permute-start.28) | collective-permute-done | bytes 360480 | tf_op jit(solution)/shard_map/ppermute | solution.py:112
  258.9 5.9 collective-permute-done.29.refs_5_
  273.2 17.3 %ffn.4 = (bf16[256,2048]{1,0:T(8,128)(2,1)}, bf16[256,2048]{1,0:T(8,128)(2,1)}, bf16[256,2048]{1,0:T(8,128)(2,1)}, bf16[256,2048]{1,0:T(8,128)(2,1)}, bf16[256,7...) custom-call(bf16[256,2048]{1,0:T(8,128)(2,1)} %get-tuple-element.538.refs_0_, ...), custom_call_target="tpu_custom_call" | custom-call | flops 1 | bytes 1 | tf_op jit(solution)/shard_map/ffn/pallas_call | solution.py:724
  295.0 9.2 %collective-permute-done.37.refs_1_ = bf16[128,2048]{1,0:T(8,128)(2,1)S(1)} collective-permute-done((bf16[128,2048]{1,0:T(8,128)(2,1)S(1)}, bf16[128,2048]{1,0:T(8,128)(2,1)S(1)}, u32[]{:S(2)}, u32[]{:S(2)}) %collective-permute-start.37) | collective-permute-done | bytes 524320 | tf_op jit(solution)/shard_map/ppermute | solution.py:30
  309.9 17.5 %ffn.5 = (bf16[256,2048]{1,0:T(8,128)(2,1)}, bf16[256,2048]{1,0:T(8,128)(2,1)}, bf16[256,2048]{1,0:T(8,128)(2,1)}, bf16[256,2048]{1,0:T(8,128)(2,1)}, bf16[256,7...) custom-call(bf16[256,2048]{1,0:T(8,128)(2,1)} %copy-done.4, ...), custom_call_target="tpu_custom_call" | custom-call | flops 1 | bytes 1 | tf_op jit(solution)/shard_map/ffn/pallas_call | solution.py:724
  334.4 17.8 %ffn.6 = (bf16[256,2048]{1,0:T(8,128)(2,1)}, bf16[256,2048]{1,0:T(8,128)(2,1)}, bf16[256,2048]{1,0:T(8,128)(2,1)}, bf16[256,2048]{1,0:T(8,128)(2,1)}, bf16[256,7...) custom-call(bf16[256,2048]{1,0:T(8,128)(2,1)} %join.6.refs_0_.refs_6_, ...), custom_call_target="tpu_custom_call" | custom-call | flops 1 | bytes 1 | tf_op jit(solution)/shard_map/ffn/pallas_call | solution.py:724
  360.4 17.5 %ffn.7 = (bf16[256,2048]{1,0:T(8,128)(2,1)}, bf16[256,2048]{1,0:T(8,128)(2,1)}, bf16[256,2048]{1,0:T(8,128)(2,1)}, bf16[256,2048]{1,0:T(8,128)(2,1)}, bf16[256,7...) custom-call(bf16[256,2048]{1,0:T(8,128)(2,1)} %copy-done.3, ...), custom_call_target="tpu_custom_call" | custom-call | flops 1 | bytes 1 | tf_op jit(solution)/shard_map/ffn/pallas_call | solution.py:724
  379.6 10.8 %outer.3 = bf16[704,2048]{1,0:T(8,128)(2,1)} custom-call(bf16[256,704]{1,0:T(8,128)(2,1)} %get-tuple-element.502.refs_0_, bf16[256,704]{1,0:T(8,128)(2,1)} %get-tuple-element.503.refs_1_, bf16[256,704]{1,0:T(8,128)(2,1)} %get-tuple-element.504.refs_2_, bf16[256,704]{1,0:T(8,128)(2,1)} %get-tuple-element.505.refs_3_, ...), custom_call_target="tpu_custom_call" | custom-call | flops 1 | bytes 1 | tf_op jit(solution)/shard_map/outer/pallas_call | solution.py:764
  391.8 3.9 sums_for_sides.4
  398.2 19.1 %outer.4 = bf16[2048,1408]{1,0:T(8,128)(2,1)} custom-call(bf16[256,2048]{1,0:T(8,128)(2,1)} %get-tuple-element.538.refs_0_, bf16[256,2048]{1,0:T(8,128)(2,1)} %collective-permute-done.27.refs_1_, bf16[256,2048]{1,0:T(8,128)(2,1)} %copy-done.4, bf16[256,2048]{1,0:T(8,128)(2,1)} %copy-done.12, bf16[256,2048]{1,0:T(8,128)(2,1)} %copy-done.3, ...), custom_call_target="tpu_custom_call" | custom-call | flops 1 | bytes 1 | tf_op jit(solution)/shard_map/outer/pallas_call | solution.py:764
  423.1 5.6 back_through_norm.2
  428.7 7.2 %back_to_heads.1 = bf16[8,256,256]{2,1,0:T(8,128)(2,1)} custom-call(s32[1]{0:T(128)} %bitcast.me_ref.me, bf16[256,2048]{1,0:T(8,128)(2,1)} %get-tuple-element.570.grad, bf16[256,2048]{1,0:T(8,128)(2,1)} %bitcast.52, bf16[256,2048]{1,0:T(8,128)(2,1)} %collective-permute-done.19.refs_1_, bf16[256,2048]{1,0:T(8,128)(2,1)} %copy-done.8, ...), custom_call_target="tpu_custom_call" | custom-call | flops 1 | bytes 1 | tf_op jit(solution)/shard_map/back_to_heads/pallas_call | solution.py:427
  438.4 5.8 out_products.1
  444.3 17.8 %all_to_all.31 = bf16[8,256,256]{2,1,0:T(8,128)(2,1)} all-to-all(bf16[8,256,256]{2,1,0:T(8,128)(2,1)S(1)} %copy-done.21), channel_id=1, replica_groups=mesh['dp'=4,'seq'=8] {'seq'}, dimensions={0} | all-to-all | bytes 2097152 | tf_op jit(solution)/shard_map/all_to_all | solution.py:95
  463.7 4.4 sums_for_sides.5
  473.6 28.6 %attend_back.1 = (bf16[2,128,384]{2,1,0:T(8,128)(2,1)}, bf16[2,128,384]{2,1,0:T(8,128)(2,1)}, bf16[2,128,384]{2,1,0:T(8,128)(2,1)}, bf16[2,128,384]{2,1,0:T(8,12...) custom-call(s32[1]{0:T(128)} %bitcast.me_ref.me, ...), custom_call_target="tpu_custom_call" | custom-call | flops 1 | bytes 1 | tf_op jit(solution)/shard_map/attend_back/pallas_call | solution.py:1042
  506.3 3.9 multiply.4
  512.7 3.7 sums_for_sides.6
  516.5 8.8 %outer.5 = bf16[2048,384]{1,0:T(8,128)(2,1)} custom-call(bf16[256,2048]{1,0:T(8,128)(2,1)} %get-tuple-element.652.refs_0_, bf16[256,2048]{1,0:T(8,128)(2,1)} %get-tuple-element.653.refs_1_, bf16[256,2048]{1,0:T(8,128)(2,1)} %get-tuple-element.654.refs_2_, bf16[256,2048]{1,0:T(8,128)(2,1)} %get-tuple-element.655.refs_3_, ...), custom_call_target="tpu_custom_call" | custom-call | flops 1 | bytes 1 | tf_op jit(solution)/shard_map/outer/pallas_call | solution.py:764
  534.5 3.9 multiply.5
  538.4 3.9 multiply.6
  542.4 4.0 multiply.7
  546.3 5.3 collective-permute-done.63.refs_4_
  557.7 3.7 sums_for_sides.7
  563.2 31.7 %all-to-all-done.4.parts = bf16[32,64,384]{2,1,0:T(8,128)(2,1)S(1)} async-done(((bf16[32,64,384]{2,1,0:T(8,128)(2,1)}), bf16[32,64,384]{2,1,0:T(8,128)(2,1)S(1)}, u32[]{:S(2)}, u32[]{:S(2)}) %all-to-all-start.4) | async-done | bytes 1572896 | tf_op jit(solution)/shard_map/all_to_all | solution.py:99
  594.9 4.0 all-to-all-start.5
  608.2 5.1 back_through_norm.3
  614.7 10.0 %collective-permute-done.73.refs_2_ = bf16[64,2048]{1,0:T(8,128)(2,1)S(1)} collective-permute-done((bf16[64,2048]{1,0:T(8,128)(2,1)}, bf16[64,2048]{1,0:T(8,128)(2,1)S(1)}, u32[]{:S(2)}, u32[]{:S(2)}) %collective-permute-start.73) | collective-permute-done | bytes 262176 | tf_op jit(solution)/shard_map/ppermute | solution.py:112
  627.5 5.2 collective-permute-start.75
  634.0 4.0 end_output.1
  638.0 15.3 %collective-permute-done.75 = bf16[64,2048]{1,0:T(8,128)(2,1)S(1)} collective-permute-done((bf16[64,2048]{1,0:T(8,128)(2,1)}, bf16[64,2048]{1,0:T(8,128)(2,1)S(1)}, u32[]{:S(2)}, u32[]{:S(2)}) %collective-permute-start.75) | collective-permute-done | bytes 262176 | tf_op jit(solution)/shard_map/ppermute | solution.py:107
  659.1 3.8 unpack_units.1
  (334 shorter events, 160.2 us)
Async XLA Ops:
  10.6 45.8 %all-to-all-start = ((bf16[8,64,1408]{2,1,0:T(8,128)(2,1)}), bf16[8,64,1408]{2,1,0:T(8,128)(2,1)S(1)}, u32[]{:S(2)}, u32[]{:S(2)}) async-start(bf16[8,64,1408]{2,1,0:T(8,128)(2,1)} %pack_units.1), calls=%async_computation | async-start | bytes 2883584 | tf_op jit(solution)/shard_map/all_to_all | solution.py:95
  16.0 37.6 %collective-permute-start.2 = (bf16[256,2048]{1,0:T(8,128)(2,1)S(1)}, bf16[256,2048]{1,0:T(8,128)(2,1)S(1)}, u32[]{:S(2)}, u32[]{:S(2)}) collective-permute-start(bf16[256,2048]{1,0:T(8,128)(2,1)S(1)} %bitcast.45), channel_id=1, source_target_pairs={{0,1},{1,0},{2,3},{3,2},{4,5},{5,4},{6,7},{7,6},{8,9},{9,8},{10,11... | collective-permute-start | bytes 3145736 | tf_op jit(solution)/shard_map/ppermute | solution.py:30
  16.1 40.3 %collective-permute-start.1 = (bf16[256,2048]{1,0:T(8,128)(2,1)S(1)}, bf16[256,2048]{1,0:T(8,128)(2,1)S(1)}, u32[]{:S(2)}, u32[]{:S(2)}) collective-permute-start(bf16[256,2048]{1,0:T(8,128)(2,1)S(1)} %bitcast.46), channel_id=1, source_target_pairs={{0,4},{1,5},{2,6},{3,7},{4,0},{5,1},{6,2},{7,3},{8,12},{9,13},{10,... | collective-permute-start | bytes 3145736 | tf_op jit(solution)/shard_map/ppermute | solution.py:30
  17.7 38.7 %collective-permute-start = (bf16[256,2048]{1,0:T(8,128)(2,1)S(1)}, bf16[256,2048]{1,0:T(8,128)(2,1)}, u32[]{:S(2)}, u32[]{:S(2)}) collective-permute-start(bf16[256,2048]{1,0:T(8,128)(2,1)S(1)} %bitcast.47), channel_id=1, source_target_pairs={{0,2},{1,3},{2,0},{3,1},{4,6},{5,7},{6,4},{7,5},{8,10},{9,11},{10,... | collective-permute-start | bytes 3145736 | tf_op jit(solution)/shard_map/ppermute | solution.py:30
  22.2 31.3 %collective-permute-start.4 = (bf16[176,2048]{1,0:T(8,128)(2,1)}, bf16[176,2048]{1,0:T(8,128)(2,1)S(1)}, u32[]{:S(2)}, u32[]{:S(2)}) collective-permute-start(bf16[176,2048]{1,0:T(8,128)(2,1)} %refs_1_), channel_id=1, source_target_pairs={{0,8},{8,16},{16,24},{24,0},{1,9},{9,17},{17,25},{25,1},{2,10},{10... | collective-permute-start | bytes 2162696 | tf_op jit(solution)/shard_map/ppermute | solution.py:112
  57.6 60.0 %all-to-all-start.1 = ((bf16[32,208,128]{2,1,0:T(8,128)(2,1)}), bf16[32,208,128]{2,1,0:T(8,128)(2,1)}, u32[]{:S(2)}, u32[]{:S(2)}) async-start(bf16[32,208,128]{2,1,0:T(8,128)(2,1)} %pack_projections.1), calls=%async_computation.1 | async-start | bytes 3407872 | tf_op jit(solution)/shard_map/all_to_all | solution.py:99
  63.1 210.1 %all-gather.2.cloned.1.call-start = ((), (), s32[]{:S(2)}) async-start(), calls=%async_computation.8 | async-start | bytes 7208960 | tf_op jit(solution)/shard_map/all_gather | solution.py:1132
  63.1 52.5 %collective-permute-start.5 = (bf16[256,2048]{1,0:T(8,128)(2,1)}, bf16[256,2048]{1,0:T(8,128)(2,1)S(1)}, u32[]{:S(2)}, u32[]{:S(2)}) collective-permute-start(bf16[256,2048]{1,0:T(8,128)(2,1)} %collective-permute-done.refs_1_.refs_0_), channel_id=1, source_target_pairs={{0,1},{1,0},{2,3},{3,2},{4,5},{5,4},{6,7},{7,6},{8,9},{9,8},{10,11... | collective-permute-start | bytes 3145736 | tf_op jit(solution)/shard_map/ppermute | solution.py:30
  65.6 27.0 %collective-permute-start.7 = (bf16[128,2048]{1,0:T(8,128)(2,1)}, bf16[128,2048]{1,0:T(8,128)(2,1)S(1)}, u32[]{:S(2)}, u32[]{:S(2)}) collective-permute-start(bf16[128,2048]{1,0:T(8,128)(2,1)} %get-tuple-element.369), channel_id=1, source_target_pairs={{0,2},{1,3},{2,0},{3,1},{4,6},{5,7},{6,4},{7,5},{8,10},{9,11},{10,... | collective-permute-start | bytes 1572872 | tf_op jit(solution)/shard_map/ppermute | solution.py:30
  67.1 25.5 %collective-permute-start.8 = (bf16[128,2048]{1,0:T(8,128)(2,1)}, bf16[128,2048]{1,0:T(8,128)(2,1)S(1)}, u32[]{:S(2)}, u32[]{:S(2)}) collective-permute-start(bf16[128,2048]{1,0:T(8,128)(2,1)} %get-tuple-element.370), channel_id=1, source_target_pairs={{0,4},{1,5},{2,6},{3,7},{4,0},{5,1},{6,2},{7,3},{8,12},{9,13},{10,... | collective-permute-start | bytes 1572872 | tf_op jit(solution)/shard_map/ppermute | solution.py:30
  68.3 48.3 %collective-permute-start.6 = (bf16[256,2048]{1,0:T(8,128)(2,1)}, bf16[256,2048]{1,0:T(8,128)(2,1)S(1)}, u32[]{:S(2)}, u32[]{:S(2)}) collective-permute-start(bf16[256,2048]{1,0:T(8,128)(2,1)} %copy-done.17), channel_id=1, source_target_pairs={{0,1},{1,0},{2,3},{3,2},{4,5},{5,4},{6,7},{7,6},{8,9},{9,8},{10,11... | collective-permute-start | bytes 3145736 | tf_op jit(solution)/shard_map/ppermute | solution.py:30
  104.8 42.3 %collective-permute-start.15 = (bf16[256,2048]{1,0:T(8,128)(2,1)S(1)}, bf16[256,2048]{1,0:T(8,128)(2,1)S(1)}, u32[]{:S(2)}, u32[]{:S(2)}) collective-permute-start(bf16[256,2048]{1,0:T(8,128)(2,1)S(1)} %bitcast.40), channel_id=1, source_target_pairs={{0,4},{1,5},{2,6},{3,7},{4,0},{5,1},{6,2},{7,3},{8,12},{9,13},{10,... | collective-permute-start | bytes 3145736 | tf_op jit(solution)/shard_map/ppermute | solution.py:30
  115.6 31.4 %collective-permute-start.14 = (bf16[256,2048]{1,0:T(8,128)(2,1)S(1)}, bf16[256,2048]{1,0:T(8,128)(2,1)S(1)}, u32[]{:S(2)}, u32[]{:S(2)}) collective-permute-start(bf16[256,2048]{1,0:T(8,128)(2,1)S(1)} %bitcast.41), channel_id=1, source_target_pairs={{0,2},{1,3},{2,0},{3,1},{4,6},{5,7},{6,4},{7,5},{8,10},{9,11},{10,... | collective-permute-start | bytes 3145736 | tf_op jit(solution)/shard_map/ppermute | solution.py:30
  117.6 29.4 %collective-permute-start.13 = (bf16[64,2048]{1,0:T(8,128)(2,1)S(1)}, bf16[64,2048]{1,0:T(8,128)(2,1)}, u32[]{:S(2)}, u32[]{:S(2)}) collective-permute-start(bf16[64,2048]{1,0:T(8,128)(2,1)S(1)} %collective-permute-done.10.refs_1_), channel_id=1, source_target_pairs={{0,8},{8,16},{16,24},{24,0},{1,9},{9,17},{17,25},{25,1},{2,10},{10... | collective-permute-start | bytes 786440 | tf_op jit(solution)/shard_map/ppermute | solution.py:112
  117.6 29.4 %collective-permute-start.12 = (bf16[64,2048]{1,0:T(8,128)(2,1)S(1)}, bf16[64,2048]{1,0:T(8,128)(2,1)}, u32[]{:S(2)}, u32[]{:S(2)}) collective-permute-start(bf16[64,2048]{1,0:T(8,128)(2,1)S(1)} %collective-permute-done.10.refs_1_), channel_id=1, source_target_pairs={{0,16},{8,24},{16,0},{24,8},{1,17},{9,25},{17,1},{25,9},{2,18},{10... | collective-permute-start | bytes 786440 | tf_op jit(solution)/shard_map/ppermute | solution.py:112
  119.3 27.8 %collective-permute-start.11 = (bf16[64,2048]{1,0:T(8,128)(2,1)S(1)}, bf16[64,2048]{1,0:T(8,128)(2,1)}, u32[]{:S(2)}, u32[]{:S(2)}) collective-permute-start(bf16[64,2048]{1,0:T(8,128)(2,1)S(1)} %collective-permute-done.10.refs_1_), channel_id=1, source_target_pairs={{0,24},{8,0},{16,8},{24,16},{1,25},{9,1},{17,9},{25,17},{2,26},{10... | collective-permute-start | bytes 786440 | tf_op jit(solution)/shard_map/ppermute | solution.py:112
  147.1 315.0 %reduce-scatter.3.cloned.1.call-start = ((), (), s32[]{:S(2)}) async-start(), calls=%async_computation.9 | async-start | bytes 3604480 | tf_op jit(solution)/shard_map/reduce_scatter | solution.py:1183
  149.8 26.2 %collective-permute-start.19 = (bf16[256,2048]{1,0:T(8,128)(2,1)}, bf16[256,2048]{1,0:T(8,128)(2,1)}, u32[]{:S(2)}, u32[]{:S(2)}) collective-permute-start(bf16[256,2048]{1,0:T(8,128)(2,1)} %bitcast.48), channel_id=1, source_target_pairs={{0,1},{1,0},{2,3},{3,2},{4,5},{5,4},{6,7},{7,6},{8,9},{9,8},{10,11... | collective-permute-start | bytes 3145736 | tf_op jit(solution)/shard_map/ppermute | solution.py:30
  151.3 25.1 %collective-permute-start.18 = (bf16[256,2048]{1,0:T(8,128)(2,1)}, bf16[256,2048]{1,0:T(8,128)(2,1)S(1)}, u32[]{:S(2)}, u32[]{:S(2)}) collective-permute-start(bf16[256,2048]{1,0:T(8,128)(2,1)} %bitcast.49), channel_id=1, source_target_pairs={{0,4},{1,5},{2,6},{3,7},{4,0},{5,1},{6,2},{7,3},{8,12},{9,13},{10,... | collective-permute-start | bytes 3145736 | tf_op jit(solution)/shard_map/ppermute | solution.py:30
  151.3 25.1 %collective-permute-start.17 = (bf16[256,2048]{1,0:T(8,128)(2,1)}, bf16[256,2048]{1,0:T(8,128)(2,1)S(1)}, u32[]{:S(2)}, u32[]{:S(2)}) collective-permute-start(bf16[256,2048]{1,0:T(8,128)(2,1)} %bitcast.50), channel_id=1, source_target_pairs={{0,2},{1,3},{2,0},{3,1},{4,6},{5,7},{6,4},{7,5},{8,10},{9,11},{10,... | collective-permute-start | bytes 3145736 | tf_op jit(solution)/shard_map/ppermute | solution.py:30
  181.5 33.8 %collective-permute-start.20 = (bf16[256,2048]{1,0:T(8,128)(2,1)}, bf16[256,2048]{1,0:T(8,128)(2,1)S(1)}, u32[]{:S(2)}, u32[]{:S(2)}) collective-permute-start(bf16[256,2048]{1,0:T(8,128)(2,1)} %copy-done.8), channel_id=1, source_target_pairs={{0,1},{1,0},{2,3},{3,2},{4,5},{5,4},{6,7},{7,6},{8,9},{9,8},{10,11... | collective-permute-start | bytes 3145736 | tf_op jit(solution)/shard_map/ppermute | solution.py:30
  183.0 32.3 %collective-permute-start.21 = (bf16[256,2048]{1,0:T(8,128)(2,1)}, bf16[256,2048]{1,0:T(8,128)(2,1)S(1)}, u32[]{:S(2)}, u32[]{:S(2)}) collective-permute-start(bf16[256,2048]{1,0:T(8,128)(2,1)} %copy-done.7), channel_id=1, source_target_pairs={{0,1},{1,0},{2,3},{3,2},{4,5},{5,4},{6,7},{7,6},{8,9},{9,8},{10,11... | collective-permute-start | bytes 3145736 | tf_op jit(solution)/shard_map/ppermute | solution.py:30
  226.0 47.1 %collective-permute-start.27 = (bf16[256,2048]{1,0:T(8,128)(2,1)}, bf16[256,2048]{1,0:T(8,128)(2,1)}, u32[]{:S(2)}, u32[]{:S(2)}) collective-permute-start(bf16[256,2048]{1,0:T(8,128)(2,1)} %get-tuple-element.538.refs_0_), channel_id=1, source_target_pairs={{0,1},{1,0},{2,3},{3,2},{4,5},{5,4},{6,7},{7,6},{8,9},{9,8},{10,11... | collective-permute-start | bytes 3145736 | tf_op jit(solution)/shard_map/ppermute | solution.py:30
  227.4 63.1 %collective-permute-start.26 = (bf16[256,2048]{1,0:T(8,128)(2,1)}, bf16[256,2048]{1,0:T(8,128)(2,1)S(1)}, u32[]{:S(2)}, u32[]{:S(2)}) collective-permute-start(bf16[256,2048]{1,0:T(8,128)(2,1)} %get-tuple-element.538.refs_0_), channel_id=1, source_target_pairs={{0,4},{1,5},{2,6},{3,7},{4,0},{5,1},{6,2},{7,3},{8,12},{9,13},{10,... | collective-permute-start | bytes 3145736 | tf_op jit(solution)/shard_map/ppermute | solution.py:30
  227.7 62.8 %collective-permute-start.25 = (bf16[256,2048]{1,0:T(8,128)(2,1)}, bf16[256,2048]{1,0:T(8,128)(2,1)S(1)}, u32[]{:S(2)}, u32[]{:S(2)}) collective-permute-start(bf16[256,2048]{1,0:T(8,128)(2,1)} %get-tuple-element.538.refs_0_), channel_id=1, source_target_pairs={{0,2},{1,3},{2,0},{3,1},{4,6},{5,7},{6,4},{7,5},{8,10},{9,11},{10,... | collective-permute-start | bytes 3145736 | tf_op jit(solution)/shard_map/ppermute | solution.py:30
  229.9 29.0 %collective-permute-start.28 = (bf16[176,1024]{1,0:T(8,128)(2,1)}, bf16[176,1024]{1,0:T(8,128)(2,1)S(1)}, u32[]{:S(2)}, u32[]{:S(2)}) collective-permute-start(bf16[176,1024]{1,0:T(8,128)(2,1)} %get-tuple-element.453), channel_id=1, source_target_pairs={{0,24},{8,0},{16,8},{24,16},{1,25},{9,1},{17,9},{25,17},{2,26},{10... | collective-permute-start | bytes 1081352 | tf_op jit(solution)/shard_map/ppermute | solution.py:112
  230.8 34.0 %collective-permute-start.29 = (bf16[176,1024]{1,0:T(8,128)(2,1)}, bf16[176,1024]{1,0:T(8,128)(2,1)S(1)}, u32[]{:S(2)}, u32[]{:S(2)}) collective-permute-start(bf16[176,1024]{1,0:T(8,128)(2,1)} %get-tuple-element.454), channel_id=1, source_target_pairs={{0,8},{8,16},{16,24},{24,0},{1,9},{9,17},{17,25},{25,1},{2,10},{10... | collective-permute-start | bytes 1081352 | tf_op jit(solution)/shard_map/ppermute | solution.py:112
  268.4 39.1 %collective-permute-start.34 = (bf16[256,2048]{1,0:T(8,128)(2,1)S(1)}, bf16[256,2048]{1,0:T(8,128)(2,1)}, u32[]{:S(2)}, u32[]{:S(2)}) collective-permute-start(bf16[256,2048]{1,0:T(8,128)(2,1)S(1)} %collective-permute-done.14.refs_2_.refs_1_.refs_10_), channel_id=1, source_target_pairs={{0,1},{1,0},{2,3},{3,2},{4,5},{5,4},{6,7},{7,6},{8,9},{9,8},{10,11... | collective-permute-start | bytes 3145736 | tf_op jit(solution)/shard_map/ppermute | solution.py:30
  292.1 35.3 %collective-permute-start.33 = (bf16[256,2048]{1,0:T(8,128)(2,1)S(1)}, bf16[256,2048]{1,0:T(8,128)(2,1)S(1)}, u32[]{:S(2)}, u32[]{:S(2)}) collective-permute-start(bf16[256,2048]{1,0:T(8,128)(2,1)S(1)} %collective-permute-done.26.refs_0_.refs_4_), channel_id=1, source_target_pairs={{0,1},{1,0},{2,3},{3,2},{4,5},{5,4},{6,7},{7,6},{8,9},{9,8},{10,11... | collective-permute-start | bytes 3145736 | tf_op jit(solution)/shard_map/ppermute | solution.py:30
  294.7 32.7 %collective-permute-start.30 = (bf16[128,2048]{1,0:T(8,128)(2,1)}, bf16[128,2048]{1,0:T(8,128)(2,1)S(1)}, u32[]{:S(2)}, u32[]{:S(2)}) collective-permute-start(bf16[128,2048]{1,0:T(8,128)(2,1)} %get-tuple-element.459), channel_id=1, source_target_pairs={{0,2},{1,3},{2,0},{3,1},{4,6},{5,7},{6,4},{7,5},{8,10},{9,11},{10,... | collective-permute-start | bytes 1572872 | tf_op jit(solution)/shard_map/ppermute | solution.py:30
  390.5 204.4 %reduce-scatter.5.cloned.1.call-start = ((), (), s32[]{:S(2)}) async-start(), calls=%async_computation.10 | async-start | bytes 7208960 | tf_op jit(solution)/shard_map/reduce_scatter | solution.py:1204
  396.1 24.9 %collective-permute-start.46 = (bf16[256,2048]{1,0:T(8,128)(2,1)}, bf16[256,2048]{1,0:T(8,128)(2,1)S(1)}, u32[]{:S(2)}, u32[]{:S(2)}) collective-permute-start(bf16[256,2048]{1,0:T(8,128)(2,1)} %get-tuple-element.536), channel_id=1, source_target_pairs={{0,2},{1,3},{2,0},{3,1},{4,6},{5,7},{6,4},{7,5},{8,10},{9,11},{10,... | collective-permute-start | bytes 3145736 | tf_op jit(solution)/shard_map/ppermute | solution.py:30
  397.2 24.6 %collective-permute-start.47 = (bf16[256,2048]{1,0:T(8,128)(2,1)}, bf16[256,2048]{1,0:T(8,128)(2,1)}, u32[]{:S(2)}, u32[]{:S(2)}) collective-permute-start(bf16[256,2048]{1,0:T(8,128)(2,1)} %get-tuple-element.537), channel_id=1, source_target_pairs={{0,4},{1,5},{2,6},{3,7},{4,0},{5,1},{6,2},{7,3},{8,12},{9,13},{10,... | collective-permute-start | bytes 3145736 | tf_op jit(solution)/shard_map/ppermute | solution.py:30
  435.9 26.1 %collective-permute-start.52 = (bf16[256,2048]{1,0:T(8,128)(2,1)S(1)}, bf16[256,2048]{1,0:T(8,128)(2,1)}, u32[]{:S(2)}, u32[]{:S(2)}) collective-permute-start(bf16[256,2048]{1,0:T(8,128)(2,1)S(1)} %copy-done.67), channel_id=1, source_target_pairs={{0,1},{1,0},{2,3},{3,2},{4,5},{5,4},{6,7},{7,6},{8,9},{9,8},{10,11... | collective-permute-start | bytes 3145736 | tf_op jit(solution)/shard_map/ppermute | solution.py:30
  437.9 24.2 %collective-permute-start.53 = (bf16[256,2048]{1,0:T(8,128)(2,1)S(1)}, bf16[256,2048]{1,0:T(8,128)(2,1)S(1)}, u32[]{:S(2)}, u32[]{:S(2)}) collective-permute-start(bf16[256,2048]{1,0:T(8,128)(2,1)S(1)} %copy-done.68), channel_id=1, source_target_pairs={{0,1},{1,0},{2,3},{3,2},{4,5},{5,4},{6,7},{7,6},{8,9},{9,8},{10,11... | collective-permute-start | bytes 3145736 | tf_op jit(solution)/shard_map/ppermute | solution.py:30
  438.0 24.1 %collective-permute-start.54 = (bf16[256,2048]{1,0:T(8,128)(2,1)}, bf16[256,2048]{1,0:T(8,128)(2,1)S(1)}, u32[]{:S(2)}, u32[]{:S(2)}) collective-permute-start(bf16[256,2048]{1,0:T(8,128)(2,1)} %get-tuple-element.583), channel_id=1, source_target_pairs={{0,1},{1,0},{2,3},{3,2},{4,5},{5,4},{6,7},{7,6},{8,9},{9,8},{10,11... | collective-permute-start | bytes 3145736 | tf_op jit(solution)/shard_map/ppermute | solution.py:30
  468.1 35.7 %collective-permute-start.57 = (bf16[256,2048]{1,0:T(8,128)(2,1)}, bf16[256,2048]{1,0:T(8,128)(2,1)S(1)}, u32[]{:S(2)}, u32[]{:S(2)}) collective-permute-start(bf16[256,2048]{1,0:T(8,128)(2,1)} %get-tuple-element.611), channel_id=1, source_target_pairs={{0,2},{1,3},{2,0},{3,1},{4,6},{5,7},{6,4},{7,5},{8,10},{9,11},{10,... | collective-permute-start | bytes 3145736 | tf_op jit(solution)/shard_map/ppermute | solution.py:30
  468.7 35.0 %collective-permute-start.58 = (bf16[256,2048]{1,0:T(8,128)(2,1)}, bf16[256,2048]{1,0:T(8,128)(2,1)S(1)}, u32[]{:S(2)}, u32[]{:S(2)}) collective-permute-start(bf16[256,2048]{1,0:T(8,128)(2,1)} %get-tuple-element.612), channel_id=1, source_target_pairs={{0,4},{1,5},{2,6},{3,7},{4,0},{5,1},{6,2},{7,3},{8,12},{9,13},{10,... | collective-permute-start | bytes 3145736 | tf_op jit(solution)/shard_map/ppermute | solution.py:30
  471.3 31.3 %collective-permute-start.55 = (bf16[128,2048]{1,0:T(8,128)(2,1)}, bf16[128,2048]{1,0:T(8,128)(2,1)S(1)}, u32[]{:S(2)}, u32[]{:S(2)}) collective-permute-start(bf16[128,2048]{1,0:T(8,128)(2,1)} %get-tuple-element.601), channel_id=1, source_target_pairs={{0,2},{1,3},{2,0},{3,1},{4,6},{5,7},{6,4},{7,5},{8,10},{9,11},{10,... | collective-permute-start | bytes 1572872 | tf_op jit(solution)/shard_map/ppermute | solution.py:30
  472.1 31.6 %collective-permute-start.56 = (bf16[128,2048]{1,0:T(8,128)(2,1)}, bf16[128,2048]{1,0:T(8,128)(2,1)S(1)}, u32[]{:S(2)}, u32[]{:S(2)}) collective-permute-start(bf16[128,2048]{1,0:T(8,128)(2,1)} %get-tuple-element.602), channel_id=1, source_target_pairs={{0,4},{1,5},{2,6},{3,7},{4,0},{5,1},{6,2},{7,3},{8,12},{9,13},{10,... | collective-permute-start | bytes 1572872 | tf_op jit(solution)/shard_map/ppermute | solution.py:30
  526.3 68.6 %all-to-all-start.4 = ((bf16[32,64,384]{2,1,0:T(8,128)(2,1)}), bf16[32,64,384]{2,1,0:T(8,128)(2,1)S(1)}, u32[]{:S(2)}, u32[]{:S(2)}) async-start(bf16[32,64,384]{2,1,0:T(8,128)(2,1)} %bitcast.53), calls=%async_computation.5 | async-start | bytes 3145728 | tf_op jit(solution)/shard_map/all_to_all | solution.py:99
  552.8 46.2 %collective-permute-start.70 = (bf16[256,2048]{1,0:T(8,128)(2,1)}, bf16[256,2048]{1,0:T(8,128)(2,1)}, u32[]{:S(2)}, u32[]{:S(2)}) collective-permute-start(bf16[256,2048]{1,0:T(8,128)(2,1)} %get-tuple-element.698), channel_id=1, source_target_pairs={{0,2},{1,3},{2,0},{3,1},{4,6},{5,7},{6,4},{7,5},{8,10},{9,11},{10,... | collective-permute-start | bytes 3145736 | tf_op jit(solution)/shard_map/ppermute | solution.py:30
  553.2 45.7 %collective-permute-start.71 = (bf16[256,2048]{1,0:T(8,128)(2,1)}, bf16[256,2048]{1,0:T(8,128)(2,1)}, u32[]{:S(2)}, u32[]{:S(2)}) collective-permute-start(bf16[256,2048]{1,0:T(8,128)(2,1)} %get-tuple-element.699), channel_id=1, source_target_pairs={{0,4},{1,5},{2,6},{3,7},{4,0},{5,1},{6,2},{7,3},{8,12},{9,13},{10,... | collective-permute-start | bytes 3145736 | tf_op jit(solution)/shard_map/ppermute | solution.py:30
  554.5 51.6 %collective-permute-start.65 = (bf16[256,2048]{1,0:T(8,128)(2,1)}, bf16[256,2048]{1,0:T(8,128)(2,1)}, u32[]{:S(2)}, u32[]{:S(2)}) collective-permute-start(bf16[256,2048]{1,0:T(8,128)(2,1)} %get-tuple-element.687), channel_id=1, source_target_pairs={{0,1},{1,0},{2,3},{3,2},{4,5},{5,4},{6,7},{7,6},{8,9},{9,8},{10,11... | collective-permute-start | bytes 3145736 | tf_op jit(solution)/shard_map/ppermute | solution.py:30
  561.4 46.5 %collective-permute-start.68 = (bf16[256,2048]{1,0:T(8,128)(2,1)}, bf16[256,2048]{1,0:T(8,128)(2,1)}, u32[]{:S(2)}, u32[]{:S(2)}) collective-permute-start(bf16[256,2048]{1,0:T(8,128)(2,1)} %get-tuple-element.694), channel_id=1, source_target_pairs={{0,2},{1,3},{2,0},{3,1},{4,6},{5,7},{6,4},{7,5},{8,10},{9,11},{10,... | collective-permute-start | bytes 3145736 | tf_op jit(solution)/shard_map/ppermute | solution.py:30
  561.9 46.4 %collective-permute-start.69 = (bf16[256,2048]{1,0:T(8,128)(2,1)}, bf16[256,2048]{1,0:T(8,128)(2,1)}, u32[]{:S(2)}, u32[]{:S(2)}) collective-permute-start(bf16[256,2048]{1,0:T(8,128)(2,1)} %get-tuple-element.695), channel_id=1, source_target_pairs={{0,4},{1,5},{2,6},{3,7},{4,0},{5,1},{6,2},{7,3},{8,12},{9,13},{10,... | collective-permute-start | bytes 3145736 | tf_op jit(solution)/shard_map/ppermute | solution.py:30
  594.9 63.1 %all-to-all-start.5 = ((bf16[8,64,1408]{2,1,0:T(8,128)(2,1)}), bf16[8,64,1408]{2,1,0:T(8,128)(2,1)S(1)}, u32[]{:S(2)}, u32[]{:S(2)}) async-start(bf16[8,64,1408]{2,1,0:T(8,128)(2,1)} %bitcast.58), calls=%async_computation.7 | async-start | bytes 2883584 | tf_op jit(solution)/shard_map/all_to_all | solution.py:95
  627.5 25.7 %collective-permute-start.75 = (bf16[64,2048]{1,0:T(8,128)(2,1)}, bf16[64,2048]{1,0:T(8,128)(2,1)S(1)}, u32[]{:S(2)}, u32[]{:S(2)}) collective-permute-start(bf16[64,2048]{1,0:T(8,128)(2,1)} %add_up.3), channel_id=1, source_target_pairs={{0,0},{8,1},{16,2},{24,3},{1,4},{9,5},{17,6},{25,7},{2,8},{10,9},{... | collective-permute-start | bytes 786440 | tf_op jit(solution)/shard_map/ppermute | solution.py:107
  (111 other events, 1168.7 us)
Sparse Core Ops, SparseCore 0:
  147.2 121.3 all-gather.1
  390.6 53.5 reduce-scatter.2
  462.3 123.0 reduce-scatter.4

commit v3 on v2

--- a/solution.py
+++ b/solution.py
@@ -148,9 +148,8 @@
     return [block] + [shift(block, -d) for d in range(1, size)]
 
 
-def scatter_dp_direct(term):
+def scatter_dp_direct(blocks):
     size = lax.axis_size("dp")
-    blocks = pick(lax.axis_index("dp"), term)
     return [blocks[0]] + [shift(blocks[d], d) for d in range(1, size)]
 
 
@@ -1226,7 +1225,9 @@
     sums = scatter_seq_sums(terms, corner)
     (sums,) = tie(sums)
     out_term = add_up(out_sides, BF16).reshape(n_dp, owned, width)
-    out_parts = scatter_dp_direct(out_term)
+    out_blocks = pick(me_dp, out_term)
+    out_blocks, both_sum = tie(out_blocks, both_sum)
+    out_parts = scatter_dp_direct(out_blocks)
     sides = scatter_seq_sides(terms, corner, sums)
     (grad_input,) = back_through_norm(grad_res, block, sides, gain_one, False)
     grad_input, out_parts = tie(grad_input, out_parts)

time: 676 us -> 666 us (0.985)
  waiting for transfers between devices: 187 us -> 175 us
    all_to_all x2, waiting for transfers between devices: 31.7 us -> 5.16 us  [exchange_all(): return lax.all_to_all(blocks, ('dp', 'seq'), 0, 0, tiled=True)]
    ppermute x64, waiting for transfers between devices: 61.9 us -> 82.6 us  [swap(): return lax.ppermute(block, 'seq', [(i, i ^ distance) for i in range(size)])]
    ppermute x10, waiting for transfers between devices: 73 us -> 64.1 us  [shift(): lax.ppermute(block, 'dp', [(i, (i + step) % size) for i in range(size)])]
    unnamed x152 -> x156, local copies, waits for them, and re-layouts: 23.3 us -> 24.2 us
  transfers between devices with their start and end apart: 83 -> 83, of which waited for: 27 -> 26; matrix products, arithmetic and copies ran while one was open for 1% -> 1% of each run, Pallas kernels for 42% -> 43%
where the time goes in v3:
time: 666 us; the launch traced here: 662 us
  Pallas kernels  309 us (46%)
  waiting for transfers between devices  175 us (26%)
  starting transfers between devices  96.7 us (15%)
  blocking collectives  34.9 us (5%)
  local copies, waits for them, and re-layouts  25.9 us (4%)
  between operations  14.9 us (2%)
    ppermute x64, waiting for transfers between devices, swap(): return lax.ppermute(block, 'seq', [(i, i ^ distance) for i in range(size)])  82.6 us
    pallas_call x4, Pallas kernels, ffn(): pl.pallas_call(functools.partial(ffn_kernel, count), out_shape=shapes, co...  70.2 us
    ppermute x10, waiting for transfers between devices, shift(): lax.ppermute(block, 'dp', [(i, (i + step) % size) for i in range(size)])  64.1 us
    ppermute x64, starting transfers between devices, swap(): return lax.ppermute(block, 'seq', [(i, i ^ distance) for i in range(size)])  58.3 us
    pallas_call x11, Pallas kernels, by_rows(): pl.pallas_call(kernel, out_shape=[jax.ShapeDtypeStruct(shape[:2], shape[2...  40.6 us
    pallas_call x3, Pallas kernels, outer(): pl.pallas_call(functools.partial(outer_kernel, count, along_left), out_sh...  38.7 us
    pallas_call x9, Pallas kernels, local(): pl.pallas_call(kernel, out_shape=[jax.ShapeDtypeStruct(*out) for out in o...  38.6 us
    all_to_all x2, blocking collectives, exchange_seq(): return lax.all_to_all(blocks, 'seq', 0, 0, tiled=True)  34.9 us
  transfers between devices with their start and end apart: 83, of which 26 were waited for; matrix products, arithmetic and copies ran while one was open for 1% of the time, Pallas kernels for 43%

profile of v3, /device:TPU:1, one launch (start us, length us, event | category | flops | bytes accessed | tf_op | source)
XLA Modules:
  0.0 661.5 jit_solution(14332843012505728908)
XLA Ops:
  10.6 5.4 all-to-all-start
  25.3 12.1 %collective-permute-done.3.refs_0_.refs_2_ = bf16[176,2048]{1,0:T(8,128)(2,1)S(1)} collective-permute-done((bf16[176,2048]{1,0:T(8,128)(2,1)}, bf16[176,2048]{1,0:T(8,128)(2,1)S(1)}, u32[]{:S(2)}, u32[]{:S(2)}) %collective-permute-start.3) | collective-permute-done | bytes 720928 | tf_op jit(solution)/shard_map/ppermute | solution.py:112
  37.4 16.2 %collective-permute-done.4.refs_1_.refs_3_ = bf16[176,2048]{1,0:T(8,128)(2,1)S(1)} collective-permute-done((bf16[176,2048]{1,0:T(8,128)(2,1)}, bf16[176,2048]{1,0:T(8,128)(2,1)S(1)}, u32[]{:S(2)}, u32[]{:S(2)}) %collective-permute-start.4) | collective-permute-done | bytes 720928 | tf_op jit(solution)/shard_map/ppermute | solution.py:112
  57.6 5.5 all-to-all-start.1
  69.0 23.6 %collective-permute-done.7.refs_0_ = bf16[128,2048]{1,0:T(8,128)(2,1)S(1)} collective-permute-done((bf16[128,2048]{1,0:T(8,128)(2,1)}, bf16[128,2048]{1,0:T(8,128)(2,1)S(1)}, u32[]{:S(2)}, u32[]{:S(2)}) %collective-permute-start.7) | collective-permute-done | bytes 524320 | tf_op jit(solution)/shard_map/ppermute | solution.py:30
  100.2 4.6 collective-permute-done.10.refs_1_
  104.8 10.9 %collective-permute-start.15 = (bf16[256,2048]{1,0:T(8,128)(2,1)S(1)}, bf16[256,2048]{1,0:T(8,128)(2,1)S(1)}, u32[]{:S(2)}, u32[]{:S(2)}) collective-permute-start(bf16[256,2048]{1,0:T(8,128)(2,1)S(1)} %bitcast.40), channel_id=1, source_target_pairs={{0,4},{1,5},{2,6},{3,7},{4,0},{5,1},{6,2},{7,3},{8,12},{9,13},{10,... | collective-permute-start | bytes 3145736 | tf_op jit(solution)/shard_map/ppermute | solution.py:30
  121.1 7.7 %unpack_projections.1 = (bf16[2048,384]{1,0:T(8,128)(2,1)}, f32[1,2048]{1,0:T(1,128)}, f32[1,2048]{1,0:T(1,128)}, f32[2,1024,128]{2,1,0:T(8,128)}, f32[2,1024,128]{2,1,0:T(8,128)}, /*index=5*/s32[2,1,1024]{2,1,0:T(1,128)}) custom-call(s32[1]{0:T(128)} %bitcast.4.me.refs_0_, bf16[32,208,128]{2,1,0:T(8,128)(2,1)} %all-to-all-done.1.packed), custom_call_target="tpu_custom_call" | custom-call | flops 1 | bytes 1 | tf_op jit(solution)/shard_map/unpack_projections/pallas_call | solution.py:426
  128.8 4.6 enter.7
  133.5 4.6 enter.6
  138.0 4.6 enter.5
  142.7 4.5 enter.4
  152.2 24.0 %attend.1 = (bf16[8,2,128,256]{3,2,1,0:T(8,128)(2,1)}, bf16[2,1024,256]{2,1,0:T(8,128)(2,1)}, bf16[2,2,1024,128]{3,2,1,0:T(8,128)(2,1)}, bf16[2,1024,128]{2,1,0:T(8,128)(2,1)}, f32[2,4,1,1024]{3,2,1,0:T(1,128)}) custom-call(s32[1]{0:T(128)} %bitcast.me_ref.me, f32[2,128,384]{2,1,0:T(8,128)} %bitcast.83, f32[2,128,384]{2,1,0:T(8,128)} %bitcast.84, ...), custom_call_target="tpu_custom_call" | custom-call | flops 1 | bytes 1 | tf_op jit(solution)/shard_map/attend/pallas_call | solution.py:1008
  183.2 9.8 %collective-permute-done.22.refs_0_ = bf16[128,2048]{1,0:T(8,128)(2,1)S(1)} collective-permute-done((bf16[128,2048]{1,0:T(8,128)(2,1)}, bf16[128,2048]{1,0:T(8,128)(2,1)S(1)}, u32[]{:S(2)}, u32[]{:S(2)}) %collective-permute-start.22) | collective-permute-done | bytes 524320 | tf_op jit(solution)/shard_map/ppermute | solution.py:30
  198.2 17.2 %all_to_all.30.mixed = bf16[8,256,256]{2,1,0:T(8,128)(2,1)} all-to-all(bf16[8,256,256]{2,1,0:T(8,128)(2,1)S(1)} %bitcast.60), channel_id=1, replica_groups=mesh['dp'=4,'seq'=8] {'seq'}, dimensions={0} | all-to-all | bytes 2097152 | tf_op jit(solution)/shard_map/all_to_all | solution.py:95
  217.1 9.1 %end_attention.1 = (f32[256,2048]{1,0:T(8,128)}, bf16[256,2048]{1,0:T(8,128)(2,1)}) custom-call(s32[1]{0:T(128)} %bitcast.me_ref.me, bf16[256,2048]{1,0:T(8,128)(2,1)} %bitcast.43, bf16[8,256,256]{2,1,0:T(8,128)(2,1)} %all_to_all.30.mixed, f32[1,2048]{1,0:T(1,128)} %get-tuple-element.437.gain.refs_6_, bf16[256,2048]{1,0:T(8,128)(2,1)} %bitcast.51, ...), custom_call_target="tpu_custom_call" | custom-call | flops 1 | bytes 1 | tf_op jit(solution)/shard_map/end_attention/pallas_call | solution.py:361
  231.6 27.3 %collective-permute-done.28.refs_4_ = bf16[176,1024]{1,0:T(8,128)(2,1)S(1)} collective-permute-done((bf16[176,1024]{1,0:T(8,128)(2,1)}, bf16[176,1024]{1,0:T(8,128)(2,1)S(1)}, u32[]{:S(2)}, u32[]{:S(2)}) %collective-permute-start.28) | collective-permute-done | bytes 360480 | tf_op jit(solution)/shard_map/ppermute | solution.py:112
  259.0 6.0 collective-permute-done.29.refs_5_
  273.4 17.5 %ffn.4 = (bf16[256,2048]{1,0:T(8,128)(2,1)}, bf16[256,2048]{1,0:T(8,128)(2,1)}, bf16[256,2048]{1,0:T(8,128)(2,1)}, bf16[256,2048]{1,0:T(8,128)(2,1)}, bf16[256,7...) custom-call(bf16[256,2048]{1,0:T(8,128)(2,1)} %get-tuple-element.543.refs_0_, ...), custom_call_target="tpu_custom_call" | custom-call | flops 1 | bytes 1 | tf_op jit(solution)/shard_map/ffn/pallas_call | solution.py:723
  295.4 9.2 %collective-permute-done.37.refs_1_ = bf16[128,2048]{1,0:T(8,128)(2,1)S(1)} collective-permute-done((bf16[128,2048]{1,0:T(8,128)(2,1)S(1)}, bf16[128,2048]{1,0:T(8,128)(2,1)S(1)}, u32[]{:S(2)}, u32[]{:S(2)}) %collective-permute-start.37) | collective-permute-done | bytes 524320 | tf_op jit(solution)/shard_map/ppermute | solution.py:30
  310.3 17.5 %ffn.5 = (bf16[256,2048]{1,0:T(8,128)(2,1)}, bf16[256,2048]{1,0:T(8,128)(2,1)}, bf16[256,2048]{1,0:T(8,128)(2,1)}, bf16[256,2048]{1,0:T(8,128)(2,1)}, bf16[256,7...) custom-call(bf16[256,2048]{1,0:T(8,128)(2,1)} %copy-done.4, ...), custom_call_target="tpu_custom_call" | custom-call | flops 1 | bytes 1 | tf_op jit(solution)/shard_map/ffn/pallas_call | solution.py:723
  334.8 17.7 %ffn.6 = (bf16[256,2048]{1,0:T(8,128)(2,1)}, bf16[256,2048]{1,0:T(8,128)(2,1)}, bf16[256,2048]{1,0:T(8,128)(2,1)}, bf16[256,2048]{1,0:T(8,128)(2,1)}, bf16[256,7...) custom-call(bf16[256,2048]{1,0:T(8,128)(2,1)} %join.6.refs_0_.refs_6_, ...), custom_call_target="tpu_custom_call" | custom-call | flops 1 | bytes 1 | tf_op jit(solution)/shard_map/ffn/pallas_call | solution.py:723
  361.0 17.5 %ffn.7 = (bf16[256,2048]{1,0:T(8,128)(2,1)}, bf16[256,2048]{1,0:T(8,128)(2,1)}, bf16[256,2048]{1,0:T(8,128)(2,1)}, bf16[256,2048]{1,0:T(8,128)(2,1)}, bf16[256,7...) custom-call(bf16[256,2048]{1,0:T(8,128)(2,1)} %copy-done.3, ...), custom_call_target="tpu_custom_call" | custom-call | flops 1 | bytes 1 | tf_op jit(solution)/shard_map/ffn/pallas_call | solution.py:723
  380.2 10.8 %outer.3 = bf16[704,2048]{1,0:T(8,128)(2,1)} custom-call(bf16[256,704]{1,0:T(8,128)(2,1)} %get-tuple-element.507.refs_0_, bf16[256,704]{1,0:T(8,128)(2,1)} %get-tuple-element.508.refs_1_, bf16[256,704]{1,0:T(8,128)(2,1)} %get-tuple-element.509.refs_2_, bf16[256,704]{1,0:T(8,128)(2,1)} %get-tuple-element.510.refs_3_, ...), custom_call_target="tpu_custom_call" | custom-call | flops 1 | bytes 1 | tf_op jit(solution)/shard_map/outer/pallas_call | solution.py:763
  392.4 3.9 sums_for_sides.4
  398.6 19.1 %outer.4 = bf16[2048,1408]{1,0:T(8,128)(2,1)} custom-call(bf16[256,2048]{1,0:T(8,128)(2,1)} %get-tuple-element.543.refs_0_, bf16[256,2048]{1,0:T(8,128)(2,1)} %collective-permute-done.27.refs_1_, bf16[256,2048]{1,0:T(8,128)(2,1)} %copy-done.4, bf16[256,2048]{1,0:T(8,128)(2,1)} %copy-done.12, bf16[256,2048]{1,0:T(8,128)(2,1)} %copy-done.3, ...), custom_call_target="tpu_custom_call" | custom-call | flops 1 | bytes 1 | tf_op jit(solution)/shard_map/outer/pallas_call | solution.py:763
  423.6 5.5 back_through_norm.2
  429.1 7.2 %back_to_heads.1 = bf16[8,256,256]{2,1,0:T(8,128)(2,1)} custom-call(s32[1]{0:T(128)} %bitcast.me_ref.me, bf16[256,2048]{1,0:T(8,128)(2,1)} %get-tuple-element.575.grad, bf16[256,2048]{1,0:T(8,128)(2,1)} %bitcast.52, bf16[256,2048]{1,0:T(8,128)(2,1)} %collective-permute-done.19.refs_1_, bf16[256,2048]{1,0:T(8,128)(2,1)} %copy-done.8, ...), custom_call_target="tpu_custom_call" | custom-call | flops 1 | bytes 1 | tf_op jit(solution)/shard_map/back_to_heads/pallas_call | solution.py:426
  438.7 5.8 out_products.1
  444.6 17.8 %all_to_all.31 = bf16[8,256,256]{2,1,0:T(8,128)(2,1)} all-to-all(bf16[8,256,256]{2,1,0:T(8,128)(2,1)S(1)} %copy-done.21), channel_id=1, replica_groups=mesh['dp'=4,'seq'=8] {'seq'}, dimensions={0} | all-to-all | bytes 2097152 | tf_op jit(solution)/shard_map/all_to_all | solution.py:95
  464.1 4.3 sums_for_sides.5
  473.9 28.6 %attend_back.1 = (bf16[2,128,384]{2,1,0:T(8,128)(2,1)}, bf16[2,128,384]{2,1,0:T(8,128)(2,1)}, bf16[2,128,384]{2,1,0:T(8,128)(2,1)}, bf16[2,128,384]{2,1,0:T(8,12...) custom-call(s32[1]{0:T(128)} %bitcast.me_ref.me, ...), custom_call_target="tpu_custom_call" | custom-call | flops 1 | bytes 1 | tf_op jit(solution)/shard_map/attend_back/pallas_call | solution.py:1041
  506.7 3.9 multiply.4
  516.7 8.8 %outer.5 = bf16[2048,384]{1,0:T(8,128)(2,1)} custom-call(bf16[256,2048]{1,0:T(8,128)(2,1)} %get-tuple-element.657.refs_0_, bf16[256,2048]{1,0:T(8,128)(2,1)} %get-tuple-element.658.refs_1_, bf16[256,2048]{1,0:T(8,128)(2,1)} %get-tuple-element.659.refs_2_, bf16[256,2048]{1,0:T(8,128)(2,1)} %get-tuple-element.660.refs_3_, ...), custom_call_target="tpu_custom_call" | custom-call | flops 1 | bytes 1 | tf_op jit(solution)/shard_map/outer/pallas_call | solution.py:763
  533.9 3.9 multiply.5
  537.7 4.0 multiply.6
  541.7 3.9 multiply.7
  545.6 5.7 collective-permute-done.63.refs_4_
  557.4 3.8 sums_for_sides.7
  562.8 19.6 %collective-permute-done.70.refs_2_ = bf16[256,2048]{1,0:T(8,128)(2,1)S(1)} collective-permute-done((bf16[256,2048]{1,0:T(8,128)(2,1)}, bf16[256,2048]{1,0:T(8,128)(2,1)S(1)}, u32[]{:S(2)}, u32[]{:S(2)}) %collective-permute-start.70) | collective-permute-done | bytes 1048608 | tf_op jit(solution)/shard_map/ppermute | solution.py:30
  584.3 3.8 add_up.2
  590.1 5.2 all-to-all-done.4.parts
  595.3 4.0 all-to-all-start.5
  605.0 3.9 end_output.1
  608.9 5.1 back_through_norm.3
  622.5 5.4 collective-permute-start.75
  629.3 18.3 %collective-permute-done.75 = bf16[64,2048]{1,0:T(8,128)(2,1)S(1)} collective-permute-done((bf16[64,2048]{1,0:T(8,128)(2,1)}, bf16[64,2048]{1,0:T(8,128)(2,1)S(1)}, u32[]{:S(2)}, u32[]{:S(2)}) %collective-permute-start.75) | collective-permute-done | bytes 262176 | tf_op jit(solution)/shard_map/ppermute | solution.py:107
  649.6 3.8 unpack_units.1
  (338 shorter events, 163.8 us)
Async XLA Ops:
  10.6 45.8 %all-to-all-start = ((bf16[8,64,1408]{2,1,0:T(8,128)(2,1)}), bf16[8,64,1408]{2,1,0:T(8,128)(2,1)S(1)}, u32[]{:S(2)}, u32[]{:S(2)}) async-start(bf16[8,64,1408]{2,1,0:T(8,128)(2,1)} %pack_units.1), calls=%async_computation | async-start | bytes 2883584 | tf_op jit(solution)/shard_map/all_to_all | solution.py:95
  16.0 37.6 %collective-permute-start.2 = (bf16[256,2048]{1,0:T(8,128)(2,1)S(1)}, bf16[256,2048]{1,0:T(8,128)(2,1)S(1)}, u32[]{:S(2)}, u32[]{:S(2)}) collective-permute-start(bf16[256,2048]{1,0:T(8,128)(2,1)S(1)} %bitcast.45), channel_id=1, source_target_pairs={{0,1},{1,0},{2,3},{3,2},{4,5},{5,4},{6,7},{7,6},{8,9},{9,8},{10,11... | collective-permute-start | bytes 3145736 | tf_op jit(solution)/shard_map/ppermute | solution.py:30
  16.1 40.3 %collective-permute-start.1 = (bf16[256,2048]{1,0:T(8,128)(2,1)S(1)}, bf16[256,2048]{1,0:T(8,128)(2,1)S(1)}, u32[]{:S(2)}, u32[]{:S(2)}) collective-permute-start(bf16[256,2048]{1,0:T(8,128)(2,1)S(1)} %bitcast.46), channel_id=1, source_target_pairs={{0,4},{1,5},{2,6},{3,7},{4,0},{5,1},{6,2},{7,3},{8,12},{9,13},{10,... | collective-permute-start | bytes 3145736 | tf_op jit(solution)/shard_map/ppermute | solution.py:30
  17.7 38.7 %collective-permute-start = (bf16[256,2048]{1,0:T(8,128)(2,1)S(1)}, bf16[256,2048]{1,0:T(8,128)(2,1)}, u32[]{:S(2)}, u32[]{:S(2)}) collective-permute-start(bf16[256,2048]{1,0:T(8,128)(2,1)S(1)} %bitcast.47), channel_id=1, source_target_pairs={{0,2},{1,3},{2,0},{3,1},{4,6},{5,7},{6,4},{7,5},{8,10},{9,11},{10,... | collective-permute-start | bytes 3145736 | tf_op jit(solution)/shard_map/ppermute | solution.py:30
  22.2 31.3 %collective-permute-start.4 = (bf16[176,2048]{1,0:T(8,128)(2,1)}, bf16[176,2048]{1,0:T(8,128)(2,1)S(1)}, u32[]{:S(2)}, u32[]{:S(2)}) collective-permute-start(bf16[176,2048]{1,0:T(8,128)(2,1)} %refs_1_), channel_id=1, source_target_pairs={{0,8},{8,16},{16,24},{24,0},{1,9},{9,17},{17,25},{25,1},{2,10},{10... | collective-permute-start | bytes 2162696 | tf_op jit(solution)/shard_map/ppermute | solution.py:112
  57.6 60.0 %all-to-all-start.1 = ((bf16[32,208,128]{2,1,0:T(8,128)(2,1)}), bf16[32,208,128]{2,1,0:T(8,128)(2,1)}, u32[]{:S(2)}, u32[]{:S(2)}) async-start(bf16[32,208,128]{2,1,0:T(8,128)(2,1)} %pack_projections.1), calls=%async_computation.1 | async-start | bytes 3407872 | tf_op jit(solution)/shard_map/all_to_all | solution.py:99
  63.1 210.3 %all-gather.2.cloned.1.call-start = ((), (), s32[]{:S(2)}) async-start(), calls=%async_computation.8 | async-start | bytes 7208960 | tf_op jit(solution)/shard_map/all_gather | solution.py:1131
  63.1 52.5 %collective-permute-start.5 = (bf16[256,2048]{1,0:T(8,128)(2,1)}, bf16[256,2048]{1,0:T(8,128)(2,1)S(1)}, u32[]{:S(2)}, u32[]{:S(2)}) collective-permute-start(bf16[256,2048]{1,0:T(8,128)(2,1)} %collective-permute-done.refs_1_.refs_0_), channel_id=1, source_target_pairs={{0,1},{1,0},{2,3},{3,2},{4,5},{5,4},{6,7},{7,6},{8,9},{9,8},{10,11... | collective-permute-start | bytes 3145736 | tf_op jit(solution)/shard_map/ppermute | solution.py:30
  65.6 27.0 %collective-permute-start.7 = (bf16[128,2048]{1,0:T(8,128)(2,1)}, bf16[128,2048]{1,0:T(8,128)(2,1)S(1)}, u32[]{:S(2)}, u32[]{:S(2)}) collective-permute-start(bf16[128,2048]{1,0:T(8,128)(2,1)} %get-tuple-element.374), channel_id=1, source_target_pairs={{0,2},{1,3},{2,0},{3,1},{4,6},{5,7},{6,4},{7,5},{8,10},{9,11},{10,... | collective-permute-start | bytes 1572872 | tf_op jit(solution)/shard_map/ppermute | solution.py:30
  67.1 25.5 %collective-permute-start.8 = (bf16[128,2048]{1,0:T(8,128)(2,1)}, bf16[128,2048]{1,0:T(8,128)(2,1)S(1)}, u32[]{:S(2)}, u32[]{:S(2)}) collective-permute-start(bf16[128,2048]{1,0:T(8,128)(2,1)} %get-tuple-element.375), channel_id=1, source_target_pairs={{0,4},{1,5},{2,6},{3,7},{4,0},{5,1},{6,2},{7,3},{8,12},{9,13},{10,... | collective-permute-start | bytes 1572872 | tf_op jit(solution)/shard_map/ppermute | solution.py:30
  68.3 48.4 %collective-permute-start.6 = (bf16[256,2048]{1,0:T(8,128)(2,1)}, bf16[256,2048]{1,0:T(8,128)(2,1)S(1)}, u32[]{:S(2)}, u32[]{:S(2)}) collective-permute-start(bf16[256,2048]{1,0:T(8,128)(2,1)} %copy-done.17), channel_id=1, source_target_pairs={{0,1},{1,0},{2,3},{3,2},{4,5},{5,4},{6,7},{7,6},{8,9},{9,8},{10,11... | collective-permute-start | bytes 3145736 | tf_op jit(solution)/shard_map/ppermute | solution.py:30
  104.8 42.4 %collective-permute-start.15 = (bf16[256,2048]{1,0:T(8,128)(2,1)S(1)}, bf16[256,2048]{1,0:T(8,128)(2,1)S(1)}, u32[]{:S(2)}, u32[]{:S(2)}) collective-permute-start(bf16[256,2048]{1,0:T(8,128)(2,1)S(1)} %bitcast.40), channel_id=1, source_target_pairs={{0,4},{1,5},{2,6},{3,7},{4,0},{5,1},{6,2},{7,3},{8,12},{9,13},{10,... | collective-permute-start | bytes 3145736 | tf_op jit(solution)/shard_map/ppermute | solution.py:30
  115.6 31.6 %collective-permute-start.14 = (bf16[256,2048]{1,0:T(8,128)(2,1)S(1)}, bf16[256,2048]{1,0:T(8,128)(2,1)S(1)}, u32[]{:S(2)}, u32[]{:S(2)}) collective-permute-start(bf16[256,2048]{1,0:T(8,128)(2,1)S(1)} %bitcast.41), channel_id=1, source_target_pairs={{0,2},{1,3},{2,0},{3,1},{4,6},{5,7},{6,4},{7,5},{8,10},{9,11},{10,... | collective-permute-start | bytes 3145736 | tf_op jit(solution)/shard_map/ppermute | solution.py:30
  117.7 29.6 %collective-permute-start.13 = (bf16[64,2048]{1,0:T(8,128)(2,1)S(1)}, bf16[64,2048]{1,0:T(8,128)(2,1)}, u32[]{:S(2)}, u32[]{:S(2)}) collective-permute-start(bf16[64,2048]{1,0:T(8,128)(2,1)S(1)} %collective-permute-done.10.refs_1_), channel_id=1, source_target_pairs={{0,8},{8,16},{16,24},{24,0},{1,9},{9,17},{17,25},{25,1},{2,10},{10... | collective-permute-start | bytes 786440 | tf_op jit(solution)/shard_map/ppermute | solution.py:112
  117.7 29.6 %collective-permute-start.12 = (bf16[64,2048]{1,0:T(8,128)(2,1)S(1)}, bf16[64,2048]{1,0:T(8,128)(2,1)}, u32[]{:S(2)}, u32[]{:S(2)}) collective-permute-start(bf16[64,2048]{1,0:T(8,128)(2,1)S(1)} %collective-permute-done.10.refs_1_), channel_id=1, source_target_pairs={{0,16},{8,24},{16,0},{24,8},{1,17},{9,25},{17,1},{25,9},{2,18},{10... | collective-permute-start | bytes 786440 | tf_op jit(solution)/shard_map/ppermute | solution.py:112
  119.3 28.0 %collective-permute-start.11 = (bf16[64,2048]{1,0:T(8,128)(2,1)S(1)}, bf16[64,2048]{1,0:T(8,128)(2,1)}, u32[]{:S(2)}, u32[]{:S(2)}) collective-permute-start(bf16[64,2048]{1,0:T(8,128)(2,1)S(1)} %collective-permute-done.10.refs_1_), channel_id=1, source_target_pairs={{0,24},{8,0},{16,8},{24,16},{1,25},{9,1},{17,9},{25,17},{2,26},{10... | collective-permute-start | bytes 786440 | tf_op jit(solution)/shard_map/ppermute | solution.py:112
  147.3 315.2 %reduce-scatter.3.cloned.1.call-start = ((), (), s32[]{:S(2)}) async-start(), calls=%async_computation.9 | async-start | bytes 3604480 | tf_op jit(solution)/shard_map/reduce_scatter | solution.py:1182
  150.0 26.2 %collective-permute-start.19 = (bf16[256,2048]{1,0:T(8,128)(2,1)}, bf16[256,2048]{1,0:T(8,128)(2,1)}, u32[]{:S(2)}, u32[]{:S(2)}) collective-permute-start(bf16[256,2048]{1,0:T(8,128)(2,1)} %bitcast.48), channel_id=1, source_target_pairs={{0,1},{1,0},{2,3},{3,2},{4,5},{5,4},{6,7},{7,6},{8,9},{9,8},{10,11... | collective-permute-start | bytes 3145736 | tf_op jit(solution)/shard_map/ppermute | solution.py:30
  151.5 25.1 %collective-permute-start.18 = (bf16[256,2048]{1,0:T(8,128)(2,1)}, bf16[256,2048]{1,0:T(8,128)(2,1)S(1)}, u32[]{:S(2)}, u32[]{:S(2)}) collective-permute-start(bf16[256,2048]{1,0:T(8,128)(2,1)} %bitcast.49), channel_id=1, source_target_pairs={{0,4},{1,5},{2,6},{3,7},{4,0},{5,1},{6,2},{7,3},{8,12},{9,13},{10,... | collective-permute-start | bytes 3145736 | tf_op jit(solution)/shard_map/ppermute | solution.py:30
  151.5 25.1 %collective-permute-start.17 = (bf16[256,2048]{1,0:T(8,128)(2,1)}, bf16[256,2048]{1,0:T(8,128)(2,1)S(1)}, u32[]{:S(2)}, u32[]{:S(2)}) collective-permute-start(bf16[256,2048]{1,0:T(8,128)(2,1)} %bitcast.50), channel_id=1, source_target_pairs={{0,2},{1,3},{2,0},{3,1},{4,6},{5,7},{6,4},{7,5},{8,10},{9,11},{10,... | collective-permute-start | bytes 3145736 | tf_op jit(solution)/shard_map/ppermute | solution.py:30
  181.7 33.7 %collective-permute-start.20 = (bf16[256,2048]{1,0:T(8,128)(2,1)}, bf16[256,2048]{1,0:T(8,128)(2,1)S(1)}, u32[]{:S(2)}, u32[]{:S(2)}) collective-permute-start(bf16[256,2048]{1,0:T(8,128)(2,1)} %copy-done.8), channel_id=1, source_target_pairs={{0,1},{1,0},{2,3},{3,2},{4,5},{5,4},{6,7},{7,6},{8,9},{9,8},{10,11... | collective-permute-start | bytes 3145736 | tf_op jit(solution)/shard_map/ppermute | solution.py:30
  183.2 32.3 %collective-permute-start.21 = (bf16[256,2048]{1,0:T(8,128)(2,1)}, bf16[256,2048]{1,0:T(8,128)(2,1)S(1)}, u32[]{:S(2)}, u32[]{:S(2)}) collective-permute-start(bf16[256,2048]{1,0:T(8,128)(2,1)} %copy-done.7), channel_id=1, source_target_pairs={{0,1},{1,0},{2,3},{3,2},{4,5},{5,4},{6,7},{7,6},{8,9},{9,8},{10,11... | collective-permute-start | bytes 3145736 | tf_op jit(solution)/shard_map/ppermute | solution.py:30
  226.2 47.2 %collective-permute-start.27 = (bf16[256,2048]{1,0:T(8,128)(2,1)}, bf16[256,2048]{1,0:T(8,128)(2,1)}, u32[]{:S(2)}, u32[]{:S(2)}) collective-permute-start(bf16[256,2048]{1,0:T(8,128)(2,1)} %get-tuple-element.543.refs_0_), channel_id=1, source_target_pairs={{0,1},{1,0},{2,3},{3,2},{4,5},{5,4},{6,7},{7,6},{8,9},{9,8},{10,11... | collective-permute-start | bytes 3145736 | tf_op jit(solution)/shard_map/ppermute | solution.py:30
  227.6 63.3 %collective-permute-start.26 = (bf16[256,2048]{1,0:T(8,128)(2,1)}, bf16[256,2048]{1,0:T(8,128)(2,1)S(1)}, u32[]{:S(2)}, u32[]{:S(2)}) collective-permute-start(bf16[256,2048]{1,0:T(8,128)(2,1)} %get-tuple-element.543.refs_0_), channel_id=1, source_target_pairs={{0,4},{1,5},{2,6},{3,7},{4,0},{5,1},{6,2},{7,3},{8,12},{9,13},{10,... | collective-permute-start | bytes 3145736 | tf_op jit(solution)/shard_map/ppermute | solution.py:30
  227.9 63.0 %collective-permute-start.25 = (bf16[256,2048]{1,0:T(8,128)(2,1)}, bf16[256,2048]{1,0:T(8,128)(2,1)S(1)}, u32[]{:S(2)}, u32[]{:S(2)}) collective-permute-start(bf16[256,2048]{1,0:T(8,128)(2,1)} %get-tuple-element.543.refs_0_), channel_id=1, source_target_pairs={{0,2},{1,3},{2,0},{3,1},{4,6},{5,7},{6,4},{7,5},{8,10},{9,11},{10,... | collective-permute-start | bytes 3145736 | tf_op jit(solution)/shard_map/ppermute | solution.py:30
  230.1 28.8 %collective-permute-start.28 = (bf16[176,1024]{1,0:T(8,128)(2,1)}, bf16[176,1024]{1,0:T(8,128)(2,1)S(1)}, u32[]{:S(2)}, u32[]{:S(2)}) collective-permute-start(bf16[176,1024]{1,0:T(8,128)(2,1)} %get-tuple-element.458), channel_id=1, source_target_pairs={{0,24},{8,0},{16,8},{24,16},{1,25},{9,1},{17,9},{25,17},{2,26},{10... | collective-permute-start | bytes 1081352 | tf_op jit(solution)/shard_map/ppermute | solution.py:112
  231.0 34.0 %collective-permute-start.29 = (bf16[176,1024]{1,0:T(8,128)(2,1)}, bf16[176,1024]{1,0:T(8,128)(2,1)S(1)}, u32[]{:S(2)}, u32[]{:S(2)}) collective-permute-start(bf16[176,1024]{1,0:T(8,128)(2,1)} %get-tuple-element.459), channel_id=1, source_target_pairs={{0,8},{8,16},{16,24},{24,0},{1,9},{9,17},{17,25},{25,1},{2,10},{10... | collective-permute-start | bytes 1081352 | tf_op jit(solution)/shard_map/ppermute | solution.py:112
  268.6 39.3 %collective-permute-start.34 = (bf16[256,2048]{1,0:T(8,128)(2,1)S(1)}, bf16[256,2048]{1,0:T(8,128)(2,1)}, u32[]{:S(2)}, u32[]{:S(2)}) collective-permute-start(bf16[256,2048]{1,0:T(8,128)(2,1)S(1)} %collective-permute-done.14.refs_2_.refs_1_.refs_10_), channel_id=1, source_target_pairs={{0,1},{1,0},{2,3},{3,2},{4,5},{5,4},{6,7},{7,6},{8,9},{9,8},{10,11... | collective-permute-start | bytes 3145736 | tf_op jit(solution)/shard_map/ppermute | solution.py:30
  292.5 35.3 %collective-permute-start.33 = (bf16[256,2048]{1,0:T(8,128)(2,1)S(1)}, bf16[256,2048]{1,0:T(8,128)(2,1)S(1)}, u32[]{:S(2)}, u32[]{:S(2)}) collective-permute-start(bf16[256,2048]{1,0:T(8,128)(2,1)S(1)} %collective-permute-done.26.refs_0_.refs_4_), channel_id=1, source_target_pairs={{0,1},{1,0},{2,3},{3,2},{4,5},{5,4},{6,7},{7,6},{8,9},{9,8},{10,11... | collective-permute-start | bytes 3145736 | tf_op jit(solution)/shard_map/ppermute | solution.py:30
  295.1 32.7 %collective-permute-start.30 = (bf16[128,2048]{1,0:T(8,128)(2,1)}, bf16[128,2048]{1,0:T(8,128)(2,1)S(1)}, u32[]{:S(2)}, u32[]{:S(2)}) collective-permute-start(bf16[128,2048]{1,0:T(8,128)(2,1)} %get-tuple-element.464), channel_id=1, source_target_pairs={{0,2},{1,3},{2,0},{3,1},{4,6},{5,7},{6,4},{7,5},{8,10},{9,11},{10,... | collective-permute-start | bytes 1572872 | tf_op jit(solution)/shard_map/ppermute | solution.py:30
  391.1 199.0 %reduce-scatter.5.cloned.1.call-start = ((), (), s32[]{:S(2)}) async-start(), calls=%async_computation.10 | async-start | bytes 7208960 | tf_op jit(solution)/shard_map/reduce_scatter | solution.py:1203
  396.7 25.0 %collective-permute-start.46 = (bf16[256,2048]{1,0:T(8,128)(2,1)}, bf16[256,2048]{1,0:T(8,128)(2,1)S(1)}, u32[]{:S(2)}, u32[]{:S(2)}) collective-permute-start(bf16[256,2048]{1,0:T(8,128)(2,1)} %get-tuple-element.541), channel_id=1, source_target_pairs={{0,2},{1,3},{2,0},{3,1},{4,6},{5,7},{6,4},{7,5},{8,10},{9,11},{10,... | collective-permute-start | bytes 3145736 | tf_op jit(solution)/shard_map/ppermute | solution.py:30
  397.8 24.6 %collective-permute-start.47 = (bf16[256,2048]{1,0:T(8,128)(2,1)}, bf16[256,2048]{1,0:T(8,128)(2,1)}, u32[]{:S(2)}, u32[]{:S(2)}) collective-permute-start(bf16[256,2048]{1,0:T(8,128)(2,1)} %get-tuple-element.542), channel_id=1, source_target_pairs={{0,4},{1,5},{2,6},{3,7},{4,0},{5,1},{6,2},{7,3},{8,12},{9,13},{10,... | collective-permute-start | bytes 3145736 | tf_op jit(solution)/shard_map/ppermute | solution.py:30
  436.3 26.1 %collective-permute-start.52 = (bf16[256,2048]{1,0:T(8,128)(2,1)S(1)}, bf16[256,2048]{1,0:T(8,128)(2,1)}, u32[]{:S(2)}, u32[]{:S(2)}) collective-permute-start(bf16[256,2048]{1,0:T(8,128)(2,1)S(1)} %copy-done.67), channel_id=1, source_target_pairs={{0,1},{1,0},{2,3},{3,2},{4,5},{5,4},{6,7},{7,6},{8,9},{9,8},{10,11... | collective-permute-start | bytes 3145736 | tf_op jit(solution)/shard_map/ppermute | solution.py:30
  438.2 24.2 %collective-permute-start.53 = (bf16[256,2048]{1,0:T(8,128)(2,1)S(1)}, bf16[256,2048]{1,0:T(8,128)(2,1)S(1)}, u32[]{:S(2)}, u32[]{:S(2)}) collective-permute-start(bf16[256,2048]{1,0:T(8,128)(2,1)S(1)} %copy-done.68), channel_id=1, source_target_pairs={{0,1},{1,0},{2,3},{3,2},{4,5},{5,4},{6,7},{7,6},{8,9},{9,8},{10,11... | collective-permute-start | bytes 3145736 | tf_op jit(solution)/shard_map/ppermute | solution.py:30
  438.3 24.1 %collective-permute-start.54 = (bf16[256,2048]{1,0:T(8,128)(2,1)}, bf16[256,2048]{1,0:T(8,128)(2,1)S(1)}, u32[]{:S(2)}, u32[]{:S(2)}) collective-permute-start(bf16[256,2048]{1,0:T(8,128)(2,1)} %get-tuple-element.588), channel_id=1, source_target_pairs={{0,1},{1,0},{2,3},{3,2},{4,5},{5,4},{6,7},{7,6},{8,9},{9,8},{10,11... | collective-permute-start | bytes 3145736 | tf_op jit(solution)/shard_map/ppermute | solution.py:30
  468.4 35.7 %collective-permute-start.57 = (bf16[256,2048]{1,0:T(8,128)(2,1)}, bf16[256,2048]{1,0:T(8,128)(2,1)S(1)}, u32[]{:S(2)}, u32[]{:S(2)}) collective-permute-start(bf16[256,2048]{1,0:T(8,128)(2,1)} %get-tuple-element.616), channel_id=1, source_target_pairs={{0,2},{1,3},{2,0},{3,1},{4,6},{5,7},{6,4},{7,5},{8,10},{9,11},{10,... | collective-permute-start | bytes 3145736 | tf_op jit(solution)/shard_map/ppermute | solution.py:30
  469.0 35.0 %collective-permute-start.58 = (bf16[256,2048]{1,0:T(8,128)(2,1)}, bf16[256,2048]{1,0:T(8,128)(2,1)S(1)}, u32[]{:S(2)}, u32[]{:S(2)}) collective-permute-start(bf16[256,2048]{1,0:T(8,128)(2,1)} %get-tuple-element.617), channel_id=1, source_target_pairs={{0,4},{1,5},{2,6},{3,7},{4,0},{5,1},{6,2},{7,3},{8,12},{9,13},{10,... | collective-permute-start | bytes 3145736 | tf_op jit(solution)/shard_map/ppermute | solution.py:30
  471.6 31.2 %collective-permute-start.55 = (bf16[128,2048]{1,0:T(8,128)(2,1)}, bf16[128,2048]{1,0:T(8,128)(2,1)S(1)}, u32[]{:S(2)}, u32[]{:S(2)}) collective-permute-start(bf16[128,2048]{1,0:T(8,128)(2,1)} %get-tuple-element.606), channel_id=1, source_target_pairs={{0,2},{1,3},{2,0},{3,1},{4,6},{5,7},{6,4},{7,5},{8,10},{9,11},{10,... | collective-permute-start | bytes 1572872 | tf_op jit(solution)/shard_map/ppermute | solution.py:30
  472.4 31.6 %collective-permute-start.56 = (bf16[128,2048]{1,0:T(8,128)(2,1)}, bf16[128,2048]{1,0:T(8,128)(2,1)S(1)}, u32[]{:S(2)}, u32[]{:S(2)}) collective-permute-start(bf16[128,2048]{1,0:T(8,128)(2,1)} %get-tuple-element.607), channel_id=1, source_target_pairs={{0,4},{1,5},{2,6},{3,7},{4,0},{5,1},{6,2},{7,3},{8,12},{9,13},{10,... | collective-permute-start | bytes 1572872 | tf_op jit(solution)/shard_map/ppermute | solution.py:30
  525.6 69.7 %all-to-all-start.4 = ((bf16[32,64,384]{2,1,0:T(8,128)(2,1)}), bf16[32,64,384]{2,1,0:T(8,128)(2,1)S(1)}, u32[]{:S(2)}, u32[]{:S(2)}) async-start(bf16[32,64,384]{2,1,0:T(8,128)(2,1)} %bitcast.53), calls=%async_computation.6 | async-start | bytes 3145728 | tf_op jit(solution)/shard_map/all_to_all | solution.py:99
  552.5 29.8 %collective-permute-start.70 = (bf16[256,2048]{1,0:T(8,128)(2,1)}, bf16[256,2048]{1,0:T(8,128)(2,1)S(1)}, u32[]{:S(2)}, u32[]{:S(2)}) collective-permute-start(bf16[256,2048]{1,0:T(8,128)(2,1)} %get-tuple-element.703), channel_id=1, source_target_pairs={{0,2},{1,3},{2,0},{3,1},{4,6},{5,7},{6,4},{7,5},{8,10},{9,11},{10,... | collective-permute-start | bytes 3145736 | tf_op jit(solution)/shard_map/ppermute | solution.py:30
  552.6 30.5 %collective-permute-start.71 = (bf16[256,2048]{1,0:T(8,128)(2,1)S(1)}, bf16[256,2048]{1,0:T(8,128)(2,1)S(1)}, u32[]{:S(2)}, u32[]{:S(2)}) collective-permute-start(bf16[256,2048]{1,0:T(8,128)(2,1)S(1)} %copy-done.70), channel_id=1, source_target_pairs={{0,4},{1,5},{2,6},{3,7},{4,0},{5,1},{6,2},{7,3},{8,12},{9,13},{10,... | collective-permute-start | bytes 3145736 | tf_op jit(solution)/shard_map/ppermute | solution.py:30
  554.1 46.7 %collective-permute-start.65 = (bf16[256,2048]{1,0:T(8,128)(2,1)}, bf16[256,2048]{1,0:T(8,128)(2,1)}, u32[]{:S(2)}, u32[]{:S(2)}) collective-permute-start(bf16[256,2048]{1,0:T(8,128)(2,1)} %get-tuple-element.692), channel_id=1, source_target_pairs={{0,1},{1,0},{2,3},{3,2},{4,5},{5,4},{6,7},{7,6},{8,9},{9,8},{10,11... | collective-permute-start | bytes 3145736 | tf_op jit(solution)/shard_map/ppermute | solution.py:30
  561.2 47.6 %collective-permute-start.68 = (bf16[256,2048]{1,0:T(8,128)(2,1)}, bf16[256,2048]{1,0:T(8,128)(2,1)}, u32[]{:S(2)}, u32[]{:S(2)}) collective-permute-start(bf16[256,2048]{1,0:T(8,128)(2,1)} %get-tuple-element.699), channel_id=1, source_target_pairs={{0,2},{1,3},{2,0},{3,1},{4,6},{5,7},{6,4},{7,5},{8,10},{9,11},{10,... | collective-permute-start | bytes 3145736 | tf_op jit(solution)/shard_map/ppermute | solution.py:30
  561.3 47.6 %collective-permute-start.69 = (bf16[256,2048]{1,0:T(8,128)(2,1)}, bf16[256,2048]{1,0:T(8,128)(2,1)}, u32[]{:S(2)}, u32[]{:S(2)}) collective-permute-start(bf16[256,2048]{1,0:T(8,128)(2,1)} %get-tuple-element.700), channel_id=1, source_target_pairs={{0,4},{1,5},{2,6},{3,7},{4,0},{5,1},{6,2},{7,3},{8,12},{9,13},{10,... | collective-permute-start | bytes 3145736 | tf_op jit(solution)/shard_map/ppermute | solution.py:30
  595.3 53.2 %all-to-all-start.5 = ((bf16[8,64,1408]{2,1,0:T(8,128)(2,1)}), bf16[8,64,1408]{2,1,0:T(8,128)(2,1)S(1)}, u32[]{:S(2)}, u32[]{:S(2)}) async-start(bf16[8,64,1408]{2,1,0:T(8,128)(2,1)} %bitcast.58), calls=%async_computation.7 | async-start | bytes 2883584 | tf_op jit(solution)/shard_map/all_to_all | solution.py:95
  622.5 25.1 %collective-permute-start.75 = (bf16[64,2048]{1,0:T(8,128)(2,1)}, bf16[64,2048]{1,0:T(8,128)(2,1)S(1)}, u32[]{:S(2)}, u32[]{:S(2)}) collective-permute-start(bf16[64,2048]{1,0:T(8,128)(2,1)} %add_up.3), channel_id=1, source_target_pairs={{0,0},{8,1},{16,2},{24,3},{1,4},{9,5},{17,6},{25,7},{2,8},{10,9},{... | collective-permute-start | bytes 786440 | tf_op jit(solution)/shard_map/ppermute | solution.py:107
  (113 other events, 1178.0 us)
Sparse Core Ops, SparseCore 0:
  147.4 121.2 all-gather.1
  391.2 53.4 reduce-scatter.2
  462.6 123.0 reduce-scatter.4

commit v4 on v3

--- a/solution.py
+++ b/solution.py
@@ -1232,13 +1232,14 @@
     (grad_input,) = back_through_norm(grad_res, block, sides, gain_one, False)
     grad_input, out_parts = tie(grad_input, out_parts)
     both_parts = exchange_seq(both_sum.reshape(n_seq, owned, 2 * padded(units)))
-    grad_out = deal(add_up(out_parts, BF16), back=True).astype(F32)
+    grad_out = deal(add_up(out_parts, BF16), back=True)
     output = end_output(residual, f_sides)
 
     grad_gate, grad_up, sums_two = unpack_units(both_parts, w_gate, w_up, n_dp, n_seq)
     grad_query, grad_key, grad_value, sums_one = unpack_columns(
         qkv_parts, w_query, w_key, w_value, n_dp, n_seq
     )
+    grad_gate, grad_up, sums_two, grad_out = tie(grad_gate, grad_up, sums_two, grad_out)
     return (
         output.reshape(seqs, here, width),
         grad_input.reshape(seqs, here, width),
@@ -1246,7 +1247,7 @@
         grad_query,
         grad_key,
         grad_value,
-        grad_out,
+        grad_out.astype(F32),
         sums_two[:, 0] / ffn_norm.astype(F32),
         grad_gate,
         grad_up,

time: 666 us -> 661 us (level)
  transfers between devices with their start and end apart: 83 -> 83, of which waited for: 26 -> 26; matrix products, arithmetic and copies ran while one was open for 1% -> 1% of each run, Pallas kernels for 43% -> 44%
where the time goes in v4:
time: 661 us; the launch traced here: 657 us
  Pallas kernels  309 us (47%)
  waiting for transfers between devices  170 us (26%)
  starting transfers between devices  96.7 us (15%)
  blocking collectives  34.9 us (5%)
  local copies, waits for them, and re-layouts  25.9 us (4%)
  between operations  14.9 us (2%)
    ppermute x64, waiting for transfers between devices, swap(): return lax.ppermute(block, 'seq', [(i, i ^ distance) for i in range(size)])  82.6 us
    pallas_call x4, Pallas kernels, ffn(): pl.pallas_call(functools.partial(ffn_kernel, count), out_shape=shapes, co...  70.2 us
    ppermute x10, waiting for transfers between devices, shift(): lax.ppermute(block, 'dp', [(i, (i + step) % size) for i in range(size)])  64.1 us
    ppermute x64, starting transfers between devices, swap(): return lax.ppermute(block, 'seq', [(i, i ^ distance) for i in range(size)])  58.3 us
    pallas_call x11, Pallas kernels, by_rows(): pl.pallas_call(kernel, out_shape=[jax.ShapeDtypeStruct(shape[:2], shape[2...  40.6 us
    pallas_call x3, Pallas kernels, outer(): pl.pallas_call(functools.partial(outer_kernel, count, along_left), out_sh...  38.7 us
    pallas_call x9, Pallas kernels, local(): pl.pallas_call(kernel, out_shape=[jax.ShapeDtypeStruct(*out) for out in o...  38.7 us
    all_to_all x2, blocking collectives, exchange_seq(): return lax.all_to_all(blocks, 'seq', 0, 0, tiled=True)  34.9 us
  transfers between devices with their start and end apart: 83, of which 26 were waited for; matrix products, arithmetic and copies ran while one was open for 1% of the time, Pallas kernels for 44%

profile of v4, /device:TPU:1, one launch (start us, length us, event | category | flops | bytes accessed | tf_op | source)
XLA Modules:
  0.0 656.7 jit_solution(5929693964728735644)
XLA Ops:
  10.6 5.4 all-to-all-start
  25.3 12.1 %collective-permute-done.3.refs_0_.refs_2_ = bf16[176,2048]{1,0:T(8,128)(2,1)S(1)} collective-permute-done((bf16[176,2048]{1,0:T(8,128)(2,1)}, bf16[176,2048]{1,0:T(8,128)(2,1)S(1)}, u32[]{:S(2)}, u32[]{:S(2)}) %collective-permute-start.3) | collective-permute-done | bytes 720928 | tf_op jit(solution)/shard_map/ppermute | solution.py:112
  37.4 16.2 %collective-permute-done.4.refs_1_.refs_3_ = bf16[176,2048]{1,0:T(8,128)(2,1)S(1)} collective-permute-done((bf16[176,2048]{1,0:T(8,128)(2,1)}, bf16[176,2048]{1,0:T(8,128)(2,1)S(1)}, u32[]{:S(2)}, u32[]{:S(2)}) %collective-permute-start.4) | collective-permute-done | bytes 720928 | tf_op jit(solution)/shard_map/ppermute | solution.py:112
  57.6 5.5 all-to-all-start.1
  69.0 23.6 %collective-permute-done.7.refs_0_ = bf16[128,2048]{1,0:T(8,128)(2,1)S(1)} collective-permute-done((bf16[128,2048]{1,0:T(8,128)(2,1)}, bf16[128,2048]{1,0:T(8,128)(2,1)S(1)}, u32[]{:S(2)}, u32[]{:S(2)}) %collective-permute-start.7) | collective-permute-done | bytes 524320 | tf_op jit(solution)/shard_map/ppermute | solution.py:30
  100.2 4.6 collective-permute-done.10.refs_1_
  104.8 10.9 %collective-permute-start.15 = (bf16[256,2048]{1,0:T(8,128)(2,1)S(1)}, bf16[256,2048]{1,0:T(8,128)(2,1)S(1)}, u32[]{:S(2)}, u32[]{:S(2)}) collective-permute-start(bf16[256,2048]{1,0:T(8,128)(2,1)S(1)} %bitcast.40), channel_id=1, source_target_pairs={{0,4},{1,5},{2,6},{3,7},{4,0},{5,1},{6,2},{7,3},{8,12},{9,13},{10,... | collective-permute-start | bytes 3145736 | tf_op jit(solution)/shard_map/ppermute | solution.py:30
  121.1 7.7 %unpack_projections.1 = (bf16[2048,384]{1,0:T(8,128)(2,1)}, f32[1,2048]{1,0:T(1,128)}, f32[1,2048]{1,0:T(1,128)}, f32[2,1024,128]{2,1,0:T(8,128)}, f32[2,1024,128]{2,1,0:T(8,128)}, /*index=5*/s32[2,1,1024]{2,1,0:T(1,128)}) custom-call(s32[1]{0:T(128)} %bitcast.4.me.refs_0_, bf16[32,208,128]{2,1,0:T(8,128)(2,1)} %all-to-all-done.1.packed), custom_call_target="tpu_custom_call" | custom-call | flops 1 | bytes 1 | tf_op jit(solution)/shard_map/unpack_projections/pallas_call | solution.py:426
  128.8 4.6 enter.7
  133.5 4.6 enter.6
  138.0 4.6 enter.5
  142.7 4.5 enter.4
  152.2 24.0 %attend.1 = (bf16[8,2,128,256]{3,2,1,0:T(8,128)(2,1)}, bf16[2,1024,256]{2,1,0:T(8,128)(2,1)}, bf16[2,2,1024,128]{3,2,1,0:T(8,128)(2,1)}, bf16[2,1024,128]{2,1,0:T(8,128)(2,1)}, f32[2,4,1,1024]{3,2,1,0:T(1,128)}) custom-call(s32[1]{0:T(128)} %bitcast.me_ref.me, f32[2,128,384]{2,1,0:T(8,128)} %bitcast.83, f32[2,128,384]{2,1,0:T(8,128)} %bitcast.84, ...), custom_call_target="tpu_custom_call" | custom-call | flops 1 | bytes 1 | tf_op jit(solution)/shard_map/attend/pallas_call | solution.py:1008
  183.2 9.8 %collective-permute-done.22.refs_0_ = bf16[128,2048]{1,0:T(8,128)(2,1)S(1)} collective-permute-done((bf16[128,2048]{1,0:T(8,128)(2,1)}, bf16[128,2048]{1,0:T(8,128)(2,1)S(1)}, u32[]{:S(2)}, u32[]{:S(2)}) %collective-permute-start.22) | collective-permute-done | bytes 524320 | tf_op jit(solution)/shard_map/ppermute | solution.py:30
  198.2 17.2 %all_to_all.30.mixed = bf16[8,256,256]{2,1,0:T(8,128)(2,1)} all-to-all(bf16[8,256,256]{2,1,0:T(8,128)(2,1)S(1)} %bitcast.60), channel_id=1, replica_groups=mesh['dp'=4,'seq'=8] {'seq'}, dimensions={0} | all-to-all | bytes 2097152 | tf_op jit(solution)/shard_map/all_to_all | solution.py:95
  217.1 9.1 %end_attention.1 = (f32[256,2048]{1,0:T(8,128)}, bf16[256,2048]{1,0:T(8,128)(2,1)}) custom-call(s32[1]{0:T(128)} %bitcast.me_ref.me, bf16[256,2048]{1,0:T(8,128)(2,1)} %bitcast.43, bf16[8,256,256]{2,1,0:T(8,128)(2,1)} %all_to_all.30.mixed, f32[1,2048]{1,0:T(1,128)} %get-tuple-element.441.gain.refs_6_, bf16[256,2048]{1,0:T(8,128)(2,1)} %bitcast.51, ...), custom_call_target="tpu_custom_call" | custom-call | flops 1 | bytes 1 | tf_op jit(solution)/shard_map/end_attention/pallas_call | solution.py:361
  231.6 27.3 %collective-permute-done.28.refs_4_ = bf16[176,1024]{1,0:T(8,128)(2,1)S(1)} collective-permute-done((bf16[176,1024]{1,0:T(8,128)(2,1)}, bf16[176,1024]{1,0:T(8,128)(2,1)S(1)}, u32[]{:S(2)}, u32[]{:S(2)}) %collective-permute-start.28) | collective-permute-done | bytes 360480 | tf_op jit(solution)/shard_map/ppermute | solution.py:112
  259.0 6.0 collective-permute-done.29.refs_5_
  273.4 17.5 %ffn.4 = (bf16[256,2048]{1,0:T(8,128)(2,1)}, bf16[256,2048]{1,0:T(8,128)(2,1)}, bf16[256,2048]{1,0:T(8,128)(2,1)}, bf16[256,2048]{1,0:T(8,128)(2,1)}, bf16[256,7...) custom-call(bf16[256,2048]{1,0:T(8,128)(2,1)} %get-tuple-element.547.refs_0_, ...), custom_call_target="tpu_custom_call" | custom-call | flops 1 | bytes 1 | tf_op jit(solution)/shard_map/ffn/pallas_call | solution.py:723
  295.4 9.2 %collective-permute-done.37.refs_1_ = bf16[128,2048]{1,0:T(8,128)(2,1)S(1)} collective-permute-done((bf16[128,2048]{1,0:T(8,128)(2,1)S(1)}, bf16[128,2048]{1,0:T(8,128)(2,1)S(1)}, u32[]{:S(2)}, u32[]{:S(2)}) %collective-permute-start.37) | collective-permute-done | bytes 524320 | tf_op jit(solution)/shard_map/ppermute | solution.py:30
  310.3 17.5 %ffn.5 = (bf16[256,2048]{1,0:T(8,128)(2,1)}, bf16[256,2048]{1,0:T(8,128)(2,1)}, bf16[256,2048]{1,0:T(8,128)(2,1)}, bf16[256,2048]{1,0:T(8,128)(2,1)}, bf16[256,7...) custom-call(bf16[256,2048]{1,0:T(8,128)(2,1)} %copy-done.4, ...), custom_call_target="tpu_custom_call" | custom-call | flops 1 | bytes 1 | tf_op jit(solution)/shard_map/ffn/pallas_call | solution.py:723
  334.8 17.7 %ffn.6 = (bf16[256,2048]{1,0:T(8,128)(2,1)}, bf16[256,2048]{1,0:T(8,128)(2,1)}, bf16[256,2048]{1,0:T(8,128)(2,1)}, bf16[256,2048]{1,0:T(8,128)(2,1)}, bf16[256,7...) custom-call(bf16[256,2048]{1,0:T(8,128)(2,1)} %join.6.refs_0_.refs_6_, ...), custom_call_target="tpu_custom_call" | custom-call | flops 1 | bytes 1 | tf_op jit(solution)/shard_map/ffn/pallas_call | solution.py:723
  361.0 17.5 %ffn.7 = (bf16[256,2048]{1,0:T(8,128)(2,1)}, bf16[256,2048]{1,0:T(8,128)(2,1)}, bf16[256,2048]{1,0:T(8,128)(2,1)}, bf16[256,2048]{1,0:T(8,128)(2,1)}, bf16[256,7...) custom-call(bf16[256,2048]{1,0:T(8,128)(2,1)} %copy-done.3, ...), custom_call_target="tpu_custom_call" | custom-call | flops 1 | bytes 1 | tf_op jit(solution)/shard_map/ffn/pallas_call | solution.py:723
  380.2 10.8 %outer.3 = bf16[704,2048]{1,0:T(8,128)(2,1)} custom-call(bf16[256,704]{1,0:T(8,128)(2,1)} %get-tuple-element.511.refs_0_, bf16[256,704]{1,0:T(8,128)(2,1)} %get-tuple-element.512.refs_1_, bf16[256,704]{1,0:T(8,128)(2,1)} %get-tuple-element.513.refs_2_, bf16[256,704]{1,0:T(8,128)(2,1)} %get-tuple-element.514.refs_3_, ...), custom_call_target="tpu_custom_call" | custom-call | flops 1 | bytes 1 | tf_op jit(solution)/shard_map/outer/pallas_call | solution.py:763
  392.4 3.9 sums_for_sides.4
  398.6 19.1 %outer.4 = bf16[2048,1408]{1,0:T(8,128)(2,1)} custom-call(bf16[256,2048]{1,0:T(8,128)(2,1)} %get-tuple-element.547.refs_0_, bf16[256,2048]{1,0:T(8,128)(2,1)} %collective-permute-done.27.refs_1_, bf16[256,2048]{1,0:T(8,128)(2,1)} %copy-done.4, bf16[256,2048]{1,0:T(8,128)(2,1)} %copy-done.12, bf16[256,2048]{1,0:T(8,128)(2,1)} %copy-done.3, ...), custom_call_target="tpu_custom_call" | custom-call | flops 1 | bytes 1 | tf_op jit(solution)/shard_map/outer/pallas_call | solution.py:763
  423.6 5.5 back_through_norm.2
  429.1 7.2 %back_to_heads.1 = bf16[8,256,256]{2,1,0:T(8,128)(2,1)} custom-call(s32[1]{0:T(128)} %bitcast.me_ref.me, bf16[256,2048]{1,0:T(8,128)(2,1)} %get-tuple-element.579.grad, bf16[256,2048]{1,0:T(8,128)(2,1)} %bitcast.52, bf16[256,2048]{1,0:T(8,128)(2,1)} %collective-permute-done.19.refs_1_, bf16[256,2048]{1,0:T(8,128)(2,1)} %copy-done.8, ...), custom_call_target="tpu_custom_call" | custom-call | flops 1 | bytes 1 | tf_op jit(solution)/shard_map/back_to_heads/pallas_call | solution.py:426
  438.7 5.8 out_products.1
  444.6 17.8 %all_to_all.31 = bf16[8,256,256]{2,1,0:T(8,128)(2,1)} all-to-all(bf16[8,256,256]{2,1,0:T(8,128)(2,1)S(1)} %copy-done.21), channel_id=1, replica_groups=mesh['dp'=4,'seq'=8] {'seq'}, dimensions={0} | all-to-all | bytes 2097152 | tf_op jit(solution)/shard_map/all_to_all | solution.py:95
  464.1 4.3 sums_for_sides.5
  473.9 28.6 %attend_back.1 = (bf16[2,128,384]{2,1,0:T(8,128)(2,1)}, bf16[2,128,384]{2,1,0:T(8,128)(2,1)}, bf16[2,128,384]{2,1,0:T(8,128)(2,1)}, bf16[2,128,384]{2,1,0:T(8,12...) custom-call(s32[1]{0:T(128)} %bitcast.me_ref.me, ...), custom_call_target="tpu_custom_call" | custom-call | flops 1 | bytes 1 | tf_op jit(solution)/shard_map/attend_back/pallas_call | solution.py:1041
  506.7 3.9 multiply.4
  516.7 8.8 %outer.5 = bf16[2048,384]{1,0:T(8,128)(2,1)} custom-call(bf16[256,2048]{1,0:T(8,128)(2,1)} %get-tuple-element.661.refs_0_, bf16[256,2048]{1,0:T(8,128)(2,1)} %get-tuple-element.662.refs_1_, bf16[256,2048]{1,0:T(8,128)(2,1)} %get-tuple-element.663.refs_2_, bf16[256,2048]{1,0:T(8,128)(2,1)} %get-tuple-element.664.refs_3_, ...), custom_call_target="tpu_custom_call" | custom-call | flops 1 | bytes 1 | tf_op jit(solution)/shard_map/outer/pallas_call | solution.py:763
  533.9 3.9 multiply.5
  537.7 4.0 multiply.6
  541.7 3.9 multiply.7
  545.6 5.7 collective-permute-done.63.refs_4_
  557.4 3.8 sums_for_sides.7
  562.8 19.6 %collective-permute-done.70.refs_2_ = bf16[256,2048]{1,0:T(8,128)(2,1)S(1)} collective-permute-done((bf16[256,2048]{1,0:T(8,128)(2,1)}, bf16[256,2048]{1,0:T(8,128)(2,1)S(1)}, u32[]{:S(2)}, u32[]{:S(2)}) %collective-permute-start.70) | collective-permute-done | bytes 1048608 | tf_op jit(solution)/shard_map/ppermute | solution.py:30
  584.3 3.8 add_up.2
  590.1 5.2 all-to-all-done.4.parts
  595.3 4.0 all-to-all-start.5
  605.0 3.9 end_output.1
  608.9 5.1 back_through_norm.3
  622.5 5.4 collective-permute-start.75
  630.4 3.8 unpack_units.1
  634.2 13.4 %collective-permute-done.75 = bf16[64,2048]{1,0:T(8,128)(2,1)S(1)} collective-permute-done((bf16[64,2048]{1,0:T(8,128)(2,1)}, bf16[64,2048]{1,0:T(8,128)(2,1)S(1)}, u32[]{:S(2)}, u32[]{:S(2)}) %collective-permute-start.75) | collective-permute-done | bytes 262176 | tf_op jit(solution)/shard_map/ppermute | solution.py:107
  (338 shorter events, 163.8 us)
Async XLA Ops:
  10.6 45.8 %all-to-all-start = ((bf16[8,64,1408]{2,1,0:T(8,128)(2,1)}), bf16[8,64,1408]{2,1,0:T(8,128)(2,1)S(1)}, u32[]{:S(2)}, u32[]{:S(2)}) async-start(bf16[8,64,1408]{2,1,0:T(8,128)(2,1)} %pack_units.1), calls=%async_computation | async-start | bytes 2883584 | tf_op jit(solution)/shard_map/all_to_all | solution.py:95
  16.0 37.6 %collective-permute-start.2 = (bf16[256,2048]{1,0:T(8,128)(2,1)S(1)}, bf16[256,2048]{1,0:T(8,128)(2,1)S(1)}, u32[]{:S(2)}, u32[]{:S(2)}) collective-permute-start(bf16[256,2048]{1,0:T(8,128)(2,1)S(1)} %bitcast.45), channel_id=1, source_target_pairs={{0,1},{1,0},{2,3},{3,2},{4,5},{5,4},{6,7},{7,6},{8,9},{9,8},{10,11... | collective-permute-start | bytes 3145736 | tf_op jit(solution)/shard_map/ppermute | solution.py:30
  16.1 40.3 %collective-permute-start.1 = (bf16[256,2048]{1,0:T(8,128)(2,1)S(1)}, bf16[256,2048]{1,0:T(8,128)(2,1)S(1)}, u32[]{:S(2)}, u32[]{:S(2)}) collective-permute-start(bf16[256,2048]{1,0:T(8,128)(2,1)S(1)} %bitcast.46), channel_id=1, source_target_pairs={{0,4},{1,5},{2,6},{3,7},{4,0},{5,1},{6,2},{7,3},{8,12},{9,13},{10,... | collective-permute-start | bytes 3145736 | tf_op jit(solution)/shard_map/ppermute | solution.py:30
  17.7 38.7 %collective-permute-start = (bf16[256,2048]{1,0:T(8,128)(2,1)S(1)}, bf16[256,2048]{1,0:T(8,128)(2,1)}, u32[]{:S(2)}, u32[]{:S(2)}) collective-permute-start(bf16[256,2048]{1,0:T(8,128)(2,1)S(1)} %bitcast.47), channel_id=1, source_target_pairs={{0,2},{1,3},{2,0},{3,1},{4,6},{5,7},{6,4},{7,5},{8,10},{9,11},{10,... | collective-permute-start | bytes 3145736 | tf_op jit(solution)/shard_map/ppermute | solution.py:30
  22.2 31.3 %collective-permute-start.4 = (bf16[176,2048]{1,0:T(8,128)(2,1)}, bf16[176,2048]{1,0:T(8,128)(2,1)S(1)}, u32[]{:S(2)}, u32[]{:S(2)}) collective-permute-start(bf16[176,2048]{1,0:T(8,128)(2,1)} %refs_1_), channel_id=1, source_target_pairs={{0,8},{8,16},{16,24},{24,0},{1,9},{9,17},{17,25},{25,1},{2,10},{10... | collective-permute-start | bytes 2162696 | tf_op jit(solution)/shard_map/ppermute | solution.py:112
  57.6 60.0 %all-to-all-start.1 = ((bf16[32,208,128]{2,1,0:T(8,128)(2,1)}), bf16[32,208,128]{2,1,0:T(8,128)(2,1)}, u32[]{:S(2)}, u32[]{:S(2)}) async-start(bf16[32,208,128]{2,1,0:T(8,128)(2,1)} %pack_projections.1), calls=%async_computation.1 | async-start | bytes 3407872 | tf_op jit(solution)/shard_map/all_to_all | solution.py:99
  63.1 210.3 %all-gather.2.cloned.1.call-start = ((), (), s32[]{:S(2)}) async-start(), calls=%async_computation.8 | async-start | bytes 7208960 | tf_op jit(solution)/shard_map/all_gather | solution.py:1131
  63.1 52.5 %collective-permute-start.5 = (bf16[256,2048]{1,0:T(8,128)(2,1)}, bf16[256,2048]{1,0:T(8,128)(2,1)S(1)}, u32[]{:S(2)}, u32[]{:S(2)}) collective-permute-start(bf16[256,2048]{1,0:T(8,128)(2,1)} %collective-permute-done.refs_1_.refs_0_), channel_id=1, source_target_pairs={{0,1},{1,0},{2,3},{3,2},{4,5},{5,4},{6,7},{7,6},{8,9},{9,8},{10,11... | collective-permute-start | bytes 3145736 | tf_op jit(solution)/shard_map/ppermute | solution.py:30
  65.6 27.0 %collective-permute-start.7 = (bf16[128,2048]{1,0:T(8,128)(2,1)}, bf16[128,2048]{1,0:T(8,128)(2,1)S(1)}, u32[]{:S(2)}, u32[]{:S(2)}) collective-permute-start(bf16[128,2048]{1,0:T(8,128)(2,1)} %get-tuple-element.378), channel_id=1, source_target_pairs={{0,2},{1,3},{2,0},{3,1},{4,6},{5,7},{6,4},{7,5},{8,10},{9,11},{10,... | collective-permute-start | bytes 1572872 | tf_op jit(solution)/shard_map/ppermute | solution.py:30
  67.1 25.5 %collective-permute-start.8 = (bf16[128,2048]{1,0:T(8,128)(2,1)}, bf16[128,2048]{1,0:T(8,128)(2,1)S(1)}, u32[]{:S(2)}, u32[]{:S(2)}) collective-permute-start(bf16[128,2048]{1,0:T(8,128)(2,1)} %get-tuple-element.379), channel_id=1, source_target_pairs={{0,4},{1,5},{2,6},{3,7},{4,0},{5,1},{6,2},{7,3},{8,12},{9,13},{10,... | collective-permute-start | bytes 1572872 | tf_op jit(solution)/shard_map/ppermute | solution.py:30
  68.3 48.4 %collective-permute-start.6 = (bf16[256,2048]{1,0:T(8,128)(2,1)}, bf16[256,2048]{1,0:T(8,128)(2,1)S(1)}, u32[]{:S(2)}, u32[]{:S(2)}) collective-permute-start(bf16[256,2048]{1,0:T(8,128)(2,1)} %copy-done.17), channel_id=1, source_target_pairs={{0,1},{1,0},{2,3},{3,2},{4,5},{5,4},{6,7},{7,6},{8,9},{9,8},{10,11... | collective-permute-start | bytes 3145736 | tf_op jit(solution)/shard_map/ppermute | solution.py:30
  104.8 42.4 %collective-permute-start.15 = (bf16[256,2048]{1,0:T(8,128)(2,1)S(1)}, bf16[256,2048]{1,0:T(8,128)(2,1)S(1)}, u32[]{:S(2)}, u32[]{:S(2)}) collective-permute-start(bf16[256,2048]{1,0:T(8,128)(2,1)S(1)} %bitcast.40), channel_id=1, source_target_pairs={{0,4},{1,5},{2,6},{3,7},{4,0},{5,1},{6,2},{7,3},{8,12},{9,13},{10,... | collective-permute-start | bytes 3145736 | tf_op jit(solution)/shard_map/ppermute | solution.py:30
  115.6 31.6 %collective-permute-start.14 = (bf16[256,2048]{1,0:T(8,128)(2,1)S(1)}, bf16[256,2048]{1,0:T(8,128)(2,1)S(1)}, u32[]{:S(2)}, u32[]{:S(2)}) collective-permute-start(bf16[256,2048]{1,0:T(8,128)(2,1)S(1)} %bitcast.41), channel_id=1, source_target_pairs={{0,2},{1,3},{2,0},{3,1},{4,6},{5,7},{6,4},{7,5},{8,10},{9,11},{10,... | collective-permute-start | bytes 3145736 | tf_op jit(solution)/shard_map/ppermute | solution.py:30
  117.7 29.6 %collective-permute-start.13 = (bf16[64,2048]{1,0:T(8,128)(2,1)S(1)}, bf16[64,2048]{1,0:T(8,128)(2,1)}, u32[]{:S(2)}, u32[]{:S(2)}) collective-permute-start(bf16[64,2048]{1,0:T(8,128)(2,1)S(1)} %collective-permute-done.10.refs_1_), channel_id=1, source_target_pairs={{0,8},{8,16},{16,24},{24,0},{1,9},{9,17},{17,25},{25,1},{2,10},{10... | collective-permute-start | bytes 786440 | tf_op jit(solution)/shard_map/ppermute | solution.py:112
  117.7 29.6 %collective-permute-start.12 = (bf16[64,2048]{1,0:T(8,128)(2,1)S(1)}, bf16[64,2048]{1,0:T(8,128)(2,1)}, u32[]{:S(2)}, u32[]{:S(2)}) collective-permute-start(bf16[64,2048]{1,0:T(8,128)(2,1)S(1)} %collective-permute-done.10.refs_1_), channel_id=1, source_target_pairs={{0,16},{8,24},{16,0},{24,8},{1,17},{9,25},{17,1},{25,9},{2,18},{10... | collective-permute-start | bytes 786440 | tf_op jit(solution)/shard_map/ppermute | solution.py:112
  119.3 28.0 %collective-permute-start.11 = (bf16[64,2048]{1,0:T(8,128)(2,1)S(1)}, bf16[64,2048]{1,0:T(8,128)(2,1)}, u32[]{:S(2)}, u32[]{:S(2)}) collective-permute-start(bf16[64,2048]{1,0:T(8,128)(2,1)S(1)} %collective-permute-done.10.refs_1_), channel_id=1, source_target_pairs={{0,24},{8,0},{16,8},{24,16},{1,25},{9,1},{17,9},{25,17},{2,26},{10... | collective-permute-start | bytes 786440 | tf_op jit(solution)/shard_map/ppermute | solution.py:112
  147.3 315.2 %reduce-scatter.3.cloned.1.call-start = ((), (), s32[]{:S(2)}) async-start(), calls=%async_computation.9 | async-start | bytes 3604480 | tf_op jit(solution)/shard_map/reduce_scatter | solution.py:1182
  150.0 26.2 %collective-permute-start.19 = (bf16[256,2048]{1,0:T(8,128)(2,1)}, bf16[256,2048]{1,0:T(8,128)(2,1)}, u32[]{:S(2)}, u32[]{:S(2)}) collective-permute-start(bf16[256,2048]{1,0:T(8,128)(2,1)} %bitcast.48), channel_id=1, source_target_pairs={{0,1},{1,0},{2,3},{3,2},{4,5},{5,4},{6,7},{7,6},{8,9},{9,8},{10,11... | collective-permute-start | bytes 3145736 | tf_op jit(solution)/shard_map/ppermute | solution.py:30
  151.5 25.1 %collective-permute-start.18 = (bf16[256,2048]{1,0:T(8,128)(2,1)}, bf16[256,2048]{1,0:T(8,128)(2,1)S(1)}, u32[]{:S(2)}, u32[]{:S(2)}) collective-permute-start(bf16[256,2048]{1,0:T(8,128)(2,1)} %bitcast.49), channel_id=1, source_target_pairs={{0,4},{1,5},{2,6},{3,7},{4,0},{5,1},{6,2},{7,3},{8,12},{9,13},{10,... | collective-permute-start | bytes 3145736 | tf_op jit(solution)/shard_map/ppermute | solution.py:30
  151.5 25.1 %collective-permute-start.17 = (bf16[256,2048]{1,0:T(8,128)(2,1)}, bf16[256,2048]{1,0:T(8,128)(2,1)S(1)}, u32[]{:S(2)}, u32[]{:S(2)}) collective-permute-start(bf16[256,2048]{1,0:T(8,128)(2,1)} %bitcast.50), channel_id=1, source_target_pairs={{0,2},{1,3},{2,0},{3,1},{4,6},{5,7},{6,4},{7,5},{8,10},{9,11},{10,... | collective-permute-start | bytes 3145736 | tf_op jit(solution)/shard_map/ppermute | solution.py:30
  181.7 33.7 %collective-permute-start.20 = (bf16[256,2048]{1,0:T(8,128)(2,1)}, bf16[256,2048]{1,0:T(8,128)(2,1)S(1)}, u32[]{:S(2)}, u32[]{:S(2)}) collective-permute-start(bf16[256,2048]{1,0:T(8,128)(2,1)} %copy-done.8), channel_id=1, source_target_pairs={{0,1},{1,0},{2,3},{3,2},{4,5},{5,4},{6,7},{7,6},{8,9},{9,8},{10,11... | collective-permute-start | bytes 3145736 | tf_op jit(solution)/shard_map/ppermute | solution.py:30
  183.2 32.3 %collective-permute-start.21 = (bf16[256,2048]{1,0:T(8,128)(2,1)}, bf16[256,2048]{1,0:T(8,128)(2,1)S(1)}, u32[]{:S(2)}, u32[]{:S(2)}) collective-permute-start(bf16[256,2048]{1,0:T(8,128)(2,1)} %copy-done.7), channel_id=1, source_target_pairs={{0,1},{1,0},{2,3},{3,2},{4,5},{5,4},{6,7},{7,6},{8,9},{9,8},{10,11... | collective-permute-start | bytes 3145736 | tf_op jit(solution)/shard_map/ppermute | solution.py:30
  226.2 47.2 %collective-permute-start.27 = (bf16[256,2048]{1,0:T(8,128)(2,1)}, bf16[256,2048]{1,0:T(8,128)(2,1)}, u32[]{:S(2)}, u32[]{:S(2)}) collective-permute-start(bf16[256,2048]{1,0:T(8,128)(2,1)} %get-tuple-element.547.refs_0_), channel_id=1, source_target_pairs={{0,1},{1,0},{2,3},{3,2},{4,5},{5,4},{6,7},{7,6},{8,9},{9,8},{10,11... | collective-permute-start | bytes 3145736 | tf_op jit(solution)/shard_map/ppermute | solution.py:30
  227.6 63.3 %collective-permute-start.26 = (bf16[256,2048]{1,0:T(8,128)(2,1)}, bf16[256,2048]{1,0:T(8,128)(2,1)S(1)}, u32[]{:S(2)}, u32[]{:S(2)}) collective-permute-start(bf16[256,2048]{1,0:T(8,128)(2,1)} %get-tuple-element.547.refs_0_), channel_id=1, source_target_pairs={{0,4},{1,5},{2,6},{3,7},{4,0},{5,1},{6,2},{7,3},{8,12},{9,13},{10,... | collective-permute-start | bytes 3145736 | tf_op jit(solution)/shard_map/ppermute | solution.py:30
  227.9 63.0 %collective-permute-start.25 = (bf16[256,2048]{1,0:T(8,128)(2,1)}, bf16[256,2048]{1,0:T(8,128)(2,1)S(1)}, u32[]{:S(2)}, u32[]{:S(2)}) collective-permute-start(bf16[256,2048]{1,0:T(8,128)(2,1)} %get-tuple-element.547.refs_0_), channel_id=1, source_target_pairs={{0,2},{1,3},{2,0},{3,1},{4,6},{5,7},{6,4},{7,5},{8,10},{9,11},{10,... | collective-permute-start | bytes 3145736 | tf_op jit(solution)/shard_map/ppermute | solution.py:30
  230.1 28.8 %collective-permute-start.28 = (bf16[176,1024]{1,0:T(8,128)(2,1)}, bf16[176,1024]{1,0:T(8,128)(2,1)S(1)}, u32[]{:S(2)}, u32[]{:S(2)}) collective-permute-start(bf16[176,1024]{1,0:T(8,128)(2,1)} %get-tuple-element.462), channel_id=1, source_target_pairs={{0,24},{8,0},{16,8},{24,16},{1,25},{9,1},{17,9},{25,17},{2,26},{10... | collective-permute-start | bytes 1081352 | tf_op jit(solution)/shard_map/ppermute | solution.py:112
  231.0 34.0 %collective-permute-start.29 = (bf16[176,1024]{1,0:T(8,128)(2,1)}, bf16[176,1024]{1,0:T(8,128)(2,1)S(1)}, u32[]{:S(2)}, u32[]{:S(2)}) collective-permute-start(bf16[176,1024]{1,0:T(8,128)(2,1)} %get-tuple-element.463), channel_id=1, source_target_pairs={{0,8},{8,16},{16,24},{24,0},{1,9},{9,17},{17,25},{25,1},{2,10},{10... | collective-permute-start | bytes 1081352 | tf_op jit(solution)/shard_map/ppermute | solution.py:112
  268.6 39.3 %collective-permute-start.34 = (bf16[256,2048]{1,0:T(8,128)(2,1)S(1)}, bf16[256,2048]{1,0:T(8,128)(2,1)}, u32[]{:S(2)}, u32[]{:S(2)}) collective-permute-start(bf16[256,2048]{1,0:T(8,128)(2,1)S(1)} %collective-permute-done.14.refs_2_.refs_1_.refs_10_), channel_id=1, source_target_pairs={{0,1},{1,0},{2,3},{3,2},{4,5},{5,4},{6,7},{7,6},{8,9},{9,8},{10,11... | collective-permute-start | bytes 3145736 | tf_op jit(solution)/shard_map/ppermute | solution.py:30
  292.5 35.3 %collective-permute-start.33 = (bf16[256,2048]{1,0:T(8,128)(2,1)S(1)}, bf16[256,2048]{1,0:T(8,128)(2,1)S(1)}, u32[]{:S(2)}, u32[]{:S(2)}) collective-permute-start(bf16[256,2048]{1,0:T(8,128)(2,1)S(1)} %collective-permute-done.26.refs_0_.refs_4_), channel_id=1, source_target_pairs={{0,1},{1,0},{2,3},{3,2},{4,5},{5,4},{6,7},{7,6},{8,9},{9,8},{10,11... | collective-permute-start | bytes 3145736 | tf_op jit(solution)/shard_map/ppermute | solution.py:30
  295.1 32.7 %collective-permute-start.30 = (bf16[128,2048]{1,0:T(8,128)(2,1)}, bf16[128,2048]{1,0:T(8,128)(2,1)S(1)}, u32[]{:S(2)}, u32[]{:S(2)}) collective-permute-start(bf16[128,2048]{1,0:T(8,128)(2,1)} %get-tuple-element.468), channel_id=1, source_target_pairs={{0,2},{1,3},{2,0},{3,1},{4,6},{5,7},{6,4},{7,5},{8,10},{9,11},{10,... | collective-permute-start | bytes 1572872 | tf_op jit(solution)/shard_map/ppermute | solution.py:30
  391.1 199.0 %reduce-scatter.5.cloned.1.call-start = ((), (), s32[]{:S(2)}) async-start(), calls=%async_computation.10 | async-start | bytes 7208960 | tf_op jit(solution)/shard_map/reduce_scatter | solution.py:1203
  396.7 25.0 %collective-permute-start.46 = (bf16[256,2048]{1,0:T(8,128)(2,1)}, bf16[256,2048]{1,0:T(8,128)(2,1)S(1)}, u32[]{:S(2)}, u32[]{:S(2)}) collective-permute-start(bf16[256,2048]{1,0:T(8,128)(2,1)} %get-tuple-element.545), channel_id=1, source_target_pairs={{0,2},{1,3},{2,0},{3,1},{4,6},{5,7},{6,4},{7,5},{8,10},{9,11},{10,... | collective-permute-start | bytes 3145736 | tf_op jit(solution)/shard_map/ppermute | solution.py:30
  397.8 24.6 %collective-permute-start.47 = (bf16[256,2048]{1,0:T(8,128)(2,1)}, bf16[256,2048]{1,0:T(8,128)(2,1)}, u32[]{:S(2)}, u32[]{:S(2)}) collective-permute-start(bf16[256,2048]{1,0:T(8,128)(2,1)} %get-tuple-element.546), channel_id=1, source_target_pairs={{0,4},{1,5},{2,6},{3,7},{4,0},{5,1},{6,2},{7,3},{8,12},{9,13},{10,... | collective-permute-start | bytes 3145736 | tf_op jit(solution)/shard_map/ppermute | solution.py:30
  436.3 26.1 %collective-permute-start.52 = (bf16[256,2048]{1,0:T(8,128)(2,1)S(1)}, bf16[256,2048]{1,0:T(8,128)(2,1)}, u32[]{:S(2)}, u32[]{:S(2)}) collective-permute-start(bf16[256,2048]{1,0:T(8,128)(2,1)S(1)} %copy-done.67), channel_id=1, source_target_pairs={{0,1},{1,0},{2,3},{3,2},{4,5},{5,4},{6,7},{7,6},{8,9},{9,8},{10,11... | collective-permute-start | bytes 3145736 | tf_op jit(solution)/shard_map/ppermute | solution.py:30
  438.2 24.2 %collective-permute-start.53 = (bf16[256,2048]{1,0:T(8,128)(2,1)S(1)}, bf16[256,2048]{1,0:T(8,128)(2,1)S(1)}, u32[]{:S(2)}, u32[]{:S(2)}) collective-permute-start(bf16[256,2048]{1,0:T(8,128)(2,1)S(1)} %copy-done.68), channel_id=1, source_target_pairs={{0,1},{1,0},{2,3},{3,2},{4,5},{5,4},{6,7},{7,6},{8,9},{9,8},{10,11... | collective-permute-start | bytes 3145736 | tf_op jit(solution)/shard_map/ppermute | solution.py:30
  438.3 24.1 %collective-permute-start.54 = (bf16[256,2048]{1,0:T(8,128)(2,1)}, bf16[256,2048]{1,0:T(8,128)(2,1)S(1)}, u32[]{:S(2)}, u32[]{:S(2)}) collective-permute-start(bf16[256,2048]{1,0:T(8,128)(2,1)} %get-tuple-element.592), channel_id=1, source_target_pairs={{0,1},{1,0},{2,3},{3,2},{4,5},{5,4},{6,7},{7,6},{8,9},{9,8},{10,11... | collective-permute-start | bytes 3145736 | tf_op jit(solution)/shard_map/ppermute | solution.py:30
  468.4 35.7 %collective-permute-start.57 = (bf16[256,2048]{1,0:T(8,128)(2,1)}, bf16[256,2048]{1,0:T(8,128)(2,1)S(1)}, u32[]{:S(2)}, u32[]{:S(2)}) collective-permute-start(bf16[256,2048]{1,0:T(8,128)(2,1)} %get-tuple-element.620), channel_id=1, source_target_pairs={{0,2},{1,3},{2,0},{3,1},{4,6},{5,7},{6,4},{7,5},{8,10},{9,11},{10,... | collective-permute-start | bytes 3145736 | tf_op jit(solution)/shard_map/ppermute | solution.py:30
  469.0 35.0 %collective-permute-start.58 = (bf16[256,2048]{1,0:T(8,128)(2,1)}, bf16[256,2048]{1,0:T(8,128)(2,1)S(1)}, u32[]{:S(2)}, u32[]{:S(2)}) collective-permute-start(bf16[256,2048]{1,0:T(8,128)(2,1)} %get-tuple-element.621), channel_id=1, source_target_pairs={{0,4},{1,5},{2,6},{3,7},{4,0},{5,1},{6,2},{7,3},{8,12},{9,13},{10,... | collective-permute-start | bytes 3145736 | tf_op jit(solution)/shard_map/ppermute | solution.py:30
  471.6 31.2 %collective-permute-start.55 = (bf16[128,2048]{1,0:T(8,128)(2,1)}, bf16[128,2048]{1,0:T(8,128)(2,1)S(1)}, u32[]{:S(2)}, u32[]{:S(2)}) collective-permute-start(bf16[128,2048]{1,0:T(8,128)(2,1)} %get-tuple-element.610), channel_id=1, source_target_pairs={{0,2},{1,3},{2,0},{3,1},{4,6},{5,7},{6,4},{7,5},{8,10},{9,11},{10,... | collective-permute-start | bytes 1572872 | tf_op jit(solution)/shard_map/ppermute | solution.py:30
  472.4 31.6 %collective-permute-start.56 = (bf16[128,2048]{1,0:T(8,128)(2,1)}, bf16[128,2048]{1,0:T(8,128)(2,1)S(1)}, u32[]{:S(2)}, u32[]{:S(2)}) collective-permute-start(bf16[128,2048]{1,0:T(8,128)(2,1)} %get-tuple-element.611), channel_id=1, source_target_pairs={{0,4},{1,5},{2,6},{3,7},{4,0},{5,1},{6,2},{7,3},{8,12},{9,13},{10,... | collective-permute-start | bytes 1572872 | tf_op jit(solution)/shard_map/ppermute | solution.py:30
  525.6 69.7 %all-to-all-start.4 = ((bf16[32,64,384]{2,1,0:T(8,128)(2,1)}), bf16[32,64,384]{2,1,0:T(8,128)(2,1)S(1)}, u32[]{:S(2)}, u32[]{:S(2)}) async-start(bf16[32,64,384]{2,1,0:T(8,128)(2,1)} %bitcast.53), calls=%async_computation.6 | async-start | bytes 3145728 | tf_op jit(solution)/shard_map/all_to_all | solution.py:99
  552.5 29.8 %collective-permute-start.70 = (bf16[256,2048]{1,0:T(8,128)(2,1)}, bf16[256,2048]{1,0:T(8,128)(2,1)S(1)}, u32[]{:S(2)}, u32[]{:S(2)}) collective-permute-start(bf16[256,2048]{1,0:T(8,128)(2,1)} %get-tuple-element.707), channel_id=1, source_target_pairs={{0,2},{1,3},{2,0},{3,1},{4,6},{5,7},{6,4},{7,5},{8,10},{9,11},{10,... | collective-permute-start | bytes 3145736 | tf_op jit(solution)/shard_map/ppermute | solution.py:30
  552.6 30.5 %collective-permute-start.71 = (bf16[256,2048]{1,0:T(8,128)(2,1)S(1)}, bf16[256,2048]{1,0:T(8,128)(2,1)S(1)}, u32[]{:S(2)}, u32[]{:S(2)}) collective-permute-start(bf16[256,2048]{1,0:T(8,128)(2,1)S(1)} %copy-done.70), channel_id=1, source_target_pairs={{0,4},{1,5},{2,6},{3,7},{4,0},{5,1},{6,2},{7,3},{8,12},{9,13},{10,... | collective-permute-start | bytes 3145736 | tf_op jit(solution)/shard_map/ppermute | solution.py:30
  554.1 46.7 %collective-permute-start.65 = (bf16[256,2048]{1,0:T(8,128)(2,1)}, bf16[256,2048]{1,0:T(8,128)(2,1)}, u32[]{:S(2)}, u32[]{:S(2)}) collective-permute-start(bf16[256,2048]{1,0:T(8,128)(2,1)} %get-tuple-element.696), channel_id=1, source_target_pairs={{0,1},{1,0},{2,3},{3,2},{4,5},{5,4},{6,7},{7,6},{8,9},{9,8},{10,11... | collective-permute-start | bytes 3145736 | tf_op jit(solution)/shard_map/ppermute | solution.py:30
  561.2 47.6 %collective-permute-start.68 = (bf16[256,2048]{1,0:T(8,128)(2,1)}, bf16[256,2048]{1,0:T(8,128)(2,1)}, u32[]{:S(2)}, u32[]{:S(2)}) collective-permute-start(bf16[256,2048]{1,0:T(8,128)(2,1)} %get-tuple-element.703), channel_id=1, source_target_pairs={{0,2},{1,3},{2,0},{3,1},{4,6},{5,7},{6,4},{7,5},{8,10},{9,11},{10,... | collective-permute-start | bytes 3145736 | tf_op jit(solution)/shard_map/ppermute | solution.py:30
  561.3 47.6 %collective-permute-start.69 = (bf16[256,2048]{1,0:T(8,128)(2,1)}, bf16[256,2048]{1,0:T(8,128)(2,1)}, u32[]{:S(2)}, u32[]{:S(2)}) collective-permute-start(bf16[256,2048]{1,0:T(8,128)(2,1)} %get-tuple-element.704), channel_id=1, source_target_pairs={{0,4},{1,5},{2,6},{3,7},{4,0},{5,1},{6,2},{7,3},{8,12},{9,13},{10,... | collective-permute-start | bytes 3145736 | tf_op jit(solution)/shard_map/ppermute | solution.py:30
  595.3 34.1 %all-to-all-start.5 = ((bf16[8,64,1408]{2,1,0:T(8,128)(2,1)}), bf16[8,64,1408]{2,1,0:T(8,128)(2,1)S(1)}, u32[]{:S(2)}, u32[]{:S(2)}) async-start(bf16[8,64,1408]{2,1,0:T(8,128)(2,1)} %bitcast.58), calls=%async_computation.7 | async-start | bytes 2883584 | tf_op jit(solution)/shard_map/all_to_all | solution.py:95
  622.5 25.1 %collective-permute-start.75 = (bf16[64,2048]{1,0:T(8,128)(2,1)}, bf16[64,2048]{1,0:T(8,128)(2,1)S(1)}, u32[]{:S(2)}, u32[]{:S(2)}) collective-permute-start(bf16[64,2048]{1,0:T(8,128)(2,1)} %add_up.3), channel_id=1, source_target_pairs={{0,0},{8,1},{16,2},{24,3},{1,4},{9,5},{17,6},{25,7},{2,8},{10,9},{... | collective-permute-start | bytes 786440 | tf_op jit(solution)/shard_map/ppermute | solution.py:107
  (113 other events, 1178.0 us)
Sparse Core Ops, SparseCore 0:
  147.4 121.2 all-gather.1
  391.2 53.4 reduce-scatter.2
  462.6 123.0 reduce-scatter.4
